TPU v7x, 32 devices: a whole 2x2x4 slice. The times are simulated.
32 devices in a mesh: section: 2 (over x), ctx: 4 (over y, core), fsdp: 4 (over z).
Axes of the slice: x: 2, y: 2, z: 4, core: 2. Of those that a mesh axis runs over, the one named last changes fastest.
Arguments:
- inputs: bfloat16 [2, 4, 256, 2048], P(None, 'fsdp', 'ctx'), may hold values from -6 to 6
- cotangent: bfloat16 [2, 4, 256, 2048], P(None, 'fsdp', 'ctx'), may hold values from -6 to 6
- norm_gains: bfloat16 [2, 2, 2048], P('section', None, 'fsdp'), may hold values from 0.5 to 1.5
- head_params: bfloat16 [2, 3, 48], P('section', None, 'fsdp'), may hold values from -4 to 0
- conv_params: bfloat16 [2, 5, 3584], P('section', None, 'fsdp'), may hold values from -0.5 to 0.5
- ssm_gain: bfloat16 [2, 3072], P('section', 'fsdp'), may hold values from 0.5 to 1.5
- w_in: bfloat16 [2, 2048, 6704], P('section', 'fsdp'), may hold values from -0.125 to 0.125
- w_out: bfloat16 [2, 3072, 2048], P('section', 'fsdp'), may hold values from -0.109375 to 0.109375
- w_qkv: bfloat16 [2, 2048, 1536], P('section', 'fsdp'), may hold values from -0.125 to 0.125
- w_o: bfloat16 [2, 1024, 2048], P('section', 'fsdp'), may hold values from -1.5 to 1.5
- w_gu: bfloat16 [2, 2048, 8192], P('section', 'fsdp'), may hold values from -0.125 to 0.125
- w_down: bfloat16 [2, 4096, 2048], P('section', 'fsdp'), may hold values from -0.09375 to 0.09375
Outputs:
- layer_outputs: bfloat16 [2, 2, 4, 256, 2048], P('section', None, 'fsdp', 'ctx')
- grad_inputs: bfloat16 [2, 2, 4, 256, 2048], P('section', None, 'fsdp', 'ctx')
- grad_norm_gains: float32 [2, 2, 2048], P('section', None, 'fsdp')
- grad_head_params: float32 [2, 3, 48], P('section', None, 'fsdp')
- grad_conv_params: float32 [2, 5, 3584], P('section', None, 'fsdp')
- grad_ssm_gain: float32 [2, 3072], P('section', 'fsdp')
- grad_w_in: float32 [2, 2048, 6704], P('section', 'fsdp')
- grad_w_out: float32 [2, 3072, 2048], P('section', 'fsdp')
- grad_w_qkv: float32 [2, 2048, 1536], P('section', 'fsdp')
- grad_w_o: float32 [2, 1024, 2048], P('section', 'fsdp')
- grad_w_gu: float32 [2, 2048, 8192], P('section', 'fsdp')
- grad_w_down: float32 [2, 4096, 2048], P('section', 'fsdp')
All inputs are finite; a program needn't handle non-finite values.
Results may differ from a plain program's by a relative error of at most 0.024.
Values may be sent and summed in bfloat16 or wider, within the bound.
A program may use at most 448 MiB of HBM per device.

v0:
```python
import jax
import jax.numpy as jnp
from jax import lax
from jax.sharding import PartitionSpec as P

FF = 4096
SSM_HEADS = 48
SSM_HEAD = 64
STATE = 256
Q_HEADS = 8
KV_HEADS = 2
HEAD_DIM = 128
CONV_K = 4
D_SSM = 3072
CONV_W = 3584
D_IN = 6704


EPSILON = 1e-05
ROPE_BASE = 10000.0
NEGATIVE = -1e30
HIGHEST = lax.Precision.HIGHEST


def passed_along(value, axis, steps):
    count = lax.axis_size(axis)
    initial, last = (max(0, -steps), min(count, count - steps))
    return lax.ppermute(value, axis, [(source, source + steps) for source in range(initial, last)])


def carried_in(shard, axis, combine, identity):
    devices, index = (lax.axis_size(axis), lax.axis_index(axis))
    everything = jax.tree.map(lambda part: lax.all_gather(part, axis), shard)
    start = jax.tree.map(
        lambda part, zero: jnp.broadcast_to(jnp.asarray(zero, part.dtype), part.shape),
        shard,
        identity,
    )

    def lap(k, before):
        reached = k < index
        new = combine(before, jax.tree.map(lambda part: part[k], everything))
        return jax.tree.map(lambda a, b: jnp.where(reached, a, b), new, before)

    return lax.fori_loop(0, devices, lap, start)


def prefix(shard, axis, join, neutral):
    count = lax.axis_size(axis)
    place = lax.axis_index(axis)
    ahead = count - 1 - place
    gathered = jax.tree.map(
        lambda a, kind: lax.all_gather(a.astype(kind), axis),
        shard,
        jax.tree.map(lambda a: jnp.bfloat16 if a.dtype == jnp.float32 else a.dtype, shard),
    )
    state = jax.tree.map(lambda a, e: jnp.zeros_like(a) + jnp.asarray(e, a.dtype), shard, neutral)

    def one(lap, state):
        source = count - 1 - lap
        return join(
            state,
            jax.tree.map(
                lambda a, own: lax.dynamic_index_in_dim(a, source, 0, False).astype(own.dtype),
                gathered,
                shard,
            ),
        )

    return lax.fori_loop(0, ahead, one, state)


def narrow(values):
    return values.astype(jnp.bfloat16)


def rounded(values):
    return lax.optimization_barrier(values.astype(jnp.bfloat16)).astype(jnp.float32)


def bf_dot(left_side, right_side):
    return jnp.dot(left_side, right_side, preferred_element_type=jnp.float32)


def dot_right_t(left_side, right_side):
    return lax.dot_general(
        left_side, right_side, (((1,), (1,)), ((), ())), preferred_element_type=jnp.float32
    )


def rms_scale(values, gain_row):
    return (
        values * lax.rsqrt(jnp.mean(values * values, axis=-1, keepdims=True) + EPSILON) * gain_row
    )


def rotary(values, head_count, position, turning):
    length = values.shape[0]
    half_dim = HEAD_DIM // 2
    frequency = ROPE_BASE ** (-jnp.arange(half_dim, dtype=jnp.float32) / half_dim)
    angles = position[:, None] * frequency[None, :]
    cosine = jnp.cos(angles)[:, None, :]
    sine_part = turning * jnp.sin(angles)[:, None, :]
    halves = values.reshape(length, head_count, 2, half_dim)
    first_half = halves[:, :, 0]
    second_half = halves[:, :, 1]
    turned = jnp.stack(
        [
            first_half * cosine - second_half * sine_part,
            second_half * cosine + first_half * sine_part,
        ],
        axis=2,
    )
    return turned.reshape(length, head_count * HEAD_DIM)


def swiglu(gate_up):
    return jax.nn.silu(gate_up[:, :FF]) * gate_up[:, FF:]


def gated_norm(ssm_out, gate_z, gain_row):
    return rms_scale(ssm_out * jax.nn.silu(gate_z), gain_row)


def conv_local(extended, conv_table):
    length = extended.shape[0] - (CONV_K - 1)
    running = conv_table[CONV_K]
    for tap_index in range(CONV_K):
        running = running + conv_table[tap_index] * extended[tap_index : tap_index + length]
    return jax.nn.silu(running)


def ssd_parts(ssm_input, dt_raw, head_table):
    length = ssm_input.shape[0]
    x_heads = ssm_input[:, :D_SSM].reshape(length, SSM_HEADS, SSM_HEAD)
    b_rows = ssm_input[:, D_SSM : D_SSM + STATE]
    c_rows = ssm_input[:, D_SSM + STATE :]
    dt_step = jax.nn.softplus(dt_raw + head_table[0])
    running = jnp.cumsum(-dt_step * jnp.exp(head_table[1]), axis=0)
    return (x_heads, b_rows, c_rows, dt_step, running)


def block_summary(ssm_input, dt_raw, head_table):
    x_heads, b_rows, c_rows, dt_step, running = ssd_parts(ssm_input, dt_raw, head_table)
    to_end = jnp.exp(running[-1][None, :] - running) * dt_step
    local_state = jnp.einsum("shp,sn->hpn", to_end[:, :, None] * x_heads, b_rows, precision=HIGHEST)
    return (jnp.exp(running[-1]), local_state)


def block_output(ssm_input, dt_raw, head_table, state_in):
    length = ssm_input.shape[0]
    x_heads, b_rows, c_rows, dt_step, running = ssd_parts(ssm_input, dt_raw, head_table)
    position = jnp.arange(length)
    allowed = (position[:, None] >= position[None, :])[:, :, None]
    log_gap = jnp.where(allowed, running[:, None, :] - running[None, :, :], 0.0)
    decay_table = jnp.where(allowed, jnp.exp(log_gap), 0.0)
    mixing = jnp.dot(c_rows, b_rows.T, precision=HIGHEST, preferred_element_type=jnp.float32)
    weights = decay_table * mixing[:, :, None] * dt_step[None, :, :]
    within = jnp.einsum("tsh,shp->thp", weights, x_heads, precision=HIGHEST)
    carried = jnp.exp(running)[:, :, None] * jnp.einsum(
        "tn,hpn->thp", c_rows, state_in, precision=HIGHEST
    )
    result = within + carried + head_table[2][None, :, None] * x_heads
    return result.reshape(length, D_SSM)


def block_full(ssm_input, dt_raw, head_table, state_in):
    block_decay, local_state = block_summary(ssm_input, dt_raw, head_table)
    return (
        block_output(ssm_input, dt_raw, head_table, state_in),
        block_decay[:, None, None] * state_in + local_state,
    )


def state_pull(ssm_input, dt_raw, head_table, grad_y):
    length = ssm_input.shape[0]
    x_heads, b_rows, c_rows, dt_step, running = ssd_parts(ssm_input, dt_raw, head_table)
    weighted = jnp.exp(running)[:, :, None] * grad_y.reshape(length, SSM_HEADS, SSM_HEAD)
    return jnp.einsum("thp,tn->hpn", weighted, c_rows, precision=HIGHEST)


def chain_states(earlier, later):
    return (earlier[0] * later[0], later[0][:, None, None] * earlier[1] + later[1])


def score_block(query_b, kv_all, offset):
    row_count = query_b.shape[0]
    length = kv_all.shape[0]
    group_size = Q_HEADS // KV_HEADS
    kv_width = KV_HEADS * HEAD_DIM
    query_heads = query_b.reshape(row_count, KV_HEADS, group_size, HEAD_DIM)
    key_heads = kv_all[:, :kv_width].reshape(length, KV_HEADS, HEAD_DIM)
    value_heads = kv_all[:, kv_width:].reshape(length, KV_HEADS, HEAD_DIM)
    scores = jnp.einsum(
        "qkgd,skd->kgqs", query_heads, key_heads, preferred_element_type=jnp.float32
    ) * HEAD_DIM ** (-0.5)
    allowed = (offset + jnp.arange(row_count))[:, None] >= jnp.arange(length)[None, :]
    return (jnp.where(allowed, scores, NEGATIVE), query_heads, key_heads, value_heads)


def attend_forward(query_b, kv_all, offset):
    row_count = query_b.shape[0]
    scores, query_heads, key_heads, value_heads = score_block(query_b, kv_all, offset)
    maximum = jnp.max(scores, axis=-1, keepdims=True)
    weights = jnp.exp(scores - maximum)
    running = jnp.sum(weights, axis=-1, keepdims=True)
    probs_b = narrow(weights / running)
    mixed_out = jnp.einsum(
        "kgqs,skd->qkgd", probs_b, value_heads, preferred_element_type=jnp.float32
    )
    return (
        narrow(mixed_out.reshape(row_count, Q_HEADS * HEAD_DIM)),
        (maximum + jnp.log(running))[..., 0],
    )


def attend_backward(query_b, kv_all, offset, log_total, grad_out_b):
    row_count = query_b.shape[0]
    length = kv_all.shape[0]
    group_size = Q_HEADS // KV_HEADS
    scores, query_heads, key_heads, value_heads = score_block(query_b, kv_all, offset)
    probabilities = jnp.exp(scores - log_total[..., None])
    grad_heads = grad_out_b.reshape(row_count, KV_HEADS, group_size, HEAD_DIM)
    grad_probs = jnp.einsum(
        "qkgd,skd->kgqs", grad_heads, value_heads, preferred_element_type=jnp.float32
    )
    grad_scores = narrow(
        probabilities * (grad_probs - jnp.sum(probabilities * grad_probs, axis=-1, keepdims=True))
    )
    scale = HEAD_DIM ** (-0.5)
    grad_query = (
        jnp.einsum(
            "kgqs,skd->qkgd", grad_scores, key_heads, preferred_element_type=jnp.float32
        ).reshape(row_count, Q_HEADS * HEAD_DIM)
        * scale
    )
    grad_keys = (
        jnp.einsum(
            "kgqs,qkgd->skd", grad_scores, query_heads, preferred_element_type=jnp.float32
        ).reshape(length, KV_HEADS * HEAD_DIM)
        * scale
    )
    grad_values = jnp.einsum(
        "kgqs,qkgd->skd", narrow(probabilities), grad_heads, preferred_element_type=jnp.float32
    ).reshape(length, KV_HEADS * HEAD_DIM)
    return (grad_query, jnp.concatenate([grad_keys, grad_values], axis=1))


def layer_forward(entering_b, weights, position, offset):
    gains, head_table, conv_table, ssm_gain, w_in, w_out, w_qkv, w_o, w_gu, w_down = weights
    gains_wide = gains.astype(jnp.float32)
    head_wide = head_table.astype(jnp.float32)
    conv_wide = conv_table.astype(jnp.float32)
    entering = entering_b.astype(jnp.float32)
    row_count = entering.shape[0]
    kv_width = KV_HEADS * HEAD_DIM
    att_width = Q_HEADS * HEAD_DIM
    normed1_b = narrow(rms_scale(entering, gains_wide[0]))
    qkv_proj = bf_dot(normed1_b, w_qkv)
    query_b = narrow(rotary(qkv_proj[:, :att_width], Q_HEADS, position, 1.0))
    keys_b = narrow(rotary(qkv_proj[:, att_width : att_width + kv_width], KV_HEADS, position, 1.0))
    kv_all = lax.all_gather(
        jnp.concatenate([keys_b, narrow(qkv_proj[:, att_width + kv_width :])], axis=1),
        "ctx",
        axis=0,
        tiled=True,
    )
    mixed_b, log_total = attend_forward(query_b, kv_all, offset)
    zx_proj = bf_dot(normed1_b, w_in)
    xbc_b = narrow(zx_proj[:, D_SSM : D_SSM + CONV_W])
    before_rows = passed_along(xbc_b[row_count - CONV_K + 1 :], "ctx", 1)
    extended = jnp.concatenate([before_rows, xbc_b], axis=0).astype(jnp.float32)
    ssm_input = rounded(conv_local(extended, conv_wide))
    dt_raw = zx_proj[:, D_SSM + CONV_W :]
    block_decay, local_state = block_summary(ssm_input, dt_raw, head_wide)
    carried = carried_in(
        (block_decay, local_state),
        "ctx",
        chain_states,
        (jnp.ones_like(block_decay), jnp.zeros_like(local_state)),
    )
    state_in = carried[1]
    ssm_out = block_output(ssm_input, dt_raw, head_wide, state_in)
    ssm_normed_b = narrow(gated_norm(ssm_out, zx_proj[:, :D_SSM], ssm_gain.astype(jnp.float32)))
    mid_state = entering + bf_dot(mixed_b, w_o) + bf_dot(ssm_normed_b, w_out)
    normed2_b = narrow(rms_scale(mid_state, gains_wide[1]))
    gate_up = bf_dot(normed2_b, w_gu)
    act_b = narrow(swiglu(gate_up))
    leaving_b = narrow(mid_state + bf_dot(act_b, w_down))
    kept_values = {
        "entering": entering,
        "normed1_b": normed1_b,
        "query_b": query_b,
        "kv_all": kv_all,
        "log_total": log_total,
        "mixed_b": mixed_b,
        "zx_proj": zx_proj,
        "extended": extended,
        "block_decay": block_decay,
        "state_in": state_in,
        "ssm_out": ssm_out,
        "ssm_normed_b": ssm_normed_b,
        "mid_state": mid_state,
        "normed2_b": normed2_b,
        "gate_up": gate_up,
        "act_b": act_b,
    }
    return (leaving_b, kept_values)


def layer_backward(grad_out, kept_values, weights, position, offset):
    gains, head_table, conv_table, ssm_gain, w_in, w_out, w_qkv, w_o, w_gu, w_down = weights
    gains_wide = gains.astype(jnp.float32)
    head_wide = head_table.astype(jnp.float32)
    conv_wide = conv_table.astype(jnp.float32)
    row_count = grad_out.shape[0]
    kv_width = KV_HEADS * HEAD_DIM
    grad_mlp_b = narrow(grad_out)
    grad_act = dot_right_t(grad_mlp_b, w_down)
    pull_act = jax.vjp(swiglu, kept_values["gate_up"])[1]
    grad_gate_up_b = narrow(pull_act(grad_act)[0])
    grad_normed2 = dot_right_t(grad_gate_up_b, w_gu)
    pull_norm2 = jax.vjp(rms_scale, kept_values["mid_state"], gains_wide[1])[1]
    grad_mid_part, grad_gain2 = pull_norm2(grad_normed2)
    grad_mid = grad_out + grad_mid_part
    grad_branch_b = narrow(grad_mid)
    grad_mixed_b = narrow(dot_right_t(grad_branch_b, w_o))
    grad_ssm_normed = dot_right_t(grad_branch_b, w_out)
    zx_proj = kept_values["zx_proj"]
    pull_gate = jax.vjp(
        gated_norm, kept_values["ssm_out"], zx_proj[:, :D_SSM], ssm_gain.astype(jnp.float32)
    )[1]
    grad_y, grad_z, grad_ssm_gain = pull_gate(grad_ssm_normed)
    dt_raw = zx_proj[:, D_SSM + CONV_W :]
    conv_out, pull_conv = jax.vjp(conv_local, kept_values["extended"], conv_wide)
    ssm_input = rounded(conv_out)
    state_grad = state_pull(ssm_input, dt_raw, head_wide, grad_y)
    block_decay = kept_values["block_decay"]
    later = prefix(
        (block_decay, state_grad),
        "ctx",
        chain_states,
        (jnp.ones_like(block_decay), jnp.zeros_like(state_grad)),
    )[1]
    pull_ssd = jax.vjp(block_full, ssm_input, dt_raw, head_wide, kept_values["state_in"])[1]
    grad_input, grad_dt, grad_heads, unused = pull_ssd((grad_y, later))
    grad_extended, grad_conv = pull_conv(grad_input)
    returned = passed_along(grad_extended[: CONV_K - 1].astype(jnp.bfloat16), "ctx", -1).astype(
        jnp.float32
    )
    grad_xbc = grad_extended[CONV_K - 1 :] + jnp.concatenate(
        [jnp.zeros((row_count - CONV_K + 1, CONV_W), jnp.float32), returned], axis=0
    )
    grad_zx_b = narrow(jnp.concatenate([grad_z, grad_xbc, grad_dt], axis=1))
    grad_query, grad_kv_all = attend_backward(
        kept_values["query_b"],
        kept_values["kv_all"],
        offset,
        kept_values["log_total"],
        grad_mixed_b,
    )
    grad_kv = lax.psum_scatter(grad_kv_all, "ctx", scatter_dimension=0, tiled=True)
    grad_qkv_b = narrow(
        jnp.concatenate(
            [
                rotary(grad_query, Q_HEADS, position, -1.0),
                rotary(grad_kv[:, :kv_width], KV_HEADS, position, -1.0),
                grad_kv[:, kv_width:],
            ],
            axis=1,
        )
    )
    grad_normed1 = dot_right_t(grad_qkv_b, w_qkv) + dot_right_t(grad_zx_b, w_in)
    pull_norm1 = jax.vjp(rms_scale, kept_values["entering"], gains_wide[0])[1]
    grad_enter_part, grad_gain1 = pull_norm1(grad_normed1)
    grad_enter_b = narrow(grad_mid + grad_enter_part)
    small_terms = (jnp.stack([grad_gain1, grad_gain2]), grad_heads, grad_conv, grad_ssm_gain)
    products = (
        (kept_values["normed1_b"], jnp.concatenate([grad_zx_b, grad_qkv_b], axis=1)),
        (kept_values["ssm_normed_b"], grad_branch_b),
        (kept_values["mixed_b"], grad_branch_b),
        (kept_values["normed2_b"], grad_gate_up_b),
        (kept_values["act_b"], grad_mlp_b),
    )
    return (grad_enter_b, small_terms, products)


def shard_grad(left_rows, right_rows):
    return lax.psum_scatter(
        lax.dot_general(
            left_rows, right_rows, (((0,), (0,)), ((), ())), preferred_element_type=jnp.float32
        ).astype(jnp.bfloat16),
        "fsdp",
        scatter_dimension=0,
        tiled=True,
    ).astype(jnp.float32)


def body(
    inputs,
    cotangent,
    norm_gains,
    head_params,
    conv_params,
    ssm_gain,
    w_in,
    w_out,
    w_qkv,
    w_o,
    w_gu,
    w_down,
):
    weights = (
        lax.all_gather(norm_gains[0], "fsdp", axis=1, tiled=True),
        lax.all_gather(head_params[0], "fsdp", axis=1, tiled=True),
        lax.all_gather(conv_params[0], "fsdp", axis=1, tiled=True),
        lax.all_gather(ssm_gain[0], "fsdp", axis=0, tiled=True),
        lax.all_gather(w_in[0], "fsdp", axis=0, tiled=True),
        lax.all_gather(w_out[0], "fsdp", axis=0, tiled=True),
        lax.all_gather(w_qkv[0], "fsdp", axis=0, tiled=True),
        lax.all_gather(w_o[0], "fsdp", axis=0, tiled=True),
        lax.all_gather(w_gu[0], "fsdp", axis=0, tiled=True),
        lax.all_gather(w_down[0], "fsdp", axis=0, tiled=True),
    )
    sections = lax.axis_size("section")
    section_index = lax.axis_index("section")
    own_inputs = inputs[:, 0]
    micro_count = own_inputs.shape[0]
    row_count = own_inputs.shape[1]
    tick_total = micro_count + sections - 1
    offset = lax.axis_index("ctx") * row_count
    position = (offset + jnp.arange(row_count)).astype(jnp.float32)
    arrived = jnp.zeros_like(own_inputs[0])
    layer_out = jnp.zeros_like(own_inputs)
    kept_list = []
    for tick_index in range(tick_total):
        micro_index = tick_index - section_index
        is_valid = (micro_index >= 0) & (micro_index < micro_count)
        slot_index = jnp.clip(micro_index, 0, micro_count - 1)
        entering_b = jnp.where(
            section_index == 0,
            lax.dynamic_index_in_dim(own_inputs, slot_index, 0, keepdims=False),
            arrived,
        )
        leaving_b, kept_values = layer_forward(entering_b, weights, position, offset)
        kept_list.append(kept_values)
        layer_out = jnp.where(
            is_valid,
            lax.dynamic_update_index_in_dim(layer_out, leaving_b, slot_index, 0),
            layer_out,
        )
        if tick_index + 1 < tick_total:
            arrived = passed_along(leaving_b, "section", 1)
    stashed = jax.tree.map(lambda *pieces: jnp.stack(pieces), *kept_list)
    weights_back = (
        lax.all_gather(norm_gains[0], "fsdp", axis=1, tiled=True),
        lax.all_gather(head_params[0], "fsdp", axis=1, tiled=True),
        lax.all_gather(conv_params[0], "fsdp", axis=1, tiled=True),
        lax.all_gather(ssm_gain[0], "fsdp", axis=0, tiled=True),
        lax.all_gather(w_in[0], "fsdp", axis=0, tiled=True),
        lax.all_gather(w_out[0], "fsdp", axis=0, tiled=True),
        lax.all_gather(w_qkv[0], "fsdp", axis=0, tiled=True),
        lax.all_gather(w_o[0], "fsdp", axis=0, tiled=True),
        lax.all_gather(w_gu[0], "fsdp", axis=0, tiled=True),
        lax.all_gather(w_down[0], "fsdp", axis=0, tiled=True),
    )
    own_cotangent = cotangent[:, 0]
    arrived_back = jnp.zeros_like(own_inputs[0])
    grad_inputs = jnp.zeros_like(own_inputs)
    small_sums = None
    product_list = []
    for tick_index in range(tick_total):
        micro_index = tick_index - (sections - 1 - section_index)
        is_valid = (micro_index >= 0) & (micro_index < micro_count)
        slot_index = jnp.clip(micro_index, 0, micro_count - 1)
        source = jnp.clip(micro_index + section_index, 0, tick_total - 1)
        kept_values = jax.tree.map(
            lambda stacked: lax.dynamic_index_in_dim(stacked, source, 0, keepdims=False), stashed
        )
        given_grad = jnp.where(
            is_valid,
            lax.dynamic_index_in_dim(own_cotangent, slot_index, 0, keepdims=False).astype(
                jnp.float32
            ),
            0.0,
        )
        grad_out = jnp.where(
            section_index == sections - 1, given_grad, arrived_back.astype(jnp.float32)
        )
        grad_enter_b, small_terms, products = layer_backward(
            grad_out, kept_values, weights_back, position, offset
        )
        if small_sums is None:
            small_sums = small_terms
        else:
            small_sums = jax.tree.map(jnp.add, small_sums, small_terms)
        product_list.append(products)
        grad_inputs = jnp.where(
            is_valid,
            lax.dynamic_update_index_in_dim(grad_inputs, grad_enter_b, slot_index, 0),
            grad_inputs,
        )
        if tick_index + 1 < tick_total:
            arrived_back = passed_along(grad_enter_b, "section", -1)
    product_pairs = jax.tree.map(lambda *pieces: jnp.concatenate(pieces, axis=0), *product_list)
    large_shards = [shard_grad(pair_item[0], pair_item[1]) for pair_item in product_pairs]
    grad_in_qkv = large_shards[0]
    small_shards = (
        lax.psum_scatter(
            small_sums[0].astype(jnp.bfloat16), "fsdp", scatter_dimension=1, tiled=True
        ).astype(jnp.float32),
        lax.psum_scatter(
            small_sums[1].astype(jnp.bfloat16), "fsdp", scatter_dimension=1, tiled=True
        ).astype(jnp.float32),
        lax.psum_scatter(
            small_sums[2].astype(jnp.bfloat16), "fsdp", scatter_dimension=1, tiled=True
        ).astype(jnp.float32),
        lax.psum_scatter(
            small_sums[3].astype(jnp.bfloat16), "fsdp", scatter_dimension=0, tiled=True
        ).astype(jnp.float32),
    )
    totals = (
        lax.psum(small_shards[0].astype(jnp.bfloat16), "ctx").astype(jnp.float32),
        lax.psum(small_shards[1].astype(jnp.bfloat16), "ctx").astype(jnp.float32),
        lax.psum(small_shards[2].astype(jnp.bfloat16), "ctx").astype(jnp.float32),
        lax.psum(small_shards[3].astype(jnp.bfloat16), "ctx").astype(jnp.float32),
        lax.psum(grad_in_qkv[:, :D_IN].astype(jnp.bfloat16), "ctx").astype(jnp.float32),
        lax.psum(large_shards[1].astype(jnp.bfloat16), "ctx").astype(jnp.float32),
        lax.psum(grad_in_qkv[:, D_IN:].astype(jnp.bfloat16), "ctx").astype(jnp.float32),
        lax.psum(large_shards[2].astype(jnp.bfloat16), "ctx").astype(jnp.float32),
        lax.psum(large_shards[3].astype(jnp.bfloat16), "ctx").astype(jnp.float32),
        lax.psum(large_shards[4].astype(jnp.bfloat16), "ctx").astype(jnp.float32),
    )
    return (
        layer_out[None, :, None],
        grad_inputs[None, :, None],
        totals[0][None],
        totals[1][None],
        totals[2][None],
        totals[3][None],
        totals[4][None],
        totals[5][None],
        totals[6][None],
        totals[7][None],
        totals[8][None],
        totals[9][None],
    )


def solution(mesh):
    in_specs = (
        P(None, "fsdp", "ctx", None),
        P(None, "fsdp", "ctx", None),
        P("section", None, "fsdp"),
        P("section", None, "fsdp"),
        P("section", None, "fsdp"),
        P("section", "fsdp"),
        P("section", "fsdp", None),
        P("section", "fsdp", None),
        P("section", "fsdp", None),
        P("section", "fsdp", None),
        P("section", "fsdp", None),
        P("section", "fsdp", None),
    )
    out_specs = (
        P("section", None, "fsdp", "ctx", None),
        P("section", None, "fsdp", "ctx", None),
        P("section", None, "fsdp"),
        P("section", None, "fsdp"),
        P("section", None, "fsdp"),
        P("section", "fsdp"),
        P("section", "fsdp", None),
        P("section", "fsdp", None),
        P("section", "fsdp", None),
        P("section", "fsdp", None),
        P("section", "fsdp", None),
        P("section", "fsdp", None),
    )
    return jax.shard_map(body, mesh=mesh, in_specs=in_specs, out_specs=out_specs, check_vma=False)
```

profile of v0, /device:TPU:0, one launch (start us, length us, event | category | flops | bytes accessed | tf_op | source)
XLA Modules:
  0.0 5017.7 jit_solution(12819016617360004872)
XLA Ops:
  37.0 37.2 all-gather
  76.5 398.4 %all-gather.39.cloned.1.call-done = bf16[1,2048,6704]{1,2,0:T(8,128)(2,1)} async-done(((bf16[1,512,6704]{1,2,0:T(8,128)(2,1)}), bf16[1,2048,6704]{1,2,0:T(8,128)(2,1)}) %all-gather.39.cloned.1.call-update) | async-done | bytes 27459600 | tf_op jit(solution)/shard_map/all_gather | solution.py:418
  517.7 72.5 %all-gather.35.cloned.1.call-done = bf16[1,2048,1536]{2,1,0:T(8,128)(2,1)} async-done(((bf16[1,512,1536]{2,1,0:T(8,128)(2,1)}), bf16[1,2048,1536]{2,1,0:T(8,128)(2,1)}) %all-gather.35.cloned.1.call-update) | async-done | bytes 6291472 | tf_op jit(solution)/shard_map/all_gather | solution.py:420
  634.6 39.6 all-gather.41.cloned.1.call-done
  674.2 16.1 while.87
  698.3 195.5 %all-gather.43.cloned.1.call-done = bf16[1,3072,2048]{2,1,0:T(8,128)(2,1)} async-done(((bf16[1,768,2048]{2,1,0:T(8,128)(2,1)}), bf16[1,3072,2048]{2,1,0:T(8,128)(2,1)}) %all-gather.43.cloned.1.call-update) | async-done | bytes 12582928 | tf_op jit(solution)/shard_map/all_gather | solution.py:419
  900.9 73.4 %all-gather.37.cloned.1.call-done = bf16[1,1024,2048]{2,1,0:T(8,128)(2,1)} async-done(((bf16[1,256,2048]{2,1,0:T(8,128)(2,1)}), bf16[1,1024,2048]{2,1,0:T(8,128)(2,1)}) %all-gather.37.cloned.1.call-update) | async-done | bytes 4194320 | tf_op jit(solution)/shard_map/all_gather | solution.py:421
  977.5 558.2 %all-gather.45.cloned.1.call-done = bf16[1,2048,8192]{2,1,0:T(8,128)(2,1)} async-done(((bf16[1,512,8192]{2,1,0:T(8,128)(2,1)}), bf16[1,2048,8192]{2,1,0:T(8,128)(2,1)}) %all-gather.45.cloned.1.call-update) | async-done | bytes 33554448 | tf_op jit(solution)/shard_map/all_gather | solution.py:422
  1535.6 25.6 fusion.13
  1561.3 260.9 %all-gather.47.cloned.1.call-done = bf16[1,4096,2048]{2,1,0:T(8,128)(2,1)} async-done(((bf16[1,1024,2048]{2,1,0:T(8,128)(2,1)}), bf16[1,4096,2048]{2,1,0:T(8,128)(2,1)}) %all-gather.47.cloned.1.call-update) | async-done | bytes 16777232 | tf_op jit(solution)/shard_map/all_gather | solution.py:423
  1908.9 42.8 all-gather.49.cloned.1.call-done
  2138.0 15.6 while.89
  2207.2 17.6 fusion.492
  2425.0 16.7 fusion.484
  2616.1 16.6 fusion.476
  2789.2 15.8 convolution_convert_fusion
  2837.0 15.9 convolution_convert_fusion.1
  2856.8 501.7 %reduce-scatter.24.cloned.1.call-done = bf16[512,8240]{0,1:T(8,128)(2,1)} async-done(((bf16[2048,8240]{0,1:T(8,128)(2,1)}), bf16[512,8240]{0,1:T(8,128)(2,1)}) %reduce-scatter.24.cloned.1.call-update) | async-done | bytes 8437776 | tf_op jit(solution)/shard_map/reduce_scatter | solution.py:389
  3367.5 72.7 %reduce-scatter.28.cloned.1.call-done = bf16[256,2048]{1,0:T(8,128)(2,1)} async-done(((bf16[1024,2048]{1,0:T(8,128)(2,1)}), bf16[256,2048]{1,0:T(8,128)(2,1)}) %reduce-scatter.28.cloned.1.call-update) | async-done | bytes 1048592 | tf_op jit(solution)/shard_map/reduce_scatter | solution.py:389
  3440.2 215.3 %reduce-scatter.26.cloned.1.call-done = bf16[768,2048]{1,0:T(8,128)(2,1)} async-done(((bf16[3072,2048]{1,0:T(8,128)(2,1)}), bf16[768,2048]{1,0:T(8,128)(2,1)}) %reduce-scatter.26.cloned.1.call-update) | async-done | bytes 3145744 | tf_op jit(solution)/shard_map/reduce_scatter | solution.py:389
  3655.5 284.4 %reduce-scatter.30.cloned.1.call-done = bf16[1024,2048]{1,0:T(8,128)(2,1)} async-done(((bf16[4096,2048]{1,0:T(8,128)(2,1)}), bf16[1024,2048]{1,0:T(8,128)(2,1)}) %reduce-scatter.30.cloned.1.call-update) | async-done | bytes 4194320 | tf_op jit(solution)/shard_map/reduce_scatter | solution.py:389
  3939.9 555.0 %reduce-scatter.36.cloned.1.call-done = bf16[512,8192]{1,0:T(8,128)(2,1)} async-done(((bf16[2048,8192]{1,0:T(8,128)(2,1)}), bf16[512,8192]{1,0:T(8,128)(2,1)}) %reduce-scatter.36.cloned.1.call-update) | async-done | bytes 8388624
  4524.3 21.8 reduce-scatter.34.cloned.1.call-done
  4560.7 416.5 %all-reduce.80.cloned.1.call-done = (bf16[1,512,1536]{1,2,0:T(8,128)(2,1)}, bf16[1,512,6704]{1,2,0:T(8,128)(2,1)}, bf16[1,768,2048]{2,1,0:T(8,128)(2,1)}, bf16[1...) async-done(((bf16[1,512,1536]{1,2,0:T(8,128)(2,1)}, bf16[1,512,6704]{1,2,0:T(8,128)(2,1)}, bf16[1,768,2048]{2,1,0:T(8,128)(2,1)}, ...) | async-done | bytes 25214992 | tf_op jit(solution)/shard_map/psum | solution.py:529
  (1532 shorter events, 1170.2 us)
Async XLA Ops:
  7.2 467.7 %all-gather.39.cloned.1.call-start = ((), (), s32[]{:S(2)}) async-start(), calls=%async_computation.19 | async-start | bytes 34324480 | tf_op jit(solution)/shard_map/all_gather | solution.py:418
  8.0 582.3 %all-gather.35.cloned.1.call-start = ((), (), s32[]{:S(2)}) async-start(), calls=%async_computation.17 | async-start | bytes 7864320 | tf_op jit(solution)/shard_map/all_gather | solution.py:420
  8.7 665.5 %all-gather.41.cloned.1.call-start = ((), (), s32[]{:S(2)}) async-start(), calls=%async_computation.20 | async-start | bytes 15728640 | tf_op jit(solution)/shard_map/all_gather | solution.py:33
  497.6 396.2 %all-gather.43.cloned.1.call-start = ((), (), s32[]{:S(2)}) async-start(), calls=%async_computation.21 | async-start | bytes 15728640 | tf_op jit(solution)/shard_map/all_gather | solution.py:419
  498.2 476.0 %all-gather.37.cloned.1.call-start = ((), (), s32[]{:S(2)}) async-start(), calls=%async_computation.18 | async-start | bytes 5242880 | tf_op jit(solution)/shard_map/all_gather | solution.py:421
  498.8 1036.8 %all-gather.45.cloned.1.call-start = ((), (), s32[]{:S(2)}) async-start(), calls=%async_computation.22 | async-start | bytes 41943040 | tf_op jit(solution)/shard_map/all_gather | solution.py:422
  499.4 1322.8 %all-gather.47.cloned.1.call-start = ((), (), s32[]{:S(2)}) async-start(), calls=%async_computation.23 | async-start | bytes 20971520 | tf_op jit(solution)/shard_map/all_gather | solution.py:423
  500.1 1451.6 %all-gather.49.cloned.1.call-start = ((), (), s32[]{:S(2)}) async-start(), calls=%async_computation.24 | async-start | bytes 15728640 | tf_op jit(solution)/shard_map/all_gather | solution.py:33
  1866.8 271.1 %all-gather.51.cloned.1.call-start = ((), (), s32[]{:S(2)}) async-start(), calls=%async_computation.25 | async-start | bytes 15728640 | tf_op jit(solution)/shard_map/all_gather | solution.py:33
  2050.0 288.2 %reduce-scatter.18.cloned.1.call-start = ((), (), s32[]{:S(2)}) async-start(), calls=%async_computation.10 | async-start | bytes 655360 | tf_op jit(solution)/shard_map/reduce_scatter | solution.py:362
  2282.4 72.2 %all-gather.53.cloned.1.call-start = ((), (), s32[]{:S(2)}) async-start(), calls=%async_computation.26 | async-start | bytes 7864320 | tf_op jit(solution)/shard_map/all_gather | solution.py:53
  2297.0 235.7 %reduce-scatter.20.cloned.1.call-start = ((), (), s32[]{:S(2)}) async-start(), calls=%async_computation.11 | async-start | bytes 655360 | tf_op jit(solution)/shard_map/reduce_scatter | solution.py:362
  2475.4 69.4 %all-gather.55.cloned.1.call-start = ((), (), s32[]{:S(2)}) async-start(), calls=%async_computation.27 | async-start | bytes 7864320 | tf_op jit(solution)/shard_map/all_gather | solution.py:53
  2487.9 231.2 %reduce-scatter.22.cloned.1.call-start = ((), (), s32[]{:S(2)}) async-start(), calls=%async_computation.12 | async-start | bytes 655360 | tf_op jit(solution)/shard_map/reduce_scatter | solution.py:362
  2589.7 11.0 collective-permute-start.8
  2666.1 69.4 %all-gather.57.cloned.1.call-start = ((), (), s32[]{:S(2)}) async-start(), calls=%async_computation.28 | async-start | bytes 7864320 | tf_op jit(solution)/shard_map/all_gather | solution.py:53
  2679.8 678.8 %reduce-scatter.24.cloned.1.call-start = ((), (), s32[]{:S(2)}) async-start(), calls=%async_computation.13 | async-start | bytes 42188800 | tf_op jit(solution)/shard_map/reduce_scatter | solution.py:389
  2805.1 635.1 %reduce-scatter.28.cloned.1.call-start = ((), (), s32[]{:S(2)}) async-start(), calls=%async_computation.15 | async-start | bytes 5242880 | tf_op jit(solution)/shard_map/reduce_scatter | solution.py:389
  2809.7 845.8 %reduce-scatter.26.cloned.1.call-start = ((), (), s32[]{:S(2)}) async-start(), calls=%async_computation.14 | async-start | bytes 15728640 | tf_op jit(solution)/shard_map/reduce_scatter | solution.py:389
  2817.8 1122.1 %reduce-scatter.30.cloned.1.call-start = ((), (), s32[]{:S(2)}) async-start(), calls=%async_computation.16 | async-start | bytes 20971520 | tf_op jit(solution)/shard_map/reduce_scatter | solution.py:389
  2834.1 1660.9 %reduce-scatter.36.cloned.1.call-start = ((), (), s32[]{:S(2)}) async-start(), calls=%async_computation.31 | async-start | bytes 41943040
  2853.1 1670.0 %reduce-scatter.32.cloned.1.call-start = ((), (), s32[]{:S(2)}) async-start(), calls=%async_computation.29 | async-start | bytes 655360
  2855.2 1690.8 %reduce-scatter.34.cloned.1.call-start = ((), (), s32[]{:S(2)}) async-start(), calls=%async_computation.30 | async-start | bytes 1146880
  2856.8 2120.4 %all-reduce.80.cloned.1.call-start = ((), (), s32[]{:S(2)}) async-start(), calls=%async_computation.32 | async-start | bytes 50429952 | tf_op jit(solution)/shard_map/psum | solution.py:529
  (435 other events, 12538.6 us)
Sparse Core Ops, SparseCore 0:
  9.6 465.2 all-gather.38
  476.5 113.6 all-gather.34
  592.4 81.7 all-gather.40
  675.6 218.1 all-gather.42
  895.3 78.9 all-gather.36
  975.7 559.9 all-gather.44
  1537.2 284.9 all-gather.46
  1867.0 84.7 all-gather.48
  2050.2 84.8 all-gather.50
  2282.6 23.3 reduce-scatter.17
  2308.2 46.3 all-gather.52
  2475.6 20.7 reduce-scatter.19
  2498.5 46.3 all-gather.54
  2666.3 20.7 reduce-scatter.21
  2689.1 46.3 all-gather.56
  2805.2 553.3 reduce-scatter.23
  3361.3 78.8 reduce-scatter.27
  3443.1 212.3 reduce-scatter.25
  3658.5 281.3 reduce-scatter.29
  3942.1 552.7 reduce-scatter.35
  4497.3 22.3 reduce-scatter.31
  4522.7 23.3 reduce-scatter.33
  4550.1 427.0 all-reduce.79
where the time goes:
time: 5030 us; the launch traced here: 5020 us
  waiting for transfers between devices  3780 us (75%)
  matrix products  523 us (10%)
  local copies, waits for them, and re-layouts  273 us (5%)
  other arithmetic  239 us (5%)
  blocking collectives  161 us (3%)
    reduce_scatter x4, waiting for transfers between devices, shard_grad(): lax.psum_scatter(lax.dot_general(left_rows, right_rows, (((0,), (0,)), ((...  1070 us
    unnamed x26, waiting for transfers between devices  581 us
    all_gather x1, waiting for transfers between devices, body(): lax.all_gather(w_gu[0], 'fsdp', axis=0, tiled=True)  558 us
    psum x1, waiting for transfers between devices, body(): lax.psum(grad_in_qkv[:, D_IN:].astype(jnp.bfloat16), 'ctx')  416 us
    all_gather x1, waiting for transfers between devices, body(): lax.all_gather(w_in[0], 'fsdp', axis=0, tiled=True)  398 us
    all_gather x1, waiting for transfers between devices, body(): lax.all_gather(w_down[0], 'fsdp', axis=0, tiled=True)  261 us
    all_gather x1, waiting for transfers between devices, body(): lax.all_gather(w_out[0], 'fsdp', axis=0, tiled=True)  196 us
    dot_general x18, matrix products, dot_right_t(): lax.dot_general(left_side, right_side, (((1,), (1,)), ((), ())), preferre...  171 us
  transfers between devices with their start and end apart: 33, of which 22 were waited for; matrix products, arithmetic and copies ran while one was open for 9% of the time, Pallas kernels for 0%

commit v1 on v0

v1 whole, which is shorter than its diff:
```python
import functools

import jax
import jax.numpy as jnp
from jax import lax
from jax.experimental import pallas as pl
from jax.experimental.pallas import tpu as pltpu
from jax.sharding import Mesh
from jax.sharding import PartitionSpec as P

D = 2048
FF = 4096
SSM_HEADS = 48
SSM_HEAD = 64
STATE = 256
Q_HEADS = 8
KV_HEADS = 2
HEAD_DIM = 128
CONV_K = 4
D_SSM = 3072
CONV_W = 3584
D_IN = 6704
ATT = 1024
KV = 256
EPSILON = 1e-05
ROPE_BASE = 10000.0
NEGATIVE = -1e30
HIGHEST = lax.Precision.HIGHEST

RANKS = 4
R_HEADS = SSM_HEADS // RANKS
R_SSM = D_SSM // RANKS
R_BC = 2 * STATE // RANKS
R_CONV = R_SSM + R_BC
R_ATT = ATT // RANKS
R_FF = FF // RANKS
R_OUT = R_SSM + R_ATT
HALF = 1024
MESH = pl.DeviceIdType.MESH
BF = jnp.bfloat16
F32 = jnp.float32


def rank_place():
    return 2 * lax.axis_index("section") + lax.axis_index("y")


def rank_id(rank):
    return {"section": rank // 2, "y": lax.rem(rank, 2)}


def greet(me):
    barrier = pltpu.get_barrier_semaphore()
    for step in range(1, RANKS):
        pl.semaphore_signal(
            barrier, inc=1, device_id=rank_id(lax.rem(me + step, RANKS)), device_id_type=MESH
        )
    pl.semaphore_wait(barrier, RANKS - 1)


def swap_kernel(with_stat, *refs):
    if with_stat:
        send_ref, stat_ref, out_ref, all_stat_ref, send_sem, recv_sem, stat_send, stat_recv = refs
    else:
        send_ref, out_ref, send_sem, recv_sem = refs
    me = rank_place()
    greet(me)
    copies = []
    for step in range(1, RANKS):
        other = lax.rem(me + step, RANKS)
        copies.append(
            pltpu.make_async_remote_copy(
                src_ref=send_ref.at[other] if len(send_ref.shape) == 3 else send_ref,
                dst_ref=out_ref.at[me],
                send_sem=send_sem.at[step - 1],
                recv_sem=recv_sem.at[step - 1],
                device_id=rank_id(other),
                device_id_type=MESH,
            )
        )
        if with_stat:
            copies.append(
                pltpu.make_async_remote_copy(
                    src_ref=stat_ref,
                    dst_ref=all_stat_ref.at[me],
                    send_sem=stat_send.at[step - 1],
                    recv_sem=stat_recv.at[step - 1],
                    device_id=rank_id(other),
                    device_id_type=MESH,
                )
            )
    for copy in copies:
        copy.start()
    if len(send_ref.shape) == 3:
        out_ref[me] = send_ref[me]
    else:
        out_ref[me] = send_ref[...]
    if with_stat:
        all_stat_ref[me] = stat_ref[...]
    for copy in copies:
        copy.wait()


VMEM_SPEC = pl.BlockSpec(memory_space=pltpu.VMEM)


def swap(values, collective_id, stat=None):
    out_shape = [jax.ShapeDtypeStruct((RANKS,) + values.shape[-2:], values.dtype)]
    scratch = [pltpu.SemaphoreType.DMA((RANKS - 1,)), pltpu.SemaphoreType.DMA((RANKS - 1,))]
    args = [values]
    if stat is not None:
        out_shape.append(jax.ShapeDtypeStruct((RANKS,) + stat.shape, stat.dtype))
        scratch += scratch
        args.append(stat)
    out = pl.pallas_call(
        functools.partial(swap_kernel, stat is not None),
        out_shape=out_shape,
        in_specs=[VMEM_SPEC] * len(args),
        out_specs=[VMEM_SPEC] * len(out_shape),
        scratch_shapes=scratch,
        compiler_params=pltpu.CompilerParams(
            collective_id=collective_id, has_side_effects=True, vmem_limit_bytes=32 * 2**20
        ),
    )(*args)
    return out if stat is not None else out[0]


def scatter_sum(me, rows, part_ref, slots, send_sem, recv_sem):
    copies = []
    for step in range(1, RANKS):
        other = lax.rem(me + step, RANKS)
        copies.append(
            pltpu.make_async_remote_copy(
                src_ref=part_ref.at[pl.ds(pl.multiple_of(other * rows, rows), rows)],
                dst_ref=slots.at[step - 1],
                send_sem=send_sem.at[step - 1],
                recv_sem=recv_sem.at[step - 1],
                device_id=rank_id(other),
                device_id_type=MESH,
            )
        )
    for copy in copies:
        copy.start()
    total = part_ref[pl.ds(pl.multiple_of(me * rows, rows), rows), :].astype(F32)
    for step, copy in enumerate(copies):
        copy.wait()
        total = total + slots[step].astype(F32)
    return total


def spread(me, rows, out_ref, send_sem, recv_sem):
    here = pl.ds(pl.multiple_of(me * rows, rows), rows)
    copies = []
    for step in range(1, RANKS):
        copies.append(
            pltpu.make_async_remote_copy(
                src_ref=out_ref.at[here],
                dst_ref=out_ref.at[here],
                send_sem=send_sem.at[step - 1],
                recv_sem=recv_sem.at[step - 1],
                device_id=rank_id(lax.rem(me + step, RANKS)),
                device_id_type=MESH,
            )
        )
    for copy in copies:
        copy.start()
    for copy in copies:
        copy.wait()


def mid_kernel(part_ref, resid_ref, gain_ref, mid_ref, out_ref, slots, s1, r1, s2, r2):
    rows = resid_ref.shape[0]
    me = rank_place()
    greet(me)
    mid = scatter_sum(me, rows, part_ref, slots, s1, r1) + resid_ref[...].astype(F32)
    mid_ref[...] = mid
    scale = lax.rsqrt(jnp.mean(mid * mid, axis=-1, keepdims=True) + EPSILON)
    out_ref[pl.ds(pl.multiple_of(me * rows, rows), rows), :] = (
        mid * scale * gain_ref[...].astype(F32)
    ).astype(BF)
    spread(me, rows, out_ref, s2, r2)


def end_kernel(part_ref, resid_ref, out_ref, slots, s1, r1, s2, r2):
    rows = resid_ref.shape[0]
    me = rank_place()
    greet(me)
    total = scatter_sum(me, rows, part_ref, slots, s1, r1) + resid_ref[...]
    out_ref[pl.ds(pl.multiple_of(me * rows, rows), rows), :] = total.astype(BF)
    spread(me, rows, out_ref, s2, r2)


def back_kernel(
    part_ref, given_ref, value_ref, gain_ref, wide_ref, out_ref, gain_grad_ref, slots, s1, r1, s2, r2
):
    rows = given_ref.shape[0]
    me = rank_place()
    greet(me)
    grad = scatter_sum(me, rows, part_ref, slots, s1, r1)
    value = value_ref[...]
    scale = lax.rsqrt(jnp.mean(value * value, axis=-1, keepdims=True) + EPSILON)
    unit = value * scale
    gain_grad_ref[...] = jnp.sum(grad * unit, axis=0, keepdims=True)
    scaled = grad * gain_ref[...].astype(F32)
    total = given_ref[...] + scale * (
        scaled - unit * jnp.mean(scaled * unit, axis=-1, keepdims=True)
    )
    wide_ref[...] = total
    out_ref[pl.ds(pl.multiple_of(me * rows, rows), rows), :] = total.astype(BF)
    spread(me, rows, out_ref, s2, r2)


def rank_call(kernel, out_shape, collective_id, rows, *args):
    return pl.pallas_call(
        kernel,
        out_shape=out_shape,
        in_specs=[VMEM_SPEC] * len(args),
        out_specs=[VMEM_SPEC] * len(out_shape),
        scratch_shapes=[pltpu.VMEM((RANKS - 1, rows, D), BF)]
        + [pltpu.SemaphoreType.DMA((RANKS - 1,))] * 4,
        compiler_params=pltpu.CompilerParams(
            collective_id=collective_id, has_side_effects=True, vmem_limit_bytes=32 * 2**20
        ),
    )(*args)


def mid_step(part, resid, gain):
    rows = resid.shape[0]
    return rank_call(
        mid_kernel,
        [jax.ShapeDtypeStruct((rows, D), F32), jax.ShapeDtypeStruct(part.shape, BF)],
        3,
        rows,
        part,
        resid,
        gain[None],
    )


def end_step(part, resid):
    rows = resid.shape[0]
    return rank_call(end_kernel, [jax.ShapeDtypeStruct(part.shape, BF)], 4, rows, part, resid)[0]


def back_step(part, given, value, gain):
    rows = given.shape[0]
    return rank_call(
        back_kernel,
        [
            jax.ShapeDtypeStruct((rows, D), F32),
            jax.ShapeDtypeStruct(part.shape, BF),
            jax.ShapeDtypeStruct((1, D), F32),
        ],
        5,
        rows,
        part,
        given,
        value,
        gain[None],
    )


def narrow(values):
    return values.astype(BF)


def dot(left, right):
    return jnp.dot(left, right, preferred_element_type=F32)


def dot_t(left, right):
    return lax.dot_general(left, right, (((1,), (1,)), ((), ())), preferred_element_type=F32)


def t_dot(left, right):
    return lax.dot_general(left, right, (((0,), (0,)), ((), ())), preferred_element_type=F32)


def columns(array, start, width):
    return lax.dynamic_slice_in_dim(array, start, width, axis=1)


def cut_rows(array, start, width):
    return lax.dynamic_slice_in_dim(array, start, width, axis=0)


def rms(values, gain):
    return values * lax.rsqrt(jnp.mean(values * values, axis=-1, keepdims=True) + EPSILON) * gain


def rotary(values, turning):
    length, width = values.shape
    half = HEAD_DIM // 2
    frequency = ROPE_BASE ** (-jnp.arange(half, dtype=F32) / half)
    angles = jnp.arange(length, dtype=F32)[:, None] * frequency[None, :]
    cosine = jnp.cos(angles)[:, None, :]
    sine = turning * jnp.sin(angles)[:, None, :]
    halves = values.reshape(length, width // HEAD_DIM, 2, half)
    first, second = halves[:, :, 0], halves[:, :, 1]
    return jnp.stack(
        [first * cosine - second * sine, second * cosine + first * sine], axis=2
    ).reshape(length, width)


def causal(length):
    position = jnp.arange(length)
    return position[:, None] >= position[None, :]


def shifted(values, steps):
    if steps == 0:
        return values
    blank = jnp.zeros((abs(steps), values.shape[1]), values.dtype)
    if steps > 0:
        return jnp.concatenate([blank, values[:-steps]], axis=0)
    return jnp.concatenate([values[-steps:], blank], axis=0)


def conv_sum(rows, table):
    wide = rows.astype(F32)
    total = table[CONV_K][None, :]
    for tap in range(CONV_K):
        total = total + table[tap][None, :] * shifted(wide, CONV_K - 1 - tap)
    return total


def decays(dt_raw, heads):
    dt = jax.nn.softplus(dt_raw + heads[0][None, :])
    step = -dt * jnp.exp(heads[1])[None, :]
    length = dt.shape[0]
    running = jnp.dot(causal(length).astype(F32), step, precision=HIGHEST)
    return dt, step, running


def decay_table(running):
    length = running.shape[0]
    turned = running.T
    gap = turned[:, :, None] - turned[:, None, :]
    return jnp.exp(jnp.where(causal(length)[None], gap, NEGATIVE))


def by_head(values):
    return values.reshape(values.shape[0], R_HEADS, SSM_HEAD)


def scan_forward(x, b_rows, c_rows, dt_raw, heads):
    dt, _, running = decays(dt_raw, heads)
    mixing = dot_t(c_rows, b_rows)
    weights = narrow(decay_table(running) * mixing[None] * dt.T[:, None, :])
    x_heads = by_head(x)
    result = jnp.einsum("hts,shp->thp", weights, x_heads, preferred_element_type=F32)
    return (result + heads[2][None, :, None] * x_heads.astype(F32)).reshape(x.shape)


def scan_backward(x, b_rows, c_rows, dt_raw, heads, grad_y):
    dt, step, running = decays(dt_raw, heads)
    length = x.shape[0]
    mixing = dot_t(c_rows, b_rows)
    table = decay_table(running)
    dt_t = dt.T
    x_heads = by_head(x)
    grad_heads = by_head(narrow(grad_y))
    grad_weights = jnp.einsum("thp,shp->hts", grad_heads, x_heads, preferred_element_type=F32)
    faded = grad_weights * table
    weights = table * mixing[None] * dt_t[:, None, :]
    grad_x = jnp.einsum("hts,thp->shp", narrow(weights), grad_heads, preferred_element_type=F32)
    grad_y_heads = by_head(grad_y)
    grad_x = grad_x + heads[2][None, :, None] * grad_y_heads
    grad_skip = jnp.sum(grad_y_heads * x_heads.astype(F32), axis=(0, 2))
    grad_mixing = narrow(jnp.sum(faded * dt_t[:, None, :], axis=0))
    grad_c = dot(grad_mixing, b_rows)
    grad_b = t_dot(grad_mixing, c_rows)
    plain = faded * mixing[None]
    grad_dt = jnp.sum(plain, axis=1)
    grad_gap = plain * dt_t[:, None, :]
    grad_running = jnp.sum(grad_gap, axis=2) - jnp.sum(grad_gap, axis=1)
    grad_step = jnp.dot(grad_running, causal(length).astype(F32), precision=HIGHEST).T
    grad_dt = grad_dt.T - grad_step * jnp.exp(heads[1])[None, :]
    grad_log = jnp.sum(grad_step * step, axis=0)
    grad_raw = grad_dt * jax.nn.sigmoid(dt_raw + heads[0][None, :])
    grad_table = jnp.stack([jnp.sum(grad_raw, axis=0), grad_log, grad_skip])
    return grad_x.reshape(x.shape), grad_b, grad_c, grad_raw, grad_table


def attend(query, key, value):
    length = query.shape[0]
    heads = query.reshape(length, -1, HEAD_DIM)
    scores = jnp.einsum("qhd,sd->hqs", heads, key, preferred_element_type=F32) * HEAD_DIM**-0.5
    scores = jnp.where(causal(length)[None], scores, NEGATIVE)
    weights = jnp.exp(scores - jnp.max(scores, axis=-1, keepdims=True))
    probs = weights / jnp.sum(weights, axis=-1, keepdims=True)
    mixed = jnp.einsum("hqs,sd->qhd", narrow(probs), value, preferred_element_type=F32)
    return narrow(mixed.reshape(query.shape)), probs


def attend_back(query, key, value, probs, grad_out):
    length = query.shape[0]
    heads = query.reshape(length, -1, HEAD_DIM)
    grad_heads = grad_out.reshape(length, -1, HEAD_DIM)
    grad_probs = jnp.einsum("qhd,sd->hqs", grad_heads, value, preferred_element_type=F32)
    grad_scores = narrow(
        probs * (grad_probs - jnp.sum(probs * grad_probs, axis=-1, keepdims=True))
    )
    scale = HEAD_DIM**-0.5
    grad_query = jnp.einsum("hqs,sd->qhd", grad_scores, key, preferred_element_type=F32) * scale
    grad_key = jnp.einsum("hqs,qhd->sd", grad_scores, heads, preferred_element_type=F32) * scale
    grad_value = jnp.einsum("hqs,qhd->sd", narrow(probs), grad_heads, preferred_element_type=F32)
    return grad_query.reshape(query.shape), grad_key, grad_value


def flip(value, axis):
    return lax.ppermute(value, axis, [(0, 1), (1, 0)])


def layer_forward(entering, resid, weights, small, first):
    s, y = lax.axis_index("section"), lax.axis_index("y")
    length = entering.shape[0]
    x1 = narrow(rms(entering.astype(F32), small["gain0"][None, :]))
    left = dot(x1, weights["in"][0])
    right = dot(x1, weights["in"][1])
    dt_raw = columns(dot(x1, weights["dt"]), R_HEADS * (2 * s + y), R_HEADS)
    xbc = narrow(left[:, :R_CONV])
    u = narrow(jax.nn.silu(conv_sum(xbc, small["conv"])))
    kv_raw = left[:, R_CONV:]
    kv = narrow(jnp.where(y == 0, rotary(kv_raw, 1.0), kv_raw))
    shared = swap(jnp.concatenate([u[:, R_SSM:], kv], axis=1), 0)
    b_rows = jnp.concatenate([shared[0, :, :R_BC], shared[1, :, :R_BC]], axis=1)
    c_rows = jnp.concatenate([shared[2, :, :R_BC], shared[3, :, :R_BC]], axis=1)
    pair = lax.dynamic_slice_in_dim(shared, 2 * s, 2, axis=0)[:, :, R_BC:]
    key, value = pair[0], pair[1]
    z = right[:, :R_SSM]
    query = narrow(rotary(right[:, R_SSM:], 1.0))
    o, probs = attend(query, key, value)
    x = u[:, :R_SSM]
    scan = scan_forward(x, b_rows, c_rows, dt_raw, small["heads"])
    gated = scan * jax.nn.silu(z)
    squares = jnp.sum(gated * gated, axis=1)
    scaled = narrow(gated * small["ssm_gain"][None, :])
    message = to_rows(scaled, o)
    stat = jnp.broadcast_to(squares[None, :], (8, length))
    got, stats = swap(message, 1, stat)
    spread_of = lax.rsqrt(jnp.sum(stats[:, 0, :], axis=0) / D_SSM + EPSILON)
    wide = jnp.transpose(got, (1, 0, 2)).reshape(length, R_OUT)
    is_ssm = small["is_ssm"][None, :]
    mo = narrow(jnp.where(is_ssm, wide.astype(F32) * spread_of[:, None], wide.astype(F32)))
    part = jnp.concatenate([dot(mo, weights["out"][0]), dot(mo, weights["out"][1])], axis=1)
    mid, x2 = mid_step(narrow(part), resid, small["gain1"])
    gate = dot(x2, weights["gu"][0])
    up = dot(x2, weights["gu"][1])
    act = narrow(jax.nn.silu(gate) * up)
    part2 = jnp.concatenate([dot(act, weights["down"][0]), dot(act, weights["down"][1])], axis=1)
    leaving = end_step(narrow(part2), mid)
    kept = dict(
        resid=resid, x1=x1, xbc=xbc, u=u, b=b_rows, c=c_rows, key=key, value=value, query=query,
        probs=probs, z=z, dt_raw=dt_raw, scan=scan, spread=spread_of, mo=mo, mid=mid, x2=x2,
        gate=gate, up=up, act=act,
    )
    return leaving, kept


def to_rows(ssm_part, att_part):
    length = ssm_part.shape[0]
    nz = lax.axis_size("fsdp")
    inner = nz // RANKS
    a = ssm_part.reshape(length, inner, RANKS, R_SSM // nz)
    b = att_part.reshape(length, inner, RANKS, R_ATT // nz)
    both = jnp.concatenate([a, b], axis=3)
    return jnp.transpose(both, (2, 0, 1, 3)).reshape(RANKS, length, R_OUT // RANKS)


def from_rows(got):
    length = got.shape[1]
    nz = lax.axis_size("fsdp")
    inner = nz // RANKS
    both = jnp.transpose(got.reshape(RANKS, length, inner, R_OUT // nz), (1, 2, 0, 3))
    a = both[..., : R_SSM // nz].reshape(length, R_SSM)
    b = both[..., R_SSM // nz :].reshape(length, R_ATT)
    return a, b


def layer_backward(grad, given, kept, weights, small):
    s, y = lax.axis_index("section"), lax.axis_index("y")
    core = lax.axis_index("core")
    length = grad.shape[0]
    down, gu, out, win = weights["down"], weights["gu"], weights["out"], weights["in"]

    def product(left, right, order):
        mine = jnp.where(core == 0, right[0], right[1])
        theirs = jnp.where(core == 0, right[1], right[0])
        left_two = jnp.concatenate([left, flip(left, "core")], axis=0)
        right_two = jnp.concatenate([mine, flip(theirs, "core")], axis=0)
        return narrow(t_dot(left_two, right_two))

    halves = lambda v: (v[:, :HALF], v[:, HALF:])
    g0, g1 = halves(grad)
    grad_act = dot_t(g0, down[0]) + dot_t(g1, down[1])
    gate, up = kept["gate"], kept["up"]
    sig = jax.nn.sigmoid(gate)
    d_gate = narrow(grad_act * up * (sig * (1.0 + gate * (1.0 - sig))))
    d_up = narrow(grad_act * gate * sig)
    part = dot_t(d_gate, gu[0]) + dot_t(d_up, gu[1])
    d_mid, db, grad_gain1 = back_step(narrow(part), given, kept["mid"], small["gain1"])
    b0, b1 = halves(db)
    d_mo = dot_t(b0, out[0]) + dot_t(b1, out[1])
    mo = kept["mo"]
    is_ssm = small["is_ssm"][None, :]
    stat_row = jnp.sum(jnp.where(is_ssm, d_mo * mo.astype(F32), 0.0), axis=1)
    stat = jnp.broadcast_to(stat_row[None, :], (8, length))
    blocks = jnp.transpose(narrow(d_mo).reshape(length, RANKS, R_OUT // RANKS), (1, 0, 2))
    got, stats = swap(blocks, 1, stat)
    overlap = jnp.sum(stats[:, 0, :], axis=0)[:, None]
    d_norm, d_o = from_rows(got)
    d_norm = d_norm.astype(F32)
    spread_of = kept["spread"][:, None]
    scan, z = kept["scan"], kept["z"]
    sig_z = jax.nn.sigmoid(z)
    silu_z = z * sig_z
    gated = scan * silu_z
    grad_ssm_gain = jnp.sum(d_norm * gated * spread_of, axis=0)
    d_gated = spread_of * d_norm * small["ssm_gain"][None, :] - gated * (
        spread_of * spread_of * overlap * (1.0 / D_SSM)
    )
    d_scan = d_gated * silu_z
    d_z = d_gated * scan * (sig_z * (1.0 + z * (1.0 - sig_z)))
    d_query, d_key, d_value = attend_back(
        kept["query"], kept["key"], kept["value"], kept["probs"], d_o
    )
    u = kept["u"]
    d_x, d_b, d_c, d_dt, grad_heads = scan_backward(
        u[:, :R_SSM], kept["b"], kept["c"], kept["dt_raw"], small["heads"], d_scan
    )
    message = jnp.stack(
        [
            jnp.concatenate([d_b[:, :R_BC], d_key], axis=1),
            jnp.concatenate([d_b[:, R_BC:], d_value], axis=1),
            jnp.concatenate([d_c[:, :R_BC], d_key], axis=1),
            jnp.concatenate([d_c[:, R_BC:], d_value], axis=1),
        ]
    )
    back = swap(narrow(message), 2).astype(F32)
    d_bc = back[0, :, :R_BC] + back[1, :, :R_BC] + back[2, :, :R_BC] + back[3, :, :R_BC]
    d_kv = jnp.sum(lax.dynamic_slice_in_dim(back, 2 * s, 2, axis=0)[:, :, R_BC:], axis=0)
    d_kv = jnp.where(y == 0, rotary(d_kv, -1.0), d_kv)
    d_u = jnp.concatenate([d_x, d_bc], axis=1)
    xbc = kept["xbc"]
    table = small["conv"]
    before = conv_sum(xbc, table)
    sig_c = jax.nn.sigmoid(before)
    d_before = d_u * (sig_c * (1.0 + before * (1.0 - sig_c)))
    wide = xbc.astype(F32)
    grad_conv = jnp.stack(
        [jnp.sum(d_before * shifted(wide, CONV_K - 1 - tap), axis=0) for tap in range(CONV_K)]
        + [jnp.sum(d_before, axis=0)]
    )
    d_xbc = 0.0
    for tap in range(CONV_K):
        d_xbc = d_xbc + table[tap][None, :] * shifted(d_before, tap - CONV_K + 1)
    d_left = narrow(jnp.concatenate([d_xbc, d_kv], axis=1))
    d_right = narrow(jnp.concatenate([d_z, rotary(d_query, -1.0)], axis=1))
    d_dt_b = narrow(d_dt)
    dt_own = columns(weights["dt"], R_HEADS * (2 * s + y), R_HEADS)
    part = dot_t(d_left, win[0]) + dot_t(d_right, win[1]) + dot_t(d_dt_b, dt_own)
    _, entering_grad, grad_gain0 = back_step(
        narrow(part), d_mid, kept["resid"].astype(F32), small["gain0"]
    )
    shards = dict(
        down=product(kept["act"], (g0, g1), 0),
        gu=product(kept["x2"], (d_gate, d_up), 1),
        out=product(mo, (b0, b1), 2),
    )
    shards["in"] = product(kept["x1"], (d_left, d_right), 3)
    grad_dt_w = t_dot(kept["x1"], d_dt_b)
    ranked = jnp.concatenate(
        [grad_heads.reshape(-1), grad_conv.reshape(-1), grad_ssm_gain, grad_dt_w.reshape(-1)]
    )
    gains = jnp.concatenate([grad_gain0[0], grad_gain1[0]])
    return entering_grad, shards, ranked, gains


def body(
    inputs, cotangent, norm_gains, head_params, conv_params, ssm_gain,
    w_in, w_out, w_qkv, w_o, w_gu, w_down,
):
    s, y = lax.axis_index("section"), lax.axis_index("y")
    core = lax.axis_index("core")
    nz = lax.axis_size("fsdp")
    z_place = lax.axis_index("fsdp")
    rank = 2 * s + y
    rows = inputs.shape[2]
    length = RANKS * rows
    w_in, w_out, w_qkv, w_o, w_gu, w_down = (
        w[0] for w in (w_in, w_out, w_qkv, w_o, w_gu, w_down)
    )

    flat = jnp.concatenate(
        [
            norm_gains[0].reshape(-1),
            head_params[0].reshape(-1),
            conv_params[0].reshape(-1),
            ssm_gain[0],
            w_in[:, D_SSM + CONV_W :].reshape(-1),
        ]
    )
    everything = lax.all_gather(flat, ("section", "fsdp"), axis=0).reshape(2, nz, -1)

    def unpack(layer):
        part = everything[layer]
        sizes = [2 * D // nz, 3 * SSM_HEADS // nz, 5 * CONV_W // nz, D_SSM // nz]
        starts = [0]
        for size in sizes:
            starts.append(starts[-1] + size)
        join = lambda k, lead: jnp.transpose(
            part[:, starts[k] : starts[k + 1]].reshape(nz, lead, -1), (1, 0, 2)
        ).reshape(lead, -1).astype(F32)
        gains, heads, conv, gain = join(0, 2), join(1, 3), join(2, 5), join(3, 1)[0]
        conv_own = jnp.concatenate(
            [columns(conv, R_SSM * rank, R_SSM), columns(conv, D_SSM + R_BC * rank, R_BC)], axis=1
        )
        channel = jnp.arange(R_OUT) % (R_OUT // nz)
        small = dict(
            gain0=gains[0],
            gain1=gains[1],
            heads=columns(heads, R_HEADS * rank, R_HEADS),
            conv=conv_own,
            ssm_gain=lax.dynamic_slice_in_dim(gain, R_SSM * rank, R_SSM),
            is_ssm=channel < R_SSM // nz,
        )
        return small, part[:, starts[4] :].reshape(D, SSM_HEADS)

    def pieces(section):
        rk = 2 * section + y
        first = columns(w_in, jnp.where(core == 0, D_SSM, 0) + R_SSM * rk, R_SSM)
        second = jnp.where(
            core == 0,
            columns(w_in, 2 * D_SSM + R_BC * rk, R_BC),
            columns(w_qkv, R_ATT * rk, HEAD_DIM),
        )
        third = columns(
            w_qkv,
            jnp.where(core == 0, ATT + KV * y + HEAD_DIM * section, R_ATT * rk + HEAD_DIM),
            HEAD_DIM,
        )
        side = HALF * core
        out_rows, o_rows, down_rows = R_SSM // nz, R_ATT // nz, R_FF // nz
        ff = R_FF // nz
        return {
            "in": jnp.concatenate([first, second, third], axis=1),
            "out": jnp.concatenate(
                [
                    lax.dynamic_slice(w_out, (out_rows * rk, side), (out_rows, HALF)),
                    lax.dynamic_slice(w_o, (o_rows * rk, side), (o_rows, HALF)),
                ],
                axis=0,
            ),
            "gu": jnp.concatenate(
                [
                    columns(w_gu, FF * core + (FF // nz) * k + ff * rk, ff) for k in range(nz)
                ],
                axis=1,
            ),
            "down": lax.dynamic_slice(w_down, (down_rows * rk, side), (down_rows, HALF)),
        }

    names = ("in", "out", "gu", "down")
    own, other = pieces(s), pieces(1 - s)
    arrived = {name: flip(other[name], "section") for name in names}

    def gathered(layer):
        result = {}
        for name in names:
            piece = jnp.where(s == layer, own[name], arrived[name])
            whole = lax.all_gather(piece, ("core", "fsdp"), axis=0)
            result[name] = whole.reshape(2, nz * piece.shape[0], HALF)
        return result

    def whole_sequence(own_rows):
        place = 2 * y + core
        result = jnp.zeros((RANKS, rows, D), BF)
        result = lax.dynamic_update_index_in_dim(
            result, lax.dynamic_index_in_dim(own_rows, core, 0, False), place, 0
        )
        for dy, dc in ((0, 1), (1, 0), (1, 1)):
            sent = lax.dynamic_index_in_dim(own_rows, core ^ dc, 0, False)
            pairs = [
                (2 * a + b, 2 * (a ^ dy) + (b ^ dc)) for a in range(2) for b in range(2)
            ]
            here = lax.ppermute(sent, ("y", "core"), pairs)
            result = lax.dynamic_update_index_in_dim(
                result, here, 2 * (y ^ dy) + (core ^ dc), 0
            )
        return result.reshape(length, D)

    def rank_rows(whole):
        return cut_rows(whole, rows * rank, rows)

    smalls = []
    weights = []
    for layer in range(2):
        small, dt_w = unpack(layer)
        smalls.append(small)
        weights.append(dict(gathered(layer), dt=dt_w))
    hidden = whole_sequence(inputs[:, 0])
    grad = whole_sequence(cotangent[:, 0])
    outs, kept = [], []
    for layer in range(2):
        hidden, keep = layer_forward(
            hidden, rank_rows(hidden), weights[layer], smalls[layer], layer == 0
        )
        outs.append(hidden)
        kept.append(keep)
    grads = [None, None]
    shards, ranked, gains = [None, None], [None, None], [None, None]
    for layer in (1, 0):
        grad, shards[layer], ranked[layer], gains[layer] = layer_backward(
            grad, rank_rows(grad).astype(F32), kept[layer], weights[layer], smalls[layer]
        )
        grads[layer] = grad

    def block_rows(pair):
        chosen = jnp.where(s == 0, pair[0], pair[1]).reshape(RANKS, rows, D)
        mine = lax.dynamic_index_in_dim(chosen, 2 * y + core, 0, False)
        sent = lax.dynamic_index_in_dim(chosen, 2 * y + (1 - core), 0, False)
        theirs = flip(sent, "core")
        both = jnp.where(core == 0, jnp.stack([mine, theirs]), jnp.stack([theirs, mine]))
        return both[None, :, None]

    def assembled(name):
        parts = []
        for layer in (1, 0):
            blocks = shards[layer][name]
            parts.append(lax.psum_scatter(blocks, "fsdp", scatter_dimension=0, tiled=True))
        one, zero = parts
        mine = jnp.where(s == 0, zero, one)
        sent = jnp.where(s == 0, one, zero)
        theirs = flip(sent, "section")
        both = jnp.where(s == 0, jnp.stack([mine, theirs]), jnp.stack([theirs, mine]))
        whole = lax.all_gather(both, ("y", "core"), axis=0)
        return whole.reshape(2, 2, 2, blocks.shape[0] // nz, HALF)

    ranks = [(a, b) for a in range(2) for b in range(2)]

    def by_rank(whole, rk, side):
        return whole[rk[1], side, rk[0]]

    got_down = assembled("down")
    got_gu = assembled("gu")
    got_out = assembled("out")
    got_in = assembled("in")

    out_rows, o_rows = R_SSM // nz, R_ATT // nz
    rows_of = lambda whole, lo, hi: jnp.concatenate(
        [
            jnp.concatenate([by_rank(whole, rk, side)[lo:hi] for side in range(2)], axis=1)
            for rk in ranks
        ],
        axis=0,
    ).astype(F32)
    grad_w_down = rows_of(got_down, 0, R_FF // nz)
    grad_w_out = rows_of(got_out, 0, out_rows)
    grad_w_o = rows_of(got_out, out_rows, out_rows + o_rows)
    ff = R_FF // nz
    grad_w_gu = jnp.concatenate(
        [
            by_rank(got_gu, rk, side)[:, ff * k : ff * (k + 1)]
            for side in range(2)
            for k in range(nz)
            for rk in ranks
        ],
        axis=1,
    ).astype(F32)

    vector = jnp.concatenate([ranked[0], ranked[1], gains[0], gains[1]])
    count = vector.shape[0]
    padded = jnp.pad(vector, (0, -count % 1024)).reshape(-1, 128)
    summed = lax.psum(padded, ("core", "fsdp"))
    all_ranks = lax.all_gather(summed, ("section", "y"), axis=0).reshape(RANKS, -1)
    per = ranked[0].shape[0]
    mine = jnp.where(s == 0, all_ranks[:, :per], all_ranks[:, per : 2 * per])
    gain_all = jnp.sum(all_ranks[:, 2 * per : 2 * per + 4 * D], axis=0).reshape(2, 2, D)
    gain_mine = jnp.where(s == 0, gain_all[0], gain_all[1])
    a0 = 3 * R_HEADS
    a1 = a0 + 5 * R_CONV
    a2 = a1 + R_SSM
    head_all = jnp.concatenate([mine[k, :a0].reshape(3, R_HEADS) for k in range(RANKS)], axis=1)
    convs = [mine[k, a0:a1].reshape(5, R_CONV) for k in range(RANKS)]
    conv_all = jnp.concatenate(
        [c[:, :R_SSM] for c in convs] + [c[:, R_SSM:] for c in convs], axis=1
    )
    ssm_all = mine[:, a1:a2].reshape(-1)
    dt_all = jnp.concatenate([mine[k, a2:].reshape(D, R_HEADS) for k in range(RANKS)], axis=1)

    def shard(array, axis):
        width = array.shape[axis] // nz
        return lax.dynamic_slice_in_dim(array, width * z_place, width, axis)

    grad_w_in = jnp.concatenate(
        [by_rank(got_in, rk, 1)[:, :R_SSM].astype(F32) for rk in ranks]
        + [by_rank(got_in, rk, 0)[:, :R_SSM].astype(F32) for rk in ranks]
        + [by_rank(got_in, rk, 0)[:, R_SSM:R_CONV].astype(F32) for rk in ranks]
        + [shard(dt_all, 0)],
        axis=1,
    )
    grad_w_qkv = jnp.concatenate(
        [by_rank(got_in, rk, 1)[:, R_SSM:] for rk in ranks]
        + [by_rank(got_in, (head, part), 0)[:, R_CONV:] for part in range(2) for head in range(2)],
        axis=1,
    ).astype(F32)
    return (
        block_rows(outs),
        block_rows(grads),
        shard(gain_mine, 1)[None],
        shard(head_all, 1)[None],
        shard(conv_all, 1)[None],
        shard(ssm_all, 0)[None],
        grad_w_in[None],
        grad_w_out[None],
        grad_w_qkv[None],
        grad_w_o[None],
        grad_w_gu[None],
        grad_w_down[None],
    )


def solution(mesh):
    sections, ctx, fsdp = mesh.devices.shape
    fine = Mesh(
        mesh.devices.reshape(sections, ctx // 2, 2, fsdp), ("section", "y", "core", "fsdp")
    )
    tokens = ("y", "core")
    in_specs = (
        P(None, "fsdp", tokens, None),
        P(None, "fsdp", tokens, None),
        P("section", None, "fsdp"),
        P("section", None, "fsdp"),
        P("section", None, "fsdp"),
        P("section", "fsdp"),
    ) + (P("section", "fsdp", None),) * 6
    out_specs = (
        P("section", None, "fsdp", tokens, None),
        P("section", None, "fsdp", tokens, None),
        P("section", None, "fsdp"),
        P("section", None, "fsdp"),
        P("section", None, "fsdp"),
        P("section", "fsdp"),
    ) + (P("section", "fsdp", None),) * 6
    return jax.shard_map(body, mesh=fine, in_specs=in_specs, out_specs=out_specs, check_vma=False)
```

time: 5030 us -> 1670 us (0.33)
  waiting for transfers between devices: 3780 us -> 829 us
  matrix products: 523 us -> 167 us
  Pallas kernels: 0 us -> 292 us
  blocking collectives: 161 us -> 0 us
  other arithmetic: 239 us -> 128 us
  local copies, waits for them, and re-layouts: 273 us -> 197 us
    all_gather x12 -> x13, waiting for transfers between devices: 1680 us -> 285 us  [the longest x8 193 us: gathered(): whole = lax.all_gather(piece, ('core', 'fsdp'), axis=0)]
    reduce_scatter x7 -> x8, waiting for transfers between devices: 1070 us -> 304 us  [assembled(): lax.psum_scatter(blocks, 'fsdp', scatter_dimension=0, tiled=True)]
    unnamed x26 -> x24, waiting for transfers between devices: 581 us -> 5.77 us
    dot_general x104 -> x72, matrix products: 523 us -> 164 us  [the longest x20 45.6 us: dot(): return jnp.dot(left, right, preferred_element_type=F32)]
    psum x1, waiting for transfers between devices: 416 us -> 70.1 us  [body(): summed = lax.psum(padded, ('core', 'fsdp'))]
    pallas_call x0 -> x16, Pallas kernels: none -> 292 us  [the longest x8 218 us: rank_call(): pl.pallas_call(kernel, out_shape=out_shape, in_specs=[VMEM_SPEC] * len(ar...]
    all_gather x13 -> x0, blocking collectives: 139 us -> none  [the longest x1 37.2 us: body(): lax.all_gather(norm_gains[0], 'fsdp', axis=1, tiled=True)]
    ppermute x10 -> x32, waiting for transfers between devices: 28 us -> 164 us  [the longest x26 152 us: flip(): return lax.ppermute(value, axis, [(0, 1), (1, 0)])]
  transfers between devices with their start and end apart: 33 -> 55, of which waited for: 22 -> 37; matrix products, arithmetic and copies ran while one was open for 9% -> 18% of each run, Pallas kernels for 0% -> 10%
where the time goes in v1:
time: 1670 us; the launch traced here: 1660 us
  waiting for transfers between devices  829 us (50%)
  Pallas kernels  292 us (17%)
  local copies, waits for them, and re-layouts  197 us (12%)
  matrix products  167 us (10%)
  other arithmetic  128 us (8%)
  starting transfers between devices  25.1 us (2%)
  between operations  20.6 us (1%)
    reduce_scatter x8, waiting for transfers between devices, assembled(): lax.psum_scatter(blocks, 'fsdp', scatter_dimension=0, tiled=True)  304 us
    pallas_call x8, Pallas kernels, rank_call(): pl.pallas_call(kernel, out_shape=out_shape, in_specs=[VMEM_SPEC] * len(ar...  218 us
    all_gather x8, waiting for transfers between devices, gathered(): whole = lax.all_gather(piece, ('core', 'fsdp'), axis=0)  193 us
    ppermute x26, waiting for transfers between devices, flip(): return lax.ppermute(value, axis, [(0, 1), (1, 0)])  152 us
    all_gather x4, waiting for transfers between devices, assembled(): whole = lax.all_gather(both, ('y', 'core'), axis=0)  91.8 us
    pallas_call x8, Pallas kernels, swap(): pl.pallas_call(functools.partial(swap_kernel, stat is not None), out_shap...  73.3 us
    psum x1, waiting for transfers between devices, body(): summed = lax.psum(padded, ('core', 'fsdp'))  70.1 us
    unnamed x496, local copies, waits for them, and re-layouts  54.6 us
  transfers between devices with their start and end apart: 55, of which 37 were waited for; matrix products, arithmetic and copies ran while one was open for 18% of the time, Pallas kernels for 10%

profile of v1, /device:TPU:0, one launch (start us, length us, event | category | flops | bytes accessed | tf_op | source)
XLA Modules:
  0.0 1657.3 jit_solution(11671839633549393531)
XLA Ops:
  50.9 20.6 %collective-permute-done.3 = bf16[512,1024]{1,0:T(8,128)(2,1)S(1)} collective-permute-done((bf16[512,1024]{1,0:T(8,128)(2,1)}, bf16[512,1024]{1,0:T(8,128)(2,1)S(1)}, u32[]{:S(2)}, u32[]{:S(2)}) %collective-permute-start.3) | collective-permute-done | bytes 1048608 | tf_op jit(solution)/shard_map/ppermute | solution.py:412
  76.2 21.3 %collective-permute-done.5 = bf16[512,1024]{1,0:T(8,128)(2,1)S(1)} collective-permute-done((bf16[512,1024]{1,0:T(8,128)(2,1)S(1)}, bf16[512,1024]{1,0:T(8,128)(2,1)S(1)}, u32[]{:S(2)}, u32[]{:S(2)}) %collective-permute-start.5) | collective-permute-done | bytes 1048608 | tf_op jit(solution)/shard_map/ppermute | solution.py:412
  177.2 79.1 %all-gather.33.cloned.1.call-done = bf16[4096,1024]{1,0:T(8,128)(2,1)} async-done(((bf16[512,1024]{1,0:T(8,128)(2,1)}), bf16[4096,1024]{1,0:T(8,128)(2,1)}) %all-gather.33.cloned.1.call-update) | async-done | bytes 8388624 | tf_op jit(solution)/shard_map/all_gather | solution.py:672
  302.8 26.4 %shard_map.213 = (f32[64,2048]{1,0:T(8,128)S(1)}, bf16[256,2048]{1,0:T(8,128)(2,1)S(1)}) custom-call(bf16[256,2048]{1,0:T(8,128)(2,1)S(1)} %pad_maximum_fusion.2.part_ref, bf16[64,2048]{1,0:T(8,128)(2,1)S(1)} %get-tuple-element.185.resid_ref, f32[1,2048]{1,0:T(1,128)S(1)} %bitcast.788), custom_call_target="tpu_custom_call" | custom-call | tf_op jit(solution)/shard_map/pallas_call | solution.py:214
  346.0 39.5 %all-gather.39.cloned.1.call-done = bf16[2048,1024]{1,0:T(8,128)(2,1)} async-done(((bf16[256,1024]{1,0:T(8,128)(2,1)}), bf16[2048,1024]{1,0:T(8,128)(2,1)}) %all-gather.39.cloned.1.call-update) | async-done | bytes 4194320 | tf_op jit(solution)/shard_map/all_gather | solution.py:672
  389.2 28.3 %shard_map.214 = bf16[256,2048]{1,0:T(8,128)(2,1)S(1)} custom-call(bf16[256,2048]{1,0:T(8,128)(2,1)S(1)} %pad_maximum_fusion.5.part_ref, f32[64,2048]{1,0:T(8,128)S(1)} %get-tuple-element.37.resid_ref.value_ref), custom_call_target="tpu_custom_call" | custom-call | tf_op jit(solution)/shard_map/pallas_call | solution.py:214
  419.2 49.3 %all-gather.41.cloned.1.call-done = bf16[4096,1024]{1,0:T(8,128)(2,1)} async-done(((bf16[512,1024]{1,0:T(8,128)(2,1)}), bf16[4096,1024]{1,0:T(8,128)(2,1)}) %all-gather.41.cloned.1.call-update) | async-done | bytes 8388624 | tf_op jit(solution)/shard_map/all_gather | solution.py:672
  536.1 26.4 %shard_map.217 = (f32[64,2048]{1,0:T(8,128)S(1)}, bf16[256,2048]{1,0:T(8,128)(2,1)S(1)}) custom-call(bf16[256,2048]{1,0:T(8,128)(2,1)S(1)} %pad_maximum_fusion.6.part_ref, bf16[64,2048]{1,0:T(8,128)(2,1)S(1)} %get-tuple-element.189.resid_ref, f32[1,2048]{1,0:T(1,128)S(1)} %bitcast.790), custom_call_target="tpu_custom_call" | custom-call | tf_op jit(solution)/shard_map/pallas_call | solution.py:214
  578.0 27.9 %shard_map.219 = (f32[64,2048]{1,0:T(8,128)S(1)}, bf16[256,2048]{1,0:T(8,128)(2,1)S(1)}, f32[1,2048]{1,0:T(1,128)S(1)}) custom-call(bf16[256,2048]{1,0:T(8,128)(2,1)S(1)} %fusion.60.part_ref, f32[64,2048]{1,0:T(8,128)S(1)} %dynamic-slice_convert_fusion.1.given_ref, f32[64,2048]{1,0:T(8,128)S(1)} %get-tuple-element.41.resid_ref.value_ref, f32[1,2048]{1,0:T(1,128)S(1)} %bitcast.791), custom_call_target="tpu_custom_call" | custom-call | tf_op jit(solution)/shard_map/pallas_call | solution.py:214
  684.8 27.9 %shard_map.222 = (f32[64,2048]{1,0:T(8,128)}, bf16[256,2048]{1,0:T(8,128)(2,1)S(1)}, f32[1,2048]{1,0:T(1,128)S(1)}) custom-call(bf16[256,2048]{1,0:T(8,128)(2,1)S(1)} %fusion.57.part_ref, f32[64,2048]{1,0:T(8,128)S(1)} %copy-done.15, f32[64,2048]{1,0:T(8,128)S(1)} %copy-done.1, f32[1,2048]{1,0:T(1,128)S(1)} %bitcast.793), custom_call_target="tpu_custom_call" | custom-call | tf_op jit(solution)/shard_map/pallas_call | solution.py:214
  719.7 27.8 %shard_map.223 = (f32[64,2048]{1,0:T(8,128)S(1)}, bf16[256,2048]{1,0:T(8,128)(2,1)S(1)}, f32[1,2048]{1,0:T(1,128)S(1)}) custom-call(bf16[256,2048]{1,0:T(8,128)(2,1)S(1)} %fusion.63.part_ref, f32[64,2048]{1,0:T(8,128)S(1)} %dynamic-slice_convert_fusion.given_ref, f32[64,2048]{1,0:T(8,128)S(1)} %get-tuple-element.37.resid_ref.value_ref, f32[1,2048]{1,0:T(1,128)S(1)} %bitcast.789), custom_call_target="tpu_custom_call" | custom-call | tf_op jit(solution)/shard_map/pallas_call | solution.py:214
  838.9 28.9 %shard_map.226 = (f32[64,2048]{1,0:T(8,128)}, bf16[256,2048]{1,0:T(8,128)(2,1)S(1)}, f32[1,2048]{1,0:T(1,128)S(1)}) custom-call(bf16[256,2048]{1,0:T(8,128)(2,1)S(1)} %fusion.54.part_ref, f32[64,2048]{1,0:T(8,128)S(1)} %copy-done.13, f32[64,2048]{1,0:T(8,128)S(1)} %copy-done, f32[1,2048]{1,0:T(1,128)S(1)} %bitcast.792), custom_call_target="tpu_custom_call" | custom-call | tf_op jit(solution)/shard_map/pallas_call | solution.py:214
  919.1 70.1 %all-reduce.17.cloned.1.call-done = f32[1,536,128]{2,1,0:T(8,128)} async-done(((f32[1,536,128]{2,1,0:T(8,128)}), f32[1,536,128]{2,1,0:T(8,128)}) %all-reduce.17.cloned.1.call-update) | async-done | bytes 274448 | tf_op jit(solution)/shard_map/psum | solution.py:775
  1025.5 34.2 %reduce-scatter.23.cloned.1.call-done = bf16[256,1024]{1,0:T(8,128)(2,1)} async-done(((bf16[1024,1024]{1,0:T(8,128)(2,1)}), bf16[256,1024]{1,0:T(8,128)(2,1)}) %reduce-scatter.23.cloned.1.call-update) | async-done | bytes 524304 | tf_op jit(solution)/shard_map/reduce_scatter | solution.py:731
  1075.7 62.9 %reduce-scatter.9.cloned.1.call-done = bf16[512,1024]{1,0:T(8,128)(2,1)} async-done(((bf16[2048,1024]{1,0:T(8,128)(2,1)}), bf16[512,1024]{1,0:T(8,128)(2,1)}) %reduce-scatter.9.cloned.1.call-update) | async-done | bytes 1048592 | tf_op jit(solution)/shard_map/reduce_scatter | solution.py:731
  1138.6 80.2 %reduce-scatter.11.cloned.1.call-done = bf16[512,1024]{1,0:T(8,128)(2,1)} async-done(((bf16[2048,1024]{1,0:T(8,128)(2,1)}), bf16[512,1024]{1,0:T(8,128)(2,1)}) %reduce-scatter.11.cloned.1.call-update) | async-done | bytes 1048592 | tf_op jit(solution)/shard_map/reduce_scatter | solution.py:731
  1222.0 31.0 %collective-permute-done.16 = bf16[512,1024]{1,0:T(8,128)(2,1)S(1)} collective-permute-done((bf16[512,1024]{1,0:T(8,128)(2,1)S(1)}, bf16[512,1024]{1,0:T(8,128)(2,1)S(1)}, u32[]{:S(2)}, u32[]{:S(2)}) %collective-permute-start.16) | collective-permute-done | bytes 1048608 | tf_op jit(solution)/shard_map/ppermute | solution.py:412
  1258.5 24.7 %shard_map.218 = bf16[256,2048]{1,0:T(8,128)(2,1)S(1)} custom-call(bf16[256,2048]{1,0:T(8,128)(2,1)S(1)} %pad_maximum_fusion.7.part_ref, f32[64,2048]{1,0:T(8,128)S(1)} %get-tuple-element.41.resid_ref.value_ref), custom_call_target="tpu_custom_call" | custom-call | tf_op jit(solution)/shard_map/pallas_call | solution.py:214
  1288.3 46.5 %reduce-scatter.17.cloned.1.call-done = bf16[512,1024]{1,0:T(8,128)(2,1)} async-done(((bf16[2048,1024]{1,0:T(8,128)(2,1)}), bf16[512,1024]{1,0:T(8,128)(2,1)}) %reduce-scatter.17.cloned.1.call-update) | async-done | bytes 1048592 | tf_op jit(solution)/shard_map/reduce_scatter | solution.py:731
  1334.8 80.1 %reduce-scatter.19.cloned.1.call-done = bf16[512,1024]{1,0:T(8,128)(2,1)} async-done(((bf16[2048,1024]{1,0:T(8,128)(2,1)}), bf16[512,1024]{1,0:T(8,128)(2,1)}) %reduce-scatter.19.cloned.1.call-update) | async-done | bytes 1048592 | tf_op jit(solution)/shard_map/reduce_scatter | solution.py:731
  1421.0 21.8 %collective-permute-done.26 = bf16[512,1024]{1,0:T(8,128)(2,1)} collective-permute-done((bf16[512,1024]{1,0:T(8,128)(2,1)}, bf16[512,1024]{1,0:T(8,128)(2,1)}, u32[]{:S(2)}, u32[]{:S(2)}) %collective-permute-start.26) | collective-permute-done | bytes 1048608 | tf_op jit(solution)/shard_map/ppermute | solution.py:412
  1461.2 26.8 %all-gather.31.cloned.1.call-done = bf16[4,2,256,1024]{3,2,1,0:T(8,128)(2,1)} async-done(((bf16[1,2,256,1024]{3,2,1,0:T(8,128)(2,1)}), bf16[4,2,256,1024]{3,2,1,0:T(8,128)(2,1)}) %all-gather.31.cloned.1.call-update) | async-done | bytes 4194320 | tf_op jit(solution)/shard_map/all_gather | solution.py:737
  1501.3 47.2 %all-gather.25.cloned.1.call-done = bf16[4,2,512,1024]{3,2,1,0:T(8,128)(2,1)} async-done(((bf16[1,2,512,1024]{3,2,1,0:T(8,128)(2,1)}), bf16[4,2,512,1024]{3,2,1,0:T(8,128)(2,1)}) %all-gather.25.cloned.1.call-update) | async-done | bytes 8388624 | tf_op jit(solution)/shard_map/all_gather | solution.py:737
  1591.0 17.8 %all-gather.29.cloned.1.call-done = bf16[4,2,512,1024]{3,2,1,0:T(8,128)(2,1)} async-done(((bf16[1,2,512,1024]{3,2,1,0:T(8,128)(2,1)}), bf16[4,2,512,1024]{3,2,1,0:T(8,128)(2,1)}) %all-gather.29.cloned.1.call-update) | async-done | bytes 8388624 | tf_op jit(solution)/shard_map/all_gather | solution.py:737
  (1036 shorter events, 689.9 us)
Async XLA Ops:
  8.1 125.6 %all-reduce.19.cloned.1.call-start = ((), (), s32[]{:S(2)}) async-start(), calls=%async_computation.30 | async-start | bytes 991232
  17.5 130.9 %all-gather.35.cloned.1.call-start = ((), (), s32[]{:S(2)}) async-start(), calls=%async_computation.23 | async-start | bytes 4718592 | tf_op jit(solution)/shard_map/all_gather | solution.py:672
  27.4 125.7 %all-gather.43.cloned.1.call-start = ((), (), s32[]{:S(2)}) async-start(), calls=%async_computation.27 | async-start | bytes 4718592 | tf_op jit(solution)/shard_map/all_gather | solution.py:672
  28.0 146.0 %all-gather.47.cloned.1.call-start = ((), (), s32[]{:S(2)}) async-start(), calls=%async_computation.29 | async-start | bytes 4718592 | tf_op jit(solution)/shard_map/all_gather | solution.py:672
  43.7 212.6 %all-gather.33.cloned.1.call-start = ((), (), s32[]{:S(2)}) async-start(), calls=%async_computation.22 | async-start | bytes 9437184 | tf_op jit(solution)/shard_map/all_gather | solution.py:672
  73.4 265.2 %all-gather.37.cloned.1.call-start = ((), (), s32[]{:S(2)}) async-start(), calls=%async_computation.24 | async-start | bytes 9437184 | tf_op jit(solution)/shard_map/all_gather | solution.py:672
  99.3 286.2 %all-gather.39.cloned.1.call-start = ((), (), s32[]{:S(2)}) async-start(), calls=%async_computation.25 | async-start | bytes 4718592 | tf_op jit(solution)/shard_map/all_gather | solution.py:672
  100.1 368.4 %all-gather.41.cloned.1.call-start = ((), (), s32[]{:S(2)}) async-start(), calls=%async_computation.26 | async-start | bytes 9437184 | tf_op jit(solution)/shard_map/all_gather | solution.py:672
  106.6 458.0 %all-gather.45.cloned.1.call-start = ((), (), s32[]{:S(2)}) async-start(), calls=%async_computation.28 | async-start | bytes 9437184 | tf_op jit(solution)/shard_map/all_gather | solution.py:672
  148.1 841.1 %all-reduce.17.cloned.1.call-start = ((), (), s32[]{:S(2)}) async-start(), calls=%async_computation.8 | async-start | bytes 548864 | tf_op jit(solution)/shard_map/psum | solution.py:775
  828.6 45.3 %collective-permute-start.18 = (bf16[256,1024]{1,0:T(8,128)(2,1)}, bf16[256,1024]{1,0:T(8,128)(2,1)}, u32[]{:S(2)}, u32[]{:S(2)}) collective-permute-start(bf16[256,1024]{1,0:T(8,128)(2,1)} %get-tuple-element.285), channel_id=1, source_target_pairs={{0,4},{4,0},{1,5},{5,1},{2,6},{6,2},{3,7},{7,3},{8,12},{12,8},{9,1... | collective-permute-start | bytes 1572872 | tf_op jit(solution)/shard_map/ppermute | solution.py:412
  873.6 135.3 %reduce-scatter.13.cloned.1.call-start = ((), (), s32[]{:S(2)}) async-start(), calls=%async_computation.13 | async-start | bytes 2621440 | tf_op jit(solution)/shard_map/reduce_scatter | solution.py:731
  878.0 130.9 %reduce-scatter.15.cloned.1.call-start = ((), (), s32[]{:S(2)}) async-start(), calls=%async_computation.14 | async-start | bytes 2621440 | tf_op jit(solution)/shard_map/reduce_scatter | solution.py:731
  885.3 140.2 %reduce-scatter.21.cloned.1.call-start = ((), (), s32[]{:S(2)}) async-start(), calls=%async_computation.19 | async-start | bytes 2621440 | tf_op jit(solution)/shard_map/reduce_scatter | solution.py:731
  891.9 167.8 %reduce-scatter.23.cloned.1.call-start = ((), (), s32[]{:S(2)}) async-start(), calls=%async_computation.20 | async-start | bytes 2621440 | tf_op jit(solution)/shard_map/reduce_scatter | solution.py:731
  900.0 238.6 %reduce-scatter.9.cloned.1.call-start = ((), (), s32[]{:S(2)}) async-start(), calls=%async_computation.10 | async-start | bytes 5242880 | tf_op jit(solution)/shard_map/reduce_scatter | solution.py:731
  909.2 309.6 %reduce-scatter.11.cloned.1.call-start = ((), (), s32[]{:S(2)}) async-start(), calls=%async_computation.11 | async-start | bytes 5242880 | tf_op jit(solution)/shard_map/reduce_scatter | solution.py:731
  919.1 367.6 %all-gather.23.cloned.1.call-start = ((), (), s32[]{:S(2)}) async-start(), calls=%async_computation.9 | async-start | bytes 1372160 | tf_op jit(solution)/shard_map/all_gather | solution.py:776
  989.2 345.6 %reduce-scatter.17.cloned.1.call-start = ((), (), s32[]{:S(2)}) async-start(), calls=%async_computation.16 | async-start | bytes 5242880 | tf_op jit(solution)/shard_map/reduce_scatter | solution.py:731
  999.0 415.9 %reduce-scatter.19.cloned.1.call-start = ((), (), s32[]{:S(2)}) async-start(), calls=%async_computation.17 | async-start | bytes 5242880 | tf_op jit(solution)/shard_map/reduce_scatter | solution.py:731
  1008.9 448.1 %all-gather.27.cloned.1.call-start = ((), (), s32[]{:S(2)}) async-start(), calls=%async_computation.15 | async-start | bytes 5242880 | tf_op jit(solution)/shard_map/all_gather | solution.py:737
  1025.4 462.6 %all-gather.31.cloned.1.call-start = ((), (), s32[]{:S(2)}) async-start(), calls=%async_computation.21 | async-start | bytes 5242880 | tf_op jit(solution)/shard_map/all_gather | solution.py:737
  1075.6 472.8 %all-gather.25.cloned.1.call-start = ((), (), s32[]{:S(2)}) async-start(), calls=%async_computation.12 | async-start | bytes 10485760 | tf_op jit(solution)/shard_map/all_gather | solution.py:737
  1254.6 354.2 %all-gather.29.cloned.1.call-start = ((), (), s32[]{:S(2)}) async-start(), calls=%async_computation.18 | async-start | bytes 10485760 | tf_op jit(solution)/shard_map/all_gather | solution.py:737
  (247 other events, 2523.3 us)
Sparse Core Ops, SparseCore 0:
  17.6 115.9 all-reduce.18
  878.2 43.3 reduce-scatter.12
  924.4 44.5 reduce-scatter.14
  971.2 43.0 reduce-scatter.20
  1016.5 43.1 reduce-scatter.22
  1062.5 76.0 reduce-scatter.8
  1141.5 77.2 reduce-scatter.10
  1220.6 33.9 all-gather.22
  1257.5 77.2 reduce-scatter.16
  1337.6 77.2 reduce-scatter.18
  1417.0 34.9 all-gather.26
  1453.5 34.4 all-gather.30
  1490.1 58.2 all-gather.24
  1550.5 58.2 all-gather.28
Sparse Core Ops, SparseCore 1:
  27.5 50.3 all-gather.34
  79.9 47.1 all-gather.42
  128.7 45.2 all-gather.46
  175.7 80.7 all-gather.32
  258.1 80.4 all-gather.36
  340.2 45.3 all-gather.38
  387.7 80.7 all-gather.40
  470.0 80.4 all-gather.44
  873.7 115.5 all-reduce.16

commit v2 on v1

--- a/solution.py
+++ b/solution.py
@@ -101,10 +101,29 @@
         copy.wait()
 
 
+CHANNELS = {}
+
+
+def channel(name, *operands):
+    key = (name,) + tuple((o.shape, str(o.dtype)) for o in operands)
+    return CHANNELS.setdefault(key, len(CHANNELS))
+
+
+def lasting(us):
+    return pl.CostEstimate(flops=0, transcendentals=0, bytes_accessed=int(us * 850000))
+
+
 VMEM_SPEC = pl.BlockSpec(memory_space=pltpu.VMEM)
-
-
-def swap(values, collective_id, stat=None):
+ANY_SPEC = pl.BlockSpec(memory_space=pl.ANY)
+
+
+def ignoring(kernel, used, extra):
+    if not extra:
+        return kernel
+    return lambda *refs: kernel(*refs[:used], *refs[used + extra :])
+
+
+def swap(values, stat=None, after=()):
     out_shape = [jax.ShapeDtypeStruct((RANKS,) + values.shape[-2:], values.dtype)]
     scratch = [pltpu.SemaphoreType.DMA((RANKS - 1,)), pltpu.SemaphoreType.DMA((RANKS - 1,))]
     args = [values]
@@ -113,15 +132,18 @@
         scratch += scratch
         args.append(stat)
     out = pl.pallas_call(
-        functools.partial(swap_kernel, stat is not None),
+        ignoring(functools.partial(swap_kernel, stat is not None), len(args), len(after)),
         out_shape=out_shape,
-        in_specs=[VMEM_SPEC] * len(args),
+        in_specs=[VMEM_SPEC] * len(args) + [pl.BlockSpec(memory_space=pl.ANY)] * len(after),
         out_specs=[VMEM_SPEC] * len(out_shape),
         scratch_shapes=scratch,
+        cost_estimate=lasting(9),
         compiler_params=pltpu.CompilerParams(
-            collective_id=collective_id, has_side_effects=True, vmem_limit_bytes=32 * 2**20
+            collective_id=channel("swap", *args, *after),
+            has_side_effects=True,
+            vmem_limit_bytes=32 * 2**20,
         ),
-    )(*args)
+    )(*args, *after)
     return out if stat is not None else out[0]
 
 
@@ -210,18 +232,21 @@
     spread(me, rows, out_ref, s2, r2)
 
 
-def rank_call(kernel, out_shape, collective_id, rows, *args):
+def rank_call(kernel, out_shape, rows, *args, after=()):
     return pl.pallas_call(
-        kernel,
+        ignoring(kernel, len(args), len(after)),
         out_shape=out_shape,
-        in_specs=[VMEM_SPEC] * len(args),
+        in_specs=[VMEM_SPEC] * len(args) + [pl.BlockSpec(memory_space=pl.ANY)] * len(after),
         out_specs=[VMEM_SPEC] * len(out_shape),
         scratch_shapes=[pltpu.VMEM((RANKS - 1, rows, D), BF)]
         + [pltpu.SemaphoreType.DMA((RANKS - 1,))] * 4,
+        cost_estimate=lasting(27),
         compiler_params=pltpu.CompilerParams(
-            collective_id=collective_id, has_side_effects=True, vmem_limit_bytes=32 * 2**20
+            collective_id=channel(kernel.__name__, *args, *after),
+            has_side_effects=True,
+            vmem_limit_bytes=32 * 2**20,
         ),
-    )(*args)
+    )(*args, *after)
 
 
 def mid_step(part, resid, gain):
@@ -229,7 +254,6 @@
     return rank_call(
         mid_kernel,
         [jax.ShapeDtypeStruct((rows, D), F32), jax.ShapeDtypeStruct(part.shape, BF)],
-        3,
         rows,
         part,
         resid,
@@ -239,10 +263,10 @@
 
 def end_step(part, resid):
     rows = resid.shape[0]
-    return rank_call(end_kernel, [jax.ShapeDtypeStruct(part.shape, BF)], 4, rows, part, resid)[0]
-
-
-def back_step(part, given, value, gain):
+    return rank_call(end_kernel, [jax.ShapeDtypeStruct(part.shape, BF)], rows, part, resid)[0]
+
+
+def back_step(part, given, value, gain, after=()):
     rows = given.shape[0]
     return rank_call(
         back_kernel,
@@ -251,13 +275,238 @@
             jax.ShapeDtypeStruct(part.shape, BF),
             jax.ShapeDtypeStruct((1, D), F32),
         ],
-        5,
         rows,
         part,
         given,
         value,
         gain[None],
-    )
+        after=after,
+    )
+
+
+def copy_kernel(value_ref, out_ref):
+    out_ref[...] = value_ref[...]
+
+
+def copy_after(value, *tokens):
+    rows, width = value.shape
+    tile = min(rows, 128)
+    block = pl.BlockSpec((tile, width), lambda i: (i, 0))
+    return pl.pallas_call(
+        ignoring(copy_kernel, 1, len(tokens)),
+        grid=(rows // tile,),
+        out_shape=jax.ShapeDtypeStruct(value.shape, value.dtype),
+        in_specs=[block] + [ANY_SPEC] * len(tokens),
+        out_specs=block,
+    )(value, *tokens)
+
+
+def product_kernel(left_a, left_b, right_a, right_b, out_ref):
+    turned = lambda left, right: lax.dot_general(
+        left[...], right[...], (((0,), (0,)), ((), ())), preferred_element_type=F32
+    )
+    out_ref[...] = (turned(left_a, right_a) + turned(left_b, right_b)).astype(BF)
+
+
+def outer_sum(left, right, tokens):
+    rows, width = left[0].shape
+    columns_right = right[0].shape[1]
+    tile = 256
+    left_block = pl.BlockSpec((rows, tile), lambda i: (0, i))
+    right_block = pl.BlockSpec((rows, columns_right), lambda i: (0, 0))
+    return pl.pallas_call(
+        ignoring(product_kernel, 4, len(tokens)),
+        grid=(width // tile,),
+        out_shape=jax.ShapeDtypeStruct((width, columns_right), BF),
+        in_specs=[left_block] * 2 + [right_block] * 2 + [ANY_SPEC] * len(tokens),
+        out_specs=pl.BlockSpec((tile, columns_right), lambda i: (i, 0)),
+        cost_estimate=lasting(3),
+    )(*left, *right, *tokens)
+
+
+def share_kernel(one_ref, zero_ref, *refs):
+    own, own_c, across, across_c, local_sem, send_sem, recv_sem = refs[-7:]
+    s, y, core = (lax.axis_index(name) for name in ("section", "y", "core"))
+    rows = one_ref.shape[0]
+    half = rows // 2
+    barrier = pltpu.get_barrier_semaphore()
+    ids = {"section": {"section": 1 - s}, "y": {"y": 1 - y}, "core": {"core": 1 - core}}
+    for who in ids.values():
+        pl.semaphore_signal(barrier, inc=1, device_id=who, device_id_type=MESH)
+    pl.semaphore_wait(barrier, 3)
+
+    def remote(k, src, dst, axis):
+        return pltpu.make_async_remote_copy(
+            src_ref=src, dst_ref=dst, send_sem=send_sem.at[k], recv_sem=recv_sem.at[k],
+            device_id=ids[axis], device_id_type=MESH,
+        )
+
+    part = lambda ref, k: ref.at[pl.ds(half * k, half)]
+    slot = lambda ref, place, k: ref.at[place, pl.ds(half * k, half)]
+    for section, mine, sent in ((0, zero_ref, one_ref), (1, one_ref, zero_ref)):
+
+        @pl.when(s == section)
+        def _():
+            for k in range(2):
+                remote(k, part(sent, k), slot(own, section, k), "section").start()
+            for k in range(2):
+                remote(2 + k, part(mine, k), slot(across, section, k), "y").start()
+            remote(6, mine, own_c.at[section], "core").start()
+            keep = pltpu.make_async_copy(mine, own.at[section], local_sem)
+            keep.start()
+            for k in range(2):
+                remote(k, part(sent, k), slot(own, 1 - section, k), "section").wait_recv()
+                remote(4 + k, slot(own, 1 - section, k), slot(across, 1 - section, k), "y").start()
+                remote(
+                    7 + k, slot(own, 1 - section, k), slot(own_c, 1 - section, k), "core"
+                ).start()
+            for k in range(2):
+                remote(2 + k, part(mine, k), slot(across, section, k), "y").wait_recv()
+                remote(
+                    9 + k, slot(across, section, k), slot(across_c, section, k), "core"
+                ).start()
+            for k in range(2):
+                there = slot(across, 1 - section, k)
+                remote(4 + k, slot(own, 1 - section, k), there, "y").wait_recv()
+                remote(11 + k, there, slot(across_c, 1 - section, k), "core").start()
+            remote(6, mine, own_c.at[section], "core").wait_recv()
+            for k in range(2):
+                there = slot(own_c, 1 - section, k)
+                remote(7 + k, slot(own, 1 - section, k), there, "core").wait_recv()
+                there = slot(across_c, section, k)
+                remote(9 + k, slot(across, section, k), there, "core").wait_recv()
+                there = slot(across_c, 1 - section, k)
+                remote(11 + k, slot(across, 1 - section, k), there, "core").wait_recv()
+            for k in range(2):
+                remote(k, part(sent, k), slot(own, section, k), "section").wait_send()
+                remote(2 + k, part(mine, k), slot(across, section, k), "y").wait_send()
+                there = slot(across, 1 - section, k)
+                remote(4 + k, slot(own, 1 - section, k), there, "y").wait_send()
+                there = slot(own_c, 1 - section, k)
+                remote(7 + k, slot(own, 1 - section, k), there, "core").wait_send()
+                there = slot(across_c, section, k)
+                remote(9 + k, slot(across, section, k), there, "core").wait_send()
+                there = slot(across_c, 1 - section, k)
+                remote(11 + k, slot(across, 1 - section, k), there, "core").wait_send()
+            remote(6, mine, own_c.at[section], "core").wait_send()
+            keep.wait()
+
+
+def share(one, zero, us, after=()):
+    shape = jax.ShapeDtypeStruct((2,) + one.shape, one.dtype)
+    return pl.pallas_call(
+        ignoring(share_kernel, 2, len(after)),
+        out_shape=[shape] * 4,
+        in_specs=[ANY_SPEC] * (2 + len(after)),
+        out_specs=[ANY_SPEC] * 4,
+        scratch_shapes=[
+            pltpu.SemaphoreType.DMA,
+            pltpu.SemaphoreType.DMA((13,)),
+            pltpu.SemaphoreType.DMA((13,)),
+        ],
+        cost_estimate=lasting(us),
+        compiler_params=pltpu.CompilerParams(
+            collective_id=channel("share", one, zero, *after), has_side_effects=True
+        ),
+    )(one, zero, *after)
+
+
+def chosen(place_ref, refs):
+    y, core = place_ref[0], place_ref[1]
+    values = [ref[...] for ref in refs]
+    found = [[None, None], [None, None]]
+    for side in range(2):
+        flat = [jnp.where(core == side, values[2 * k], values[2 * k + 1]) for k in range(2)]
+        for row in range(2):
+            found[row][side] = jnp.where(y == row, flat[0], flat[1])
+    return found
+
+
+def rows_kernel(place_ref, a, b, c, d, out_ref):
+    found = chosen(place_ref, (a, b, c, d))
+    row = lax.rem(pl.program_id(0), 2)
+    for side in range(2):
+        value = jnp.where(row == 0, found[0][side][0], found[1][side][0])
+        out_ref[:, HALF * side : HALF * (side + 1)] = value.astype(F32)
+
+
+PLACE_SPEC = pl.BlockSpec(memory_space=pltpu.SMEM)
+
+
+def spread_rows(place, pieces, first, count, tile):
+    steps = count // tile
+    block = pl.BlockSpec((1, tile, HALF), lambda r, i: (r // 2, first // tile + i, 0))
+    return pl.pallas_call(
+        rows_kernel,
+        grid=(RANKS, steps),
+        out_shape=jax.ShapeDtypeStruct((RANKS * count, D), F32),
+        in_specs=[PLACE_SPEC] + [block] * 4,
+        out_specs=pl.BlockSpec((tile, D), lambda r, i: (r * steps + i, 0)),
+        compiler_params=pltpu.CompilerParams(vmem_limit_bytes=32 * 2**20),
+    )(place, *pieces)
+
+
+def gate_up_kernel(nz, place_ref, a, b, c, d, out_ref):
+    found = chosen(place_ref, (a, b, c, d))
+    width = R_FF // nz
+    for side in range(2):
+        for shard in range(nz):
+            for rank in range(RANKS):
+                start = FF * side + (FF // nz) * shard + width * rank
+                out_ref[:, start : start + width] = found[rank % 2][side][
+                    rank // 2, :, width * shard : width * (shard + 1)
+                ].astype(F32)
+
+
+def spread_gate_up(place, pieces, nz):
+    rows = pieces[0].shape[1]
+    tile = min(rows, 64)
+    block = pl.BlockSpec((2, tile, HALF), lambda i: (0, i, 0))
+    return pl.pallas_call(
+        functools.partial(gate_up_kernel, nz),
+        grid=(rows // tile,),
+        out_shape=jax.ShapeDtypeStruct((rows, 2 * FF), F32),
+        in_specs=[PLACE_SPEC] + [block] * 4,
+        out_specs=pl.BlockSpec((tile, 2 * FF), lambda i: (i, 0)),
+        compiler_params=pltpu.CompilerParams(vmem_limit_bytes=32 * 2**20),
+    )(place, *pieces)
+
+
+def in_kernel(place_ref, a, b, c, d, dt_ref, in_ref, qkv_ref):
+    found = chosen(place_ref, (a, b, c, d))
+    for rank in range(RANKS):
+        left, right = (found[rank % 2][side][rank // 2].astype(F32) for side in range(2))
+        in_ref[R_SSM * rank : R_SSM * (rank + 1)] = right[:, :R_SSM].T
+        start = D_SSM + R_SSM * rank
+        in_ref[start : start + R_SSM] = left[:, :R_SSM].T
+        start = 2 * D_SSM + R_BC * rank
+        in_ref[start : start + R_BC] = left[:, R_SSM:R_CONV].T
+        qkv_ref[:, R_ATT * rank : R_ATT * (rank + 1)] = right[:, R_SSM:]
+        start = ATT + KV * (rank % 2) + HEAD_DIM * (rank // 2)
+        qkv_ref[:, start : start + HEAD_DIM] = left[:, R_CONV:]
+    in_ref[D_SSM + CONV_W :] = dt_ref[...]
+
+
+def spread_in(place, pieces, dt):
+    rows = pieces[0].shape[1]
+    tile = min(rows, 128)
+    block = pl.BlockSpec((2, tile, HALF), lambda i: (0, i, 0))
+    return pl.pallas_call(
+        in_kernel,
+        grid=(rows // tile,),
+        out_shape=[
+            jax.ShapeDtypeStruct((D_IN, rows), F32),
+            jax.ShapeDtypeStruct((rows, ATT + 2 * KV), F32),
+        ],
+        in_specs=[PLACE_SPEC]
+        + [block] * 4
+        + [pl.BlockSpec((SSM_HEADS, tile), lambda i: (0, i))],
+        out_specs=[
+            pl.BlockSpec((D_IN, tile), lambda i: (0, i)),
+            pl.BlockSpec((tile, ATT + 2 * KV), lambda i: (i, 0)),
+        ],
+        compiler_params=pltpu.CompilerParams(vmem_limit_bytes=40 * 2**20),
+    )(place, *pieces, dt)
 
 
 def narrow(values):
@@ -423,7 +672,7 @@
     u = narrow(jax.nn.silu(conv_sum(xbc, small["conv"])))
     kv_raw = left[:, R_CONV:]
     kv = narrow(jnp.where(y == 0, rotary(kv_raw, 1.0), kv_raw))
-    shared = swap(jnp.concatenate([u[:, R_SSM:], kv], axis=1), 0)
+    shared = swap(jnp.concatenate([u[:, R_SSM:], kv], axis=1))
     b_rows = jnp.concatenate([shared[0, :, :R_BC], shared[1, :, :R_BC]], axis=1)
     c_rows = jnp.concatenate([shared[2, :, :R_BC], shared[3, :, :R_BC]], axis=1)
     pair = lax.dynamic_slice_in_dim(shared, 2 * s, 2, axis=0)[:, :, R_BC:]
@@ -438,7 +687,7 @@
     scaled = narrow(gated * small["ssm_gain"][None, :])
     message = to_rows(scaled, o)
     stat = jnp.broadcast_to(squares[None, :], (8, length))
-    got, stats = swap(message, 1, stat)
+    got, stats = swap(message, stat)
     spread_of = lax.rsqrt(jnp.sum(stats[:, 0, :], axis=0) / D_SSM + EPSILON)
     wide = jnp.transpose(got, (1, 0, 2)).reshape(length, R_OUT)
     is_ssm = small["is_ssm"][None, :]
@@ -478,28 +727,44 @@
     return a, b
 
 
-def layer_backward(grad, given, kept, weights, small):
+def layer_backward(grad, given, kept, weights, small, queue, layer, first=()):
     s, y = lax.axis_index("section"), lax.axis_index("y")
     core = lax.axis_index("core")
     length = grad.shape[0]
     down, gu, out, win = weights["down"], weights["gu"], weights["out"], weights["in"]
 
-    def product(left, right, order):
+    def product(left, right, *tokens):
         mine = jnp.where(core == 0, right[0], right[1])
         theirs = jnp.where(core == 0, right[1], right[0])
-        left_two = jnp.concatenate([left, flip(left, "core")], axis=0)
-        right_two = jnp.concatenate([mine, flip(theirs, "core")], axis=0)
-        return narrow(t_dot(left_two, right_two))
+        return outer_sum((left, flip(left, "core")), (mine, flip(theirs, "core")), tokens)
+
+    def reduce(name, block):
+        nonlocal queue
+        if queue:
+            block, queue["last"] = lax.optimization_barrier((block, queue["last"]))
+        queue[name] = queue["last"] = lax.psum_scatter(
+            block, "fsdp", scatter_dimension=0, tiled=True
+        )
+
+    def due(point):
+        return [queue[k] for k in WAITS[layer].get(point, ())]
 
     halves = lambda v: (v[:, :HALF], v[:, HALF:])
     g0, g1 = halves(grad)
+    down_block = product(kept["act"], (g0, g1))
+    if layer == 1:
+        reduce("down1", down_block)
     grad_act = dot_t(g0, down[0]) + dot_t(g1, down[1])
     gate, up = kept["gate"], kept["up"]
     sig = jax.nn.sigmoid(gate)
     d_gate = narrow(grad_act * up * (sig * (1.0 + gate * (1.0 - sig))))
     d_up = narrow(grad_act * gate * sig)
+    if layer == 1:
+        reduce("gu1", product(kept["x2"], (d_gate, d_up), *first))
     part = dot_t(d_gate, gu[0]) + dot_t(d_up, gu[1])
-    d_mid, db, grad_gain1 = back_step(narrow(part), given, kept["mid"], small["gain1"])
+    d_mid, db, grad_gain1 = back_step(
+        narrow(part), given, kept["mid"], small["gain1"], due("mlp") + list(first)
+    )
     b0, b1 = halves(db)
     d_mo = dot_t(b0, out[0]) + dot_t(b1, out[1])
     mo = kept["mo"]
@@ -507,8 +772,12 @@
     stat_row = jnp.sum(jnp.where(is_ssm, d_mo * mo.astype(F32), 0.0), axis=1)
     stat = jnp.broadcast_to(stat_row[None, :], (8, length))
     blocks = jnp.transpose(narrow(d_mo).reshape(length, RANKS, R_OUT // RANKS), (1, 0, 2))
-    got, stats = swap(blocks, 1, stat)
+    got, stats = swap(blocks, stat, due("norm"))
     overlap = jnp.sum(stats[:, 0, :], axis=0)[:, None]
+    if layer == 0:
+        reduce("gu0", product(kept["x2"], (d_gate, d_up), got))
+    else:
+        reduce("out1", product(kept["mo"], (b0, b1), got))
     d_norm, d_o = from_rows(got)
     d_norm = d_norm.astype(F32)
     spread_of = kept["spread"][:, None]
@@ -537,7 +806,8 @@
             jnp.concatenate([d_c[:, R_BC:], d_value], axis=1),
         ]
     )
-    back = swap(narrow(message), 2).astype(F32)
+    back = swap(narrow(message), None, due("scan"))
+    back = back.astype(F32)
     d_bc = back[0, :, :R_BC] + back[1, :, :R_BC] + back[2, :, :R_BC] + back[3, :, :R_BC]
     d_kv = jnp.sum(lax.dynamic_slice_in_dim(back, 2 * s, 2, axis=0)[:, :, R_BC:], axis=0)
     d_kv = jnp.where(y == 0, rotary(d_kv, -1.0), d_kv)
@@ -559,22 +829,33 @@
     d_right = narrow(jnp.concatenate([d_z, rotary(d_query, -1.0)], axis=1))
     d_dt_b = narrow(d_dt)
     dt_own = columns(weights["dt"], R_HEADS * (2 * s + y), R_HEADS)
+    reduce(f"in{layer}", product(kept["x1"], (d_left, d_right)))
     part = dot_t(d_left, win[0]) + dot_t(d_right, win[1]) + dot_t(d_dt_b, dt_own)
+    got_gu = None
+    if layer == 0:
+        got_gu = share(queue["gu1"], queue["gu0"], 50)
     _, entering_grad, grad_gain0 = back_step(
-        narrow(part), d_mid, kept["resid"].astype(F32), small["gain0"]
-    )
-    shards = dict(
-        down=product(kept["act"], (g0, g1), 0),
-        gu=product(kept["x2"], (d_gate, d_up), 1),
-        out=product(mo, (b0, b1), 2),
-    )
-    shards["in"] = product(kept["x1"], (d_left, d_right), 3)
-    grad_dt_w = t_dot(kept["x1"], d_dt_b)
-    ranked = jnp.concatenate(
-        [grad_heads.reshape(-1), grad_conv.reshape(-1), grad_ssm_gain, grad_dt_w.reshape(-1)]
-    )
-    gains = jnp.concatenate([grad_gain0[0], grad_gain1[0]])
-    return entering_grad, shards, ranked, gains
+        narrow(part),
+        d_mid,
+        kept["resid"].astype(F32),
+        small["gain0"],
+        due("in") + list(got_gu or ())[:1],
+    )
+    if layer == 0:
+        reduce("out0", product(kept["mo"], (b0, b1), got_gu[0]))
+    two = lambda v: jnp.concatenate([v, flip(v, "core")], axis=0)
+    grad_dt_w = t_dot(two(jnp.pad(d_dt_b, ((0, 0), (0, 4)))), two(kept["x1"]))
+    smalls_grad = dict(
+        heads=grad_heads, conv=grad_conv, ssm=grad_ssm_gain[None], dt=grad_dt_w,
+        gains=jnp.concatenate([grad_gain0, grad_gain1], axis=0),
+    )
+    return entering_grad, smalls_grad, (down_block, reduce, got_gu)
+
+
+WAITS = (
+    {"mlp": ("out1",), "scan": ("in1",)},
+    {"norm": ("down1",), "in": ("gu1",)},
+)
 
 
 def body(
@@ -601,7 +882,9 @@
             w_in[:, D_SSM + CONV_W :].reshape(-1),
         ]
     )
-    everything = lax.all_gather(flat, ("section", "fsdp"), axis=0).reshape(2, nz, -1)
+    count = flat.shape[0]
+    flat = jnp.pad(flat, (0, -count % 2048)).reshape(-1, 128)
+    everything = lax.all_gather(flat, ("section", "fsdp"), axis=0).reshape(2, nz, -1)[..., :count]
 
     def unpack(layer):
         part = everything[layer]
@@ -661,17 +944,48 @@
             "down": lax.dynamic_slice(w_down, (down_rows * rk, side), (down_rows, HALF)),
         }
 
-    names = ("in", "out", "gu", "down")
+    order = []
+
+    def in_turn(value):
+        if order:
+            value, order[-1] = lax.optimization_barrier((value, order[-1]))
+        return value
+
+    def gather(piece):
+        order.append(lax.all_gather(in_turn(piece), ("core", "fsdp"), axis=0))
+        return order[-1]
+
     own, other = pieces(s), pieces(1 - s)
-    arrived = {name: flip(other[name], "section") for name in names}
-
-    def gathered(layer):
-        result = {}
-        for name in names:
-            piece = jnp.where(s == layer, own[name], arrived[name])
-            whole = lax.all_gather(piece, ("core", "fsdp"), axis=0)
-            result[name] = whole.reshape(2, nz * piece.shape[0], HALF)
-        return result
+    out_own = gather(own["out"])
+    mlp = lambda found: jnp.concatenate([found["gu"], found["down"]], axis=0)
+    in_arrived = flip(other["in"], "section")
+    out_sent, in_arrived = lax.optimization_barrier((other["out"], in_arrived))
+    out_arrived = flip(out_sent, "section")
+    mlp_own = mlp(own)
+    mlp_sent, out_arrived = lax.optimization_barrier((mlp(other), out_arrived))
+    mlp_arrived = flip(mlp_sent, "section")
+    of_layer = lambda layer, mine, theirs: jnp.where(s == layer, mine, theirs)
+    flat_rows = lambda whole: whole.reshape(2, -1, HALF)
+    in0 = gather(copy_after(of_layer(0, own["in"], in_arrived), everything))
+    out_other = gather(copy_after(out_arrived, in0))
+    wide = own["gu"].shape[0]
+    mlp0, mlp1 = (of_layer(layer, mlp_own, mlp_arrived) for layer in range(2))
+    gu0 = gather(mlp0[:wide])
+    down0 = gather(mlp0[wide:])
+    in1 = gather(of_layer(1, own["in"], in_arrived))
+    gu1 = gather(mlp1[:wide])
+    down1 = gather(mlp1[wide:])
+    weights = [
+        dict(
+            out=flat_rows(of_layer(layer, out_own, out_other)),
+            **{"in": flat_rows((in0, in1)[layer])},
+        )
+        for layer in range(2)
+    ]
+    weights[0]["gu"] = flat_rows(gu0)
+    weights[0]["down"] = flat_rows(down0)
+    weights[1]["gu"] = flat_rows(gu1)
+    weights[1]["down"] = flat_rows(down1)
 
     def whole_sequence(own_rows):
         place = 2 * y + core
@@ -694,11 +1008,9 @@
         return cut_rows(whole, rows * rank, rows)
 
     smalls = []
-    weights = []
     for layer in range(2):
-        small, dt_w = unpack(layer)
+        small, weights[layer]["dt"] = unpack(layer)
         smalls.append(small)
-        weights.append(dict(gathered(layer), dt=dt_w))
     hidden = whole_sequence(inputs[:, 0])
     grad = whole_sequence(cotangent[:, 0])
     outs, kept = [], []
@@ -709,10 +1021,17 @@
         outs.append(hidden)
         kept.append(keep)
     grads = [None, None]
-    shards, ranked, gains = [None, None], [None, None], [None, None]
+    smalls_grad, queue = [None, None], {}
     for layer in (1, 0):
-        grad, shards[layer], ranked[layer], gains[layer] = layer_backward(
-            grad, rank_rows(grad).astype(F32), kept[layer], weights[layer], smalls[layer]
+        grad, smalls_grad[layer], blocks = layer_backward(
+            grad,
+            rank_rows(grad).astype(F32),
+            kept[layer],
+            weights[layer],
+            smalls[layer],
+            queue,
+            layer,
+            (outs[1],) if layer == 1 else (),
         )
         grads[layer] = grad
 
@@ -724,94 +1043,69 @@
         both = jnp.where(core == 0, jnp.stack([mine, theirs]), jnp.stack([theirs, mine]))
         return both[None, :, None]
 
-    def assembled(name):
-        parts = []
-        for layer in (1, 0):
-            blocks = shards[layer][name]
-            parts.append(lax.psum_scatter(blocks, "fsdp", scatter_dimension=0, tiled=True))
-        one, zero = parts
-        mine = jnp.where(s == 0, zero, one)
-        sent = jnp.where(s == 0, one, zero)
-        theirs = flip(sent, "section")
-        both = jnp.where(s == 0, jnp.stack([mine, theirs]), jnp.stack([theirs, mine]))
-        whole = lax.all_gather(both, ("y", "core"), axis=0)
-        return whole.reshape(2, 2, 2, blocks.shape[0] // nz, HALF)
-
-    ranks = [(a, b) for a in range(2) for b in range(2)]
-
-    def by_rank(whole, rk, side):
-        return whole[rk[1], side, rk[0]]
-
-    got_down = assembled("down")
-    got_gu = assembled("gu")
-    got_out = assembled("out")
-    got_in = assembled("in")
-
+    down_block, reduce, got_gu = blocks
+    fan = lambda array, axis: jnp.moveaxis(
+        array.reshape(array.shape[:axis] + (nz, -1) + array.shape[axis + 1 :]), axis, 0
+    )
+    dt_rows = jnp.concatenate([fan(g["dt"], 1) for g in smalls_grad], axis=2)
+    dt_rows = jnp.pad(dt_rows, ((0, 0), (0, 0), (0, HALF - dt_rows.shape[2])))
+
+    def placed(array, total, starts):
+        whole = jnp.zeros((array.shape[0], total), F32)
+        at = 0
+        for start, width in starts:
+            whole = lax.dynamic_update_slice(whole, array[:, at : at + width], (0, start))
+            at += width
+        return fan(whole, 1).reshape(nz, -1)
+
+    listed = []
+    for g in smalls_grad:
+        listed.append(fan(g["gains"], 1).reshape(nz, -1))
+        listed.append(placed(g["heads"], SSM_HEADS, [(R_HEADS * rank, R_HEADS)]))
+        listed.append(
+            placed(g["conv"], CONV_W, [(R_SSM * rank, R_SSM), (D_SSM + R_BC * rank, R_BC)])
+        )
+        listed.append(placed(g["ssm"], D_SSM, [(R_SSM * rank, R_SSM)]))
+    packed = jnp.concatenate(listed, axis=1)
+    packed = packed + flip(packed, "core")
+    amount = packed.shape[1]
+    packed = jnp.pad(packed, ((0, 0), (0, -amount % (16 * HALF)))).reshape(nz, -1, HALF)
+    down_rows = R_FF // nz
+    extra = jnp.concatenate([dt_rows, packed], axis=1)
+    extra_count = extra.shape[1]
+    last = jnp.concatenate([down_block.reshape(nz, down_rows, HALF), narrow(extra)], axis=1)
+    reduce("down0", last.reshape(-1, HALF))
+    down0, extra = queue["down0"][:down_rows], queue["down0"][down_rows:]
+
+    place = jnp.stack([y, core]).astype(jnp.int32)
+    grad_w_gu = spread_gate_up(place, got_gu, nz)
+    got_in = share(queue["in1"], queue["in0"], 50)
+    got_out = share(queue["out1"], queue["out0"], 30, (got_in[0],))
+    shared = swap(extra).astype(F32)
+    got_down = share(queue["down1"], down0, 30)
     out_rows, o_rows = R_SSM // nz, R_ATT // nz
-    rows_of = lambda whole, lo, hi: jnp.concatenate(
-        [
-            jnp.concatenate([by_rank(whole, rk, side)[lo:hi] for side in range(2)], axis=1)
-            for rk in ranks
-        ],
-        axis=0,
-    ).astype(F32)
-    grad_w_down = rows_of(got_down, 0, R_FF // nz)
-    grad_w_out = rows_of(got_out, 0, out_rows)
-    grad_w_o = rows_of(got_out, out_rows, out_rows + o_rows)
-    ff = R_FF // nz
-    grad_w_gu = jnp.concatenate(
-        [
-            by_rank(got_gu, rk, side)[:, ff * k : ff * (k + 1)]
-            for side in range(2)
-            for k in range(nz)
-            for rk in ranks
-        ],
-        axis=1,
-    ).astype(F32)
-
-    vector = jnp.concatenate([ranked[0], ranked[1], gains[0], gains[1]])
-    count = vector.shape[0]
-    padded = jnp.pad(vector, (0, -count % 1024)).reshape(-1, 128)
-    summed = lax.psum(padded, ("core", "fsdp"))
-    all_ranks = lax.all_gather(summed, ("section", "y"), axis=0).reshape(RANKS, -1)
-    per = ranked[0].shape[0]
-    mine = jnp.where(s == 0, all_ranks[:, :per], all_ranks[:, per : 2 * per])
-    gain_all = jnp.sum(all_ranks[:, 2 * per : 2 * per + 4 * D], axis=0).reshape(2, 2, D)
-    gain_mine = jnp.where(s == 0, gain_all[0], gain_all[1])
-    a0 = 3 * R_HEADS
-    a1 = a0 + 5 * R_CONV
-    a2 = a1 + R_SSM
-    head_all = jnp.concatenate([mine[k, :a0].reshape(3, R_HEADS) for k in range(RANKS)], axis=1)
-    convs = [mine[k, a0:a1].reshape(5, R_CONV) for k in range(RANKS)]
-    conv_all = jnp.concatenate(
-        [c[:, :R_SSM] for c in convs] + [c[:, R_SSM:] for c in convs], axis=1
-    )
-    ssm_all = mine[:, a1:a2].reshape(-1)
-    dt_all = jnp.concatenate([mine[k, a2:].reshape(D, R_HEADS) for k in range(RANKS)], axis=1)
-
-    def shard(array, axis):
-        width = array.shape[axis] // nz
-        return lax.dynamic_slice_in_dim(array, width * z_place, width, axis)
-
-    grad_w_in = jnp.concatenate(
-        [by_rank(got_in, rk, 1)[:, :R_SSM].astype(F32) for rk in ranks]
-        + [by_rank(got_in, rk, 0)[:, :R_SSM].astype(F32) for rk in ranks]
-        + [by_rank(got_in, rk, 0)[:, R_SSM:R_CONV].astype(F32) for rk in ranks]
-        + [shard(dt_all, 0)],
-        axis=1,
-    )
-    grad_w_qkv = jnp.concatenate(
-        [by_rank(got_in, rk, 1)[:, R_SSM:] for rk in ranks]
-        + [by_rank(got_in, (head, part), 0)[:, R_CONV:] for part in range(2) for head in range(2)],
-        axis=1,
-    ).astype(F32)
+    grad_w_out = spread_rows(place, got_out, 0, out_rows, o_rows)
+    grad_w_o = spread_rows(place, got_out, out_rows, o_rows, o_rows)
+    grad_w_down = spread_rows(place, got_down, 0, down_rows, min(down_rows, 128))
+
+    width = D // nz
+    dt_all = jnp.where(s == 0, shared[:, :12, :width], shared[:, :12, width : 2 * width])
+    grad_w_in, grad_w_qkv = spread_in(place, got_in, dt_all.reshape(SSM_HEADS, width))
+    grad_w_in = grad_w_in.T
+    small_sum = jnp.sum(shared[:, 16:], axis=0).reshape(-1)[:amount].reshape(2, -1)
+    small_sum = jnp.where(s == 0, small_sum[0], small_sum[1])
+    cuts, at = [], 0
+    for lead, total in ((2, D), (3, SSM_HEADS), (5, CONV_W), (1, D_SSM)):
+        size = lead * total // nz
+        cuts.append(small_sum[at : at + size].reshape(lead, total // nz))
+        at += size
     return (
         block_rows(outs),
         block_rows(grads),
-        shard(gain_mine, 1)[None],
-        shard(head_all, 1)[None],
-        shard(conv_all, 1)[None],
-        shard(ssm_all, 0)[None],
+        cuts[0][None],
+        cuts[1][None],
+        cuts[2][None],
+        cuts[3],
         grad_w_in[None],
         grad_w_out[None],
         grad_w_qkv[None],
@@ -822,6 +1116,7 @@
 
 
 def solution(mesh):
+    CHANNELS.clear()
     sections, ctx, fsdp = mesh.devices.shape
     fine = Mesh(
         mesh.devices.reshape(sections, ctx // 2, 2, fsdp), ("section", "y", "core", "fsdp")

time: 1670 us -> 1200 us (0.72)
  waiting for transfers between devices: 829 us -> 236 us
  Pallas kernels: 292 us -> 551 us
  local copies, waits for them, and re-layouts: 197 us -> 131 us
  other arithmetic: 128 us -> 79.5 us
  matrix products: 167 us -> 125 us
  blocking collectives: 0 us -> 35.1 us
    reduce_scatter x8, waiting for transfers between devices: 304 us -> 9.6 us  [reduce(): lax.psum_scatter(block, 'fsdp', scatter_dimension=0, tiled=True)]
    pallas_call x16 -> x36, Pallas kernels: 292 us -> 551 us  [the longest x8 224 us: rank_call(): pl.pallas_call(ignoring(kernel, len(args), len(after)), out_shape=out_sha...]
    all_gather x13 -> x8, waiting for transfers between devices: 285 us -> 169 us  [gather(): order.append(lax.all_gather(in_turn(piece), ('core', 'fsdp'), axis=0))]
    ppermute x26 -> x24, waiting for transfers between devices: 152 us -> 48.8 us  [flip(): return lax.ppermute(value, axis, [(0, 1), (1, 0)])]
    psum x1 -> x0, waiting for transfers between devices: 70.1 us -> none  [body(): summed = lax.psum(padded, ('core', 'fsdp'))]
    dot_general x12 -> x4, matrix products: 44.2 us -> 4.55 us  [t_dot(): lax.dot_general(left, right, (((0,), (0,)), ((), ())), preferred_element_...]
    all_gather x0 -> x1, blocking collectives: none -> 35.1 us  [body(): lax.all_gather(flat, ('section', 'fsdp'), axis=0).reshape(2, nz, -1)]
    convert_element_type x8 -> x3, other arithmetic: 23.6 us -> 0.21 us  [the longest x2 0.17 us: layer_backward(): back = back.astype(F32)]
  transfers between devices with their start and end apart: 55 -> 46, of which waited for: 37 -> 16; matrix products, arithmetic and copies ran while one was open for 18% -> 24% of each run, Pallas kernels for 10% -> 42%
where the time goes in v2:
time: 1200 us; the launch traced here: 1190 us
  Pallas kernels  551 us (46%)
  waiting for transfers between devices  236 us (20%)
  local copies, waits for them, and re-layouts  131 us (11%)
  matrix products  125 us (10%)
  other arithmetic  79.5 us (7%)
  blocking collectives  35.1 us (3%)
  between operations  18.5 us (2%)
  starting transfers between devices  16.1 us (1%)
    pallas_call x8, Pallas kernels, rank_call(): pl.pallas_call(ignoring(kernel, len(args), len(after)), out_shape=out_sha...  224 us
    all_gather x8, waiting for transfers between devices, gather(): order.append(lax.all_gather(in_turn(piece), ('core', 'fsdp'), axis=0))  169 us
    pallas_call x4, Pallas kernels, share(): pl.pallas_call(ignoring(share_kernel, 2, len(after)), out_shape=[shape] *...  159 us
    pallas_call x9, Pallas kernels, swap(): pl.pallas_call(ignoring(functools.partial(swap_kernel, stat is not None),...  81.8 us
    pallas_call x8, Pallas kernels, outer_sum(): pl.pallas_call(ignoring(product_kernel, 4, len(tokens)), grid=(width // t...  52.2 us
    ppermute x24, waiting for transfers between devices, flip(): return lax.ppermute(value, axis, [(0, 1), (1, 0)])  48.8 us
    dot_general x20, matrix products, dot(): return jnp.dot(left, right, preferred_element_type=F32)  43.9 us
    dot_general x20, matrix products, dot_t(): lax.dot_general(left, right, (((1,), (1,)), ((), ())), preferred_element_...  39.9 us
  transfers between devices with their start and end apart: 46, of which 16 were waited for; matrix products, arithmetic and copies ran while one was open for 24% of the time, Pallas kernels for 42%

profile of v2, /device:TPU:0, one launch (start us, length us, event | category | flops | bytes accessed | tf_op | source)
XLA Modules:
  0.0 1191.9 jit_solution(10537952107431387554)
XLA Ops:
  20.4 35.1 %all_gather.51 = bf16[8,256,128]{2,1,0:T(8,128)(2,1)S(1)} all-gather(bf16[1,256,128]{2,1,0:T(8,128)(2,1)S(1)} %pad_bitcast_fusion), channel_id=1, replica_groups=mesh['section'=2,'y'=2,'core'=2,'fsdp'=4] {'section','fsdp'}, dimensions={0}, use_global_device_ids=true | all-gather | bytes 589824 | tf_op jit(solution)/shard_map/all_gather | solution.py:887
  84.2 68.7 %all-gather.19.cloned.1.call-done = bf16[4096,1024]{1,0:T(8,128)(2,1)} async-done(((bf16[512,1024]{1,0:T(8,128)(2,1)}), bf16[4096,1024]{1,0:T(8,128)(2,1)}) %all-gather.19.cloned.1.call-update) | async-done | bytes 8388624 | tf_op jit(solution)/shard_map/all_gather | solution.py:955
  156.3 35.0 %collective-permute-done.5 = bf16[768,1024]{1,0:T(8,128)(2,1)S(1)} collective-permute-done((bf16[768,1024]{1,0:T(8,128)(2,1)S(1)}, bf16[768,1024]{1,0:T(8,128)(2,1)S(1)}, u32[]{:S(2)}, u32[]{:S(2)}) %collective-permute-start.5) | collective-permute-done | bytes 1572896 | tf_op jit(solution)/shard_map/ppermute | solution.py:661
  247.5 9.7 shard_map.212
  272.2 9.4 shard_map.213
  290.1 27.5 %shard_map.215 = (f32[64,2048]{1,0:T(8,128)S(1)}, bf16[256,2048]{1,0:T(8,128)(2,1)}) custom-call(bf16[256,2048]{1,0:T(8,128)(2,1)S(1)} %pad_maximum_fusion.5.part_ref, bf16[64,2048]{1,0:T(8,128)(2,1)S(1)} %get-tuple-element.242.resid_ref, f32[1,2048]{1,0:T(1,128)S(1)} %bitcast.564), custom_call_target="tpu_custom_call" | custom-call | bytes 22950000 | tf_op jit(solution)/shard_map/pallas_call | solution.py:236
  333.9 28.3 %shard_map.216 = bf16[256,2048]{1,0:T(8,128)(2,1)S(1)} custom-call(bf16[256,2048]{1,0:T(8,128)(2,1)S(1)} %pad_maximum_fusion.6.part_ref, f32[64,2048]{1,0:T(8,128)S(1)} %get-tuple-element.81.resid_ref.refs_2_), custom_call_target="tpu_custom_call" | custom-call | bytes 22950000 | tf_op jit(solution)/shard_map/pallas_call | solution.py:236
  363.8 49.5 %all-gather.27.cloned.1.call-done = bf16[4096,1024]{1,0:T(8,128)(2,1)} async-done(((bf16[512,1024]{1,0:T(8,128)(2,1)}), bf16[4096,1024]{1,0:T(8,128)(2,1)}) %all-gather.27.cloned.1.call-update) | async-done | bytes 8388624 | tf_op jit(solution)/shard_map/all_gather | solution.py:955
  421.9 9.5 shard_map.217
  450.0 9.1 shard_map.218
  463.1 26.5 %shard_map.219 = (f32[64,2048]{1,0:T(8,128)S(1)}, bf16[256,2048]{1,0:T(8,128)(2,1)S(1)}) custom-call(bf16[256,2048]{1,0:T(8,128)(2,1)S(1)} %pad_maximum_fusion.7.part_ref, bf16[64,2048]{1,0:T(8,128)(2,1)S(1)} %get-tuple-element.249.resid_ref, f32[1,2048]{1,0:T(1,128)S(1)} %bitcast.566), custom_call_target="tpu_custom_call" | custom-call | bytes 22950000 | tf_op jit(solution)/shard_map/pallas_call | solution.py:236
  512.8 30.1 %all-gather.31.cloned.1.call-done = bf16[2048,1024]{1,0:T(8,128)(2,1)} async-done(((bf16[256,1024]{1,0:T(8,128)(2,1)}), bf16[2048,1024]{1,0:T(8,128)(2,1)}) %all-gather.31.cloned.1.call-update) | async-done | bytes 4194320 | tf_op jit(solution)/shard_map/all_gather | solution.py:955
  550.6 28.2 %shard_map.220.refs_4_ = bf16[256,2048]{1,0:T(8,128)(2,1)S(1)} custom-call(bf16[256,2048]{1,0:T(8,128)(2,1)S(1)} %pad_maximum_fusion.8.part_ref, f32[64,2048]{1,0:T(8,128)S(1)} %get-tuple-element.88.resid_ref.refs_2_), custom_call_target="tpu_custom_call" | custom-call | bytes 22950000 | tf_op jit(solution)/shard_map/pallas_call | solution.py:236
  604.1 28.1 %shard_map.221 = (f32[64,2048]{1,0:T(8,128)S(1)}, bf16[256,2048]{1,0:T(8,128)(2,1)S(1)}, f32[1,2048]{1,0:T(1,128)S(1)}) custom-call(bf16[256,2048]{1,0:T(8,128)(2,1)S(1)} %fusion.50.refs_0_, f32[64,2048]{1,0:T(8,128)S(1)} %dynamic-slice_convert_fusion.1.refs_1_, f32[64,2048]{1,0:T(8,128)S(1)} %get-tuple-element.88.resid_ref.refs_2_, ...), custom_call_target="tpu_custom_call" | custom-call | bytes 22950000 | tf_op jit(solution)/shard_map/pallas_call | solution.py:236
  636.3 9.8 shard_map.223
  730.3 29.8 %shard_map.226 = (f32[64,2048]{1,0:T(8,128)}, bf16[256,2048]{1,0:T(8,128)(2,1)S(1)}, f32[1,2048]{1,0:T(1,128)S(1)}) custom-call(bf16[256,2048]{1,0:T(8,128)(2,1)S(1)} %fusion.48.refs_0_, f32[64,2048]{1,0:T(8,128)S(1)} %copy-done.38, f32[64,2048]{1,0:T(8,128)S(1)} %get-tuple-element.248.refs_2_, f32[1,2048]{1,0:T(1,128)S(1)} %bitcast.569, ...), custom_call_target="tpu_custom_call" | custom-call | bytes 22950000 | tf_op jit(solution)/shard_map/pallas_call | solution.py:236
  767.7 27.5 %shard_map.228 = (f32[64,2048]{1,0:T(8,128)S(1)}, bf16[256,2048]{1,0:T(8,128)(2,1)S(1)}, f32[1,2048]{1,0:T(1,128)S(1)}) custom-call(bf16[256,2048]{1,0:T(8,128)(2,1)S(1)} %fusion.53.refs_0_, f32[64,2048]{1,0:T(8,128)S(1)} %dynamic-slice_convert_fusion.refs_1_, f32[64,2048]{1,0:T(8,128)S(1)} %copy-done.15, f32[1,2048]{1,0:T(1,128)S(1)} %bitcast.565, ...), custom_call_target="tpu_custom_call" | custom-call | bytes 22950000 | tf_op jit(solution)/shard_map/pallas_call | solution.py:236
  797.7 10.0 shard_map.229
  859.4 9.7 shard_map.231
  910.8 51.6 %shard_map.233 = (bf16[2,512,1024]{2,1,0:T(8,128)(2,1)}, bf16[2,512,1024]{2,1,0:T(8,128)(2,1)}, bf16[2,512,1024]{2,1,0:T(8,128)(2,1)}, bf16[2,512,1024]{2,1,0:T(8,128)(2,1)}) custom-call(bf16[512,1024]{1,0:T(8,128)(2,1)} %reduce-scatter.11.cloned.1.call-done.refs_4_.one_ref, bf16[512,1024]{1,0:T(8,128)(2,1)} %reduce-scatter.17.cloned.1.call-done.zero_ref), custom_call_target="tpu_custom_call" | custom-call | bytes 42500000 | tf_op jit(solution)/shard_map/pallas_call | solution.py:397
  979.8 28.4 %shard_map.234 = (f32[64,2048]{1,0:T(8,128)}, bf16[256,2048]{1,0:T(8,128)(2,1)S(1)}, f32[1,2048]{1,0:T(1,128)S(1)}) custom-call(bf16[256,2048]{1,0:T(8,128)(2,1)S(1)} %fusion.49.refs_0_, f32[64,2048]{1,0:T(8,128)S(1)} %copy-done.40, f32[64,2048]{1,0:T(8,128)S(1)} %copy-done.21, f32[1,2048]{1,0:T(1,128)S(1)} %bitcast.568, bf16[2,512,1024]{2,1,0:T(8,128)(2,1)S(1)} %copy-done), custom_call_target="tpu_custom_call" | custom-call | bytes 22950000 | tf_op jit(solution)/shard_map/pallas_call | solution.py:236
  1034.0 52.5 %shard_map.239 = (bf16[2,512,1024]{2,1,0:T(8,128)(2,1)}, bf16[2,512,1024]{2,1,0:T(8,128)(2,1)}, bf16[2,512,1024]{2,1,0:T(8,128)(2,1)}, bf16[2,512,1024]{2,1,0:T(8,128)(2,1)}) custom-call(bf16[512,1024]{1,0:T(8,128)(2,1)} %reduce-scatter.15.cloned.1.call-done.refs_1_.one_ref, bf16[512,1024]{1,0:T(8,128)(2,1)} %reduce-scatter.19.cloned.1.call-done.zero_ref), custom_call_target="tpu_custom_call" | custom-call | bytes 42500000 | tf_op jit(solution)/shard_map/pallas_call | solution.py:397
  1086.5 27.6 %shard_map.241 = (bf16[2,256,1024]{2,1,0:T(8,128)(2,1)}, bf16[2,256,1024]{2,1,0:T(8,128)(2,1)}, bf16[2,256,1024]{2,1,0:T(8,128)(2,1)}, bf16[2,256,1024]{2,1,0:T(8,128)(2,1)}) custom-call(bf16[256,1024]{1,0:T(8,128)(2,1)} %reduce-scatter.13.cloned.1.call-done.refs_4_.refs_0_, bf16[256,1024]{1,0:T(8,128)(2,1)} %reduce-scatter.21.cloned.1.call-done.refs_1_, ...), custom_call_target="tpu_custom_call" | custom-call | bytes 25500000 | tf_op jit(solution)/shard_map/pallas_call | solution.py:397
  1139.0 27.5 %shard_map.245 = (bf16[2,256,1024]{2,1,0:T(8,128)(2,1)}, bf16[2,256,1024]{2,1,0:T(8,128)(2,1)}, bf16[2,256,1024]{2,1,0:T(8,128)(2,1)}, bf16[2,256,1024]{2,1,0:T(8,128)(2,1)}) custom-call(bf16[256,1024]{1,0:T(8,128)(2,1)} %reduce-scatter.9.cloned.1.call-done.refs_2_.one_ref, bf16[256,1024]{1,0:T(8,128)(2,1)} %slice.859.zero_ref), custom_call_target="tpu_custom_call" | custom-call | bytes 25500000 | tf_op jit(solution)/shard_map/pallas_call | solution.py:397
  (961 shorter events, 504.2 us)
Async XLA Ops:
  7.2 62.8 %all-gather.17.cloned.1.call-start = ((), (), s32[]{:S(2)}) async-start(), calls=%async_computation.16 | async-start | bytes 4718592 | tf_op jit(solution)/shard_map/all_gather | solution.py:955
  10.3 142.6 %all-gather.19.cloned.1.call-start = ((), (), s32[]{:S(2)}) async-start(), calls=%async_computation.17 | async-start | bytes 9437184 | tf_op jit(solution)/shard_map/all_gather | solution.py:955
  70.0 130.7 %all-gather.21.cloned.1.call-start = ((), (), s32[]{:S(2)}) async-start(), calls=%async_computation.18 | async-start | bytes 4718592 | tf_op jit(solution)/shard_map/all_gather | solution.py:955
  154.7 163.0 %all-gather.23.cloned.1.call-start = ((), (), s32[]{:S(2)}) async-start(), calls=%async_computation.19 | async-start | bytes 9437184 | tf_op jit(solution)/shard_map/all_gather | solution.py:955
  200.8 129.4 %all-gather.25.cloned.1.call-start = ((), (), s32[]{:S(2)}) async-start(), calls=%async_computation.20 | async-start | bytes 4718592 | tf_op jit(solution)/shard_map/all_gather | solution.py:955
  201.7 211.6 %all-gather.27.cloned.1.call-start = ((), (), s32[]{:S(2)}) async-start(), calls=%async_computation.21 | async-start | bytes 9437184 | tf_op jit(solution)/shard_map/all_gather | solution.py:955
  202.3 293.3 %all-gather.29.cloned.1.call-start = ((), (), s32[]{:S(2)}) async-start(), calls=%async_computation.22 | async-start | bytes 9437184 | tf_op jit(solution)/shard_map/all_gather | solution.py:955
  210.2 332.7 %all-gather.31.cloned.1.call-start = ((), (), s32[]{:S(2)}) async-start(), calls=%async_computation.23 | async-start | bytes 4718592 | tf_op jit(solution)/shard_map/all_gather | solution.py:955
  231.3 274.1 %collective-permute-start.11 = (bf16[256,1024]{1,0:T(8,128)(2,1)}, bf16[256,1024]{1,0:T(8,128)(2,1)}, u32[]{:S(2)}, u32[]{:S(2)}) collective-permute-start(bf16[256,1024]{1,0:T(8,128)(2,1)} %get-tuple-element.307), channel_id=1, source_target_pairs={{0,4},{4,0},{1,5},{5,1},{2,6},{6,2},{3,7},{7,3},{8,12},{12,8},{9,1... | collective-permute-start | bytes 1572872 | tf_op jit(solution)/shard_map/ppermute | solution.py:661
  240.1 348.8 %reduce-scatter.9.cloned.1.call-start = ((), (), s32[]{:S(2)}) async-start(), calls=%async_computation.8 | async-start | bytes 2621440 | tf_op jit(solution)/shard_map/reduce_scatter | solution.py:745
  512.7 164.6 %reduce-scatter.11.cloned.1.call-start = ((), (), s32[]{:S(2)}) async-start(), calls=%async_computation.9 | async-start | bytes 5242880 | tf_op jit(solution)/shard_map/reduce_scatter | solution.py:745
  588.9 131.2 %reduce-scatter.13.cloned.1.call-start = ((), (), s32[]{:S(2)}) async-start(), calls=%async_computation.10 | async-start | bytes 2621440 | tf_op jit(solution)/shard_map/reduce_scatter | solution.py:745
  595.7 109.5 %collective-permute-start.16 = (bf16[256,2048]{1,0:T(8,128)(2,1)}, bf16[256,2048]{1,0:T(8,128)(2,1)}, u32[]{:S(2)}, u32[]{:S(2)}) collective-permute-start(bf16[256,2048]{1,0:T(8,128)(2,1)} %fusion.61.left_a), channel_id=1, source_target_pairs={{0,4},{4,0},{1,5},{5,1},{2,6},{6,2},{3,7},{7,3},{8,12},{12,8},{9,1... | collective-permute-start | bytes 3145736 | tf_op jit(solution)/shard_map/ppermute | solution.py:661
  677.3 139.5 %reduce-scatter.15.cloned.1.call-start = ((), (), s32[]{:S(2)}) async-start(), calls=%async_computation.11 | async-start | bytes 5242880 | tf_op jit(solution)/shard_map/reduce_scatter | solution.py:745
  720.2 173.2 %reduce-scatter.17.cloned.1.call-start = ((), (), s32[]{:S(2)}) async-start(), calls=%async_computation.12 | async-start | bytes 5242880 | tf_op jit(solution)/shard_map/reduce_scatter | solution.py:745
  720.6 88.0 %collective-permute-start.18 = (bf16[256,2048]{1,0:T(8,128)(2,1)}, bf16[256,2048]{1,0:T(8,128)(2,1)}, u32[]{:S(2)}, u32[]{:S(2)}) collective-permute-start(bf16[256,2048]{1,0:T(8,128)(2,1)} %get-tuple-element.77.refs_0_), channel_id=1, source_target_pairs={{0,4},{4,0},{1,5},{5,1},{2,6},{6,2},{3,7},{7,3},{8,12},{12,8},{9,1... | collective-permute-start | bytes 3145736 | tf_op jit(solution)/shard_map/ppermute | solution.py:661
  816.8 156.8 %reduce-scatter.19.cloned.1.call-start = ((), (), s32[]{:S(2)}) async-start(), calls=%async_computation.13 | async-start | bytes 5242880 | tf_op jit(solution)/shard_map/reduce_scatter | solution.py:745
  820.1 62.6 %collective-permute-start.24 = (bf16[256,2048]{1,0:T(8,128)(2,1)}, bf16[256,2048]{1,0:T(8,128)(2,1)}, u32[]{:S(2)}, u32[]{:S(2)}) collective-permute-start(bf16[256,2048]{1,0:T(8,128)(2,1)} %multiply_convert_fusion.2.left_a), channel_id=1, source_target_pairs={{0,4},{4,0},{1,5},{5,1},{2,6},{6,2},{3,7},{7,3},{8,12},{12,8},{9,1... | collective-permute-start | bytes 3145736 | tf_op jit(solution)/shard_map/ppermute | solution.py:661
  893.4 128.5 %reduce-scatter.21.cloned.1.call-start = ((), (), s32[]{:S(2)}) async-start(), calls=%async_computation.14 | async-start | bytes 2621440 | tf_op jit(solution)/shard_map/reduce_scatter | solution.py:745
  893.7 118.5 %collective-permute-start.21 = (bf16[256,1024]{1,0:T(8,128)(2,1)}, bf16[256,1024]{1,0:T(8,128)(2,1)}, u32[]{:S(2)}, u32[]{:S(2)}) collective-permute-start(bf16[256,1024]{1,0:T(8,128)(2,1)} %copy-done.110), channel_id=1, source_target_pairs={{0,4},{4,0},{1,5},{5,1},{2,6},{6,2},{3,7},{7,3},{8,12},{12,8},{9,1... | collective-permute-start | bytes 1572872 | tf_op jit(solution)/shard_map/ppermute | solution.py:661
  894.4 115.8 %collective-permute-start.25 = (bf16[256,16]{0,1:T(8,128)(2,1)}, bf16[256,16]{0,1:T(8,128)(2,1)}, u32[]{:S(2)}, u32[]{:S(2)}) collective-permute-start(bf16[256,16]{0,1:T(8,128)(2,1)} %pad.30), channel_id=1, source_target_pairs={{0,4},{4,0},{1,5},{5,1},{2,6},{6,2},{3,7},{7,3},{8,12},{12,8},{9,1... | collective-permute-start | bytes 24584 | tf_op jit(solution)/shard_map/ppermute | solution.py:661
  899.7 112.5 %collective-permute-start.22 = (bf16[256,1024]{1,0:T(8,128)(2,1)}, bf16[256,1024]{1,0:T(8,128)(2,1)}, u32[]{:S(2)}, u32[]{:S(2)}) collective-permute-start(bf16[256,1024]{1,0:T(8,128)(2,1)} %get-tuple-element.298), channel_id=1, source_target_pairs={{0,4},{4,0},{1,5},{5,1},{2,6},{6,2},{3,7},{7,3},{8,12},{12,8},{9,1... | collective-permute-start | bytes 1572872 | tf_op jit(solution)/shard_map/ppermute | solution.py:661
  899.8 62.6 %collective-permute-start.27 = (bf16[256,1024]{1,0:T(8,128)(2,1)}, bf16[256,1024]{1,0:T(8,128)(2,1)S(1)}, u32[]{:S(2)}, u32[]{:S(2)}) collective-permute-start(bf16[256,1024]{1,0:T(8,128)(2,1)} %get-tuple-element.244.refs_0_), channel_id=1, source_target_pairs={{0,4},{4,0},{1,5},{5,1},{2,6},{6,2},{3,7},{7,3},{8,12},{12,8},{9,1... | collective-permute-start | bytes 1572872 | tf_op jit(solution)/shard_map/ppermute | solution.py:661
  973.6 153.9 %reduce-scatter.23.cloned.1.call-start = ((), (), s32[]{:S(2)}) async-start(), calls=%async_computation.15 | async-start | bytes 2949120 | tf_op jit(solution)/shard_map/reduce_scatter | solution.py:745
  (243 other events, 3024.0 us)
Sparse Core Ops, SparseCore 0:
  10.4 59.5 all-gather.16
  72.2 80.6 all-gather.18
  155.1 45.6 all-gather.20
  202.2 80.7 all-gather.22
  284.5 45.6 all-gather.24
  332.2 81.0 all-gather.26
  414.9 80.5 all-gather.28
  497.1 45.6 all-gather.30
  545.7 42.5 reduce-scatter.8
  591.1 76.0 reduce-scatter.10
  677.4 42.6 reduce-scatter.12
  723.0 76.0 reduce-scatter.14
  816.9 76.3 reduce-scatter.16
  896.2 77.3 reduce-scatter.18
  976.3 44.3 reduce-scatter.20
  1023.5 47.4 reduce-scatter.22

commit v3 on v2

--- a/solution.py
+++ b/solution.py
@@ -321,6 +321,7 @@
         in_specs=[left_block] * 2 + [right_block] * 2 + [ANY_SPEC] * len(tokens),
         out_specs=pl.BlockSpec((tile, columns_right), lambda i: (i, 0)),
         cost_estimate=lasting(3),
+        compiler_params=pltpu.CompilerParams(vmem_limit_bytes=56 * 2**20),
     )(*left, *right, *tokens)
 
 
@@ -442,7 +443,7 @@
         out_shape=jax.ShapeDtypeStruct((RANKS * count, D), F32),
         in_specs=[PLACE_SPEC] + [block] * 4,
         out_specs=pl.BlockSpec((tile, D), lambda r, i: (r * steps + i, 0)),
-        compiler_params=pltpu.CompilerParams(vmem_limit_bytes=32 * 2**20),
+        compiler_params=pltpu.CompilerParams(vmem_limit_bytes=56 * 2**20),
     )(place, *pieces)
 
 
@@ -468,11 +469,11 @@
         out_shape=jax.ShapeDtypeStruct((rows, 2 * FF), F32),
         in_specs=[PLACE_SPEC] + [block] * 4,
         out_specs=pl.BlockSpec((tile, 2 * FF), lambda i: (i, 0)),
-        compiler_params=pltpu.CompilerParams(vmem_limit_bytes=32 * 2**20),
+        compiler_params=pltpu.CompilerParams(vmem_limit_bytes=56 * 2**20),
     )(place, *pieces)
 
 
-def in_kernel(place_ref, a, b, c, d, dt_ref, in_ref, qkv_ref):
+def in_kernel(place_ref, a, b, c, d, in_ref, qkv_ref):
     found = chosen(place_ref, (a, b, c, d))
     for rank in range(RANKS):
         left, right = (found[rank % 2][side][rank // 2].astype(F32) for side in range(2))
@@ -484,10 +485,27 @@
         qkv_ref[:, R_ATT * rank : R_ATT * (rank + 1)] = right[:, R_SSM:]
         start = ATT + KV * (rank % 2) + HEAD_DIM * (rank // 2)
         qkv_ref[:, start : start + HEAD_DIM] = left[:, R_CONV:]
-    in_ref[D_SSM + CONV_W :] = dt_ref[...]
-
-
-def spread_in(place, pieces, dt):
+
+
+def dt_kernel(whole_ref, dt_ref, out_ref):
+    out_ref[...] = dt_ref[...]
+
+
+def with_dt(whole, dt):
+    rows, width = dt.shape
+    tile = 16
+    first = (whole.shape[0] - rows) // tile
+    return pl.pallas_call(
+        dt_kernel,
+        grid=(rows // tile,),
+        out_shape=jax.ShapeDtypeStruct(whole.shape, whole.dtype),
+        in_specs=[ANY_SPEC, pl.BlockSpec((tile, width), lambda i: (i, 0))],
+        out_specs=pl.BlockSpec((tile, width), lambda i: (first + i, 0)),
+        input_output_aliases={0: 0},
+    )(whole, dt)
+
+
+def spread_in(place, pieces):
     rows = pieces[0].shape[1]
     tile = min(rows, 128)
     block = pl.BlockSpec((2, tile, HALF), lambda i: (0, i, 0))
@@ -498,15 +516,251 @@
             jax.ShapeDtypeStruct((D_IN, rows), F32),
             jax.ShapeDtypeStruct((rows, ATT + 2 * KV), F32),
         ],
-        in_specs=[PLACE_SPEC]
-        + [block] * 4
-        + [pl.BlockSpec((SSM_HEADS, tile), lambda i: (0, i))],
+        in_specs=[PLACE_SPEC] + [block] * 4,
         out_specs=[
             pl.BlockSpec((D_IN, tile), lambda i: (0, i)),
             pl.BlockSpec((tile, ATT + 2 * KV), lambda i: (i, 0)),
         ],
-        compiler_params=pltpu.CompilerParams(vmem_limit_bytes=40 * 2**20),
-    )(place, *pieces, dt)
+        compiler_params=pltpu.CompilerParams(vmem_limit_bytes=56 * 2**20),
+    )(place, *pieces)
+
+
+LANES = 128
+
+
+def turned_lanes(values, cosine, sine):
+    parts = []
+    for start in range(0, values.shape[1], HEAD_DIM):
+        head = values[:, start : start + HEAD_DIM]
+        parts.append(head * cosine + pltpu.roll(head, HEAD_DIM // 2, 1) * sine)
+    return parts[0] if len(parts) == 1 else jnp.concatenate(parts, axis=1)
+
+
+def exact(left, right, contract):
+    return lax.dot_general(
+        left, right, (contract, ((), ())), precision=HIGHEST, preferred_element_type=F32
+    )
+
+
+def mixer_back_kernel(
+    nz, got_ref, scan_ref, z_ref, norm_ref, gain_ref, x_ref, b_ref, c_ref, raw_ref, heads_ref,
+    run_ref, dt_ref, q_ref, k_ref, v_ref, probs_ref, cos_ref, sin_ref,
+    message_ref, right_ref, dx_ref, draw_ref, heads_out_ref, lanes_out_ref,
+):
+    length = scan_ref.shape[0]
+    inner = nz // RANKS
+    wide, narrow_w = R_OUT // nz, R_SSM // nz
+    d_norm = jnp.concatenate(
+        [
+            got_ref[r][:, wide * i : wide * i + narrow_w].astype(F32)
+            for i in range(inner)
+            for r in range(RANKS)
+        ],
+        axis=1,
+    )
+    d_o = jnp.concatenate(
+        [
+            got_ref[r][:, wide * i + narrow_w : wide * (i + 1)].astype(F32)
+            for i in range(inner)
+            for r in range(RANKS)
+        ],
+        axis=1,
+    ).astype(BF)
+    spread_of, overlap = norm_ref[:, 0:1], norm_ref[:, 1:2]
+    scan, z = scan_ref[...], z_ref[...]
+    sig = jax.nn.sigmoid(z)
+    silu = z * sig
+    gated = scan * silu
+    lanes_out_ref[0:1, :] = jnp.sum(d_norm * gated * spread_of, axis=0, keepdims=True)
+    d_gated = spread_of * d_norm * gain_ref[...] - gated * (
+        spread_of * spread_of * overlap * (1.0 / D_SSM)
+    )
+    d_scan = d_gated * silu
+    right_ref[:, :R_SSM] = (d_gated * scan * (sig * (1.0 + z * (1.0 - sig)))).astype(BF)
+
+    row = lax.broadcasted_iota(jnp.int32, (length, length), 0)
+    column = lax.broadcasted_iota(jnp.int32, (length, length), 1)
+    allowed = row >= column
+
+    scale = HEAD_DIM**-0.5
+    key, value = k_ref[...], v_ref[...]
+    d_key = jnp.zeros((length, HEAD_DIM), F32)
+    d_value = jnp.zeros((length, HEAD_DIM), F32)
+    for head in range(R_ATT // HEAD_DIM):
+        cut = slice(HEAD_DIM * head, HEAD_DIM * (head + 1))
+        query, grad, probs = q_ref[:, cut], d_o[:, cut], probs_ref[head]
+        d_probs = dot_t(grad, value)
+        d_scores = (
+            probs * (d_probs - jnp.sum(probs * d_probs, axis=1, keepdims=True))
+        ).astype(BF)
+        d_query = dot(d_scores, key) * scale
+        right_ref[:, R_SSM + HEAD_DIM * head : R_SSM + HEAD_DIM * (head + 1)] = turned_lanes(
+            d_query, cos_ref[...], -sin_ref[...]
+        ).astype(BF)
+        d_key = d_key + t_dot(d_scores, query) * scale
+        d_value = d_value + t_dot(probs.astype(BF), grad)
+
+    b_rows, c_rows = b_ref[...], c_ref[...]
+    mixing = dot_t(c_rows, b_rows)
+    x = x_ref[...]
+    lanes_out_ref[1:2, :] = jnp.sum(d_scan * x.astype(F32), axis=0, keepdims=True)
+    grad_b = d_scan.astype(BF)
+    run_t, dt_t = run_ref[...].T, dt_ref[...].T
+    d_mixing = jnp.zeros((length, length), F32)
+    lane = lax.broadcasted_iota(jnp.int32, (length, LANES), 1)
+    head_row = lax.broadcasted_iota(jnp.int32, (LANES, length), 0)
+    by_row = jnp.zeros((length, LANES), F32)
+    direct = jnp.zeros((LANES, length), F32)
+    for pair in range(R_HEADS // 2):
+        cut = slice(LANES * pair, LANES * (pair + 1))
+        x_pair, g_pair = x[:, cut], grad_b[:, cut]
+        d_pair = []
+        for side in range(2):
+            head = 2 * pair + side
+            mine = (lane < SSM_HEAD) if side == 0 else (lane >= SSM_HEAD)
+            d_weights = dot_t(jnp.where(mine, g_pair, jnp.zeros_like(g_pair)), x_pair)
+            gap = run_ref[:, head : head + 1] - run_t[head : head + 1, :]
+            table = jnp.exp(jnp.where(allowed, gap, NEGATIVE))
+            dt_row = dt_t[head : head + 1, :]
+            faded = d_weights * table
+            faded_dt = faded * dt_row
+            d_mixing = d_mixing + faded_dt
+            plain = faded * mixing
+            direct = jnp.where(head_row == head, jnp.sum(plain, axis=0, keepdims=True), direct)
+            by_row = jnp.where(
+                lane == head, jnp.sum(faded_dt * mixing, axis=1, keepdims=True), by_row
+            )
+            weights = (table * mixing * dt_row).astype(BF)
+            d_pair.append(t_dot(weights, g_pair))
+        skip = jnp.where(
+            lane[:1] < SSM_HEAD,
+            heads_ref[2:3, 2 * pair : 2 * pair + 1],
+            heads_ref[2:3, 2 * pair + 1 : 2 * pair + 2],
+        )
+        dx_ref[:, cut] = jnp.where(lane < SSM_HEAD, d_pair[0], d_pair[1]) + skip * d_scan[:, cut]
+    d_mixing = d_mixing.astype(BF)
+    d_c = dot(d_mixing, b_rows)
+    d_b = t_dot(d_mixing, c_rows)
+    for r in range(RANKS):
+        source = d_b if r < 2 else d_c
+        start = R_BC * (r % 2)
+        message_ref[r, :, :R_BC] = source[:, start : start + R_BC].astype(BF)
+        message_ref[r, :, R_BC:] = (d_key if r % 2 == 0 else d_value).astype(BF)
+
+    later = (column >= row).astype(F32)
+    from_rows_sum = exact(later, by_row, ((1,), (0,)))
+    grad_step = from_rows_sum - exact(later, direct * dt_t, ((1,), (1,)))
+    grad_dt = direct.T
+    bias, log = heads_ref[0:1, :], heads_ref[1:2, :]
+    raw = raw_ref[...] + bias
+    rate = jnp.exp(log)
+    step = -jax.nn.softplus(raw) * rate
+    valid = lane < R_HEADS
+    grad_dt = grad_dt - grad_step * rate
+    grad_raw = jnp.where(valid, grad_dt * jax.nn.sigmoid(raw), 0.0)
+    draw_ref[...] = grad_raw.astype(BF)
+    heads_out_ref[0:1, :] = jnp.sum(grad_raw, axis=0, keepdims=True)
+    heads_out_ref[1:2, :] = jnp.sum(grad_step * step, axis=0, keepdims=True)
+
+
+def whole_block(array):
+    shape = array.shape
+    return pl.BlockSpec(shape, lambda i: (0,) * len(shape), pipeline_mode=pl.Buffered(1))
+
+
+def mixer_back(got, kept, small, overlap, tables):
+    length = got.shape[1]
+    nz = lax.axis_size("fsdp")
+    norm = jnp.stack([kept["spread"], overlap], axis=1)
+    shape = jax.ShapeDtypeStruct
+    out_shape = [
+        shape((RANKS, length, 2 * R_BC), BF),
+        shape((length, HALF), BF),
+        shape((length, R_SSM), F32),
+        shape((length, LANES), BF),
+        shape((8, LANES), F32),
+        shape((8, R_SSM), F32),
+    ]
+    args = (
+        got, kept["scan"], kept["z"], norm, small["ssm_gain"][None], kept["u"][:, :R_SSM],
+        kept["b"], kept["c"], kept["dt_raw"], small["heads"], kept["running"], kept["dt"],
+        kept["query"], kept["key"], kept["value"],
+        kept["probs"], *tables,
+    )
+    return pl.pallas_call(
+        functools.partial(mixer_back_kernel, nz),
+        grid=(1,),
+        out_shape=out_shape,
+        in_specs=[whole_block(arg) for arg in args],
+        out_specs=[whole_block(out) for out in out_shape],
+        cost_estimate=lasting(16),
+        compiler_params=pltpu.CompilerParams(vmem_limit_bytes=56 * 2**20),
+    )(*args)
+
+
+def conv_back_kernel(
+    place_ref, back_ref, dx_ref, xbc_ref, table_ref, cos_ref, sin_ref, left_ref, conv_ref
+):
+    y, s = place_ref[0], place_ref[1]
+    length = dx_ref.shape[0]
+    back = [back_ref[r].astype(F32) for r in range(RANKS)]
+    d_bc = (back[0] + back[1] + back[2] + back[3])[:, :R_BC]
+    d_kv = jnp.where(s == 0, back[0] + back[1], back[2] + back[3])[:, R_BC:]
+    d_kv = jnp.where(y == 0, turned_lanes(d_kv, cos_ref[...], -sin_ref[...]), d_kv)
+    left_ref[:, R_CONV:] = d_kv.astype(BF)
+    d_u = jnp.concatenate([dx_ref[...], d_bc], axis=1)
+    wide = xbc_ref[...].astype(F32)
+    place = lax.broadcasted_iota(jnp.int32, (length, R_CONV), 0)
+    moved = []
+    before = table_ref[CONV_K : CONV_K + 1, :] + jnp.zeros_like(wide)
+    for tap in range(CONV_K):
+        steps = CONV_K - 1 - tap
+        value = wide
+        if steps:
+            value = jnp.where(place >= steps, pltpu.roll(wide, steps, 0), 0.0)
+        moved.append(value)
+        before = before + table_ref[tap : tap + 1, :] * value
+    sig = jax.nn.sigmoid(before)
+    d_before = d_u * (sig * (1.0 + before * (1.0 - sig)))
+    d_xbc = jnp.zeros_like(wide)
+    for tap in range(CONV_K):
+        conv_ref[tap : tap + 1, :] = jnp.sum(d_before * moved[tap], axis=0, keepdims=True)
+        steps = CONV_K - 1 - tap
+        value = d_before
+        if steps:
+            value = jnp.where(
+                place < length - steps, pltpu.roll(d_before, length - steps, 0), 0.0
+            )
+        d_xbc = d_xbc + table_ref[tap : tap + 1, :] * value
+    conv_ref[CONV_K : CONV_K + 1, :] = jnp.sum(d_before, axis=0, keepdims=True)
+    left_ref[:, :R_CONV] = d_xbc.astype(BF)
+
+
+def conv_back(back, d_x, xbc, table, tables):
+    length = d_x.shape[0]
+    place = jnp.stack([lax.axis_index("y"), lax.axis_index("section")]).astype(jnp.int32)
+    args = (back, d_x, xbc, table, *tables)
+    out_shape = [
+        jax.ShapeDtypeStruct((length, HALF), BF),
+        jax.ShapeDtypeStruct((8, R_CONV), F32),
+    ]
+    return pl.pallas_call(
+        conv_back_kernel,
+        grid=(1,),
+        out_shape=out_shape,
+        in_specs=[PLACE_SPEC] + [whole_block(arg) for arg in args],
+        out_specs=[whole_block(out) for out in out_shape],
+        cost_estimate=lasting(7),
+        compiler_params=pltpu.CompilerParams(vmem_limit_bytes=56 * 2**20),
+    )(place, *args)
+
+
+def rotation_tables(length):
+    half = HEAD_DIM // 2
+    frequency = ROPE_BASE ** (-jnp.arange(half, dtype=F32) / half)
+    angles = jnp.arange(length, dtype=F32)[:, None] * frequency[None, :]
+    cosine, sine = jnp.cos(angles), jnp.sin(angles)
+    return jnp.concatenate([cosine, cosine], 1), jnp.concatenate([-sine, sine], 1)
 
 
 def narrow(values):
@@ -595,10 +849,11 @@
 def scan_forward(x, b_rows, c_rows, dt_raw, heads):
     dt, _, running = decays(dt_raw, heads)
     mixing = dot_t(c_rows, b_rows)
-    weights = narrow(decay_table(running) * mixing[None] * dt.T[:, None, :])
+    weights = narrow(decay_table(running[:, :R_HEADS]) * mixing[None] * dt.T[:R_HEADS, None, :])
     x_heads = by_head(x)
     result = jnp.einsum("hts,shp->thp", weights, x_heads, preferred_element_type=F32)
-    return (result + heads[2][None, :, None] * x_heads.astype(F32)).reshape(x.shape)
+    result = result + heads[2][None, :R_HEADS, None] * x_heads.astype(F32)
+    return result.reshape(x.shape), running, dt
 
 
 def scan_backward(x, b_rows, c_rows, dt_raw, heads, grad_y):
@@ -667,7 +922,7 @@
     x1 = narrow(rms(entering.astype(F32), small["gain0"][None, :]))
     left = dot(x1, weights["in"][0])
     right = dot(x1, weights["in"][1])
-    dt_raw = columns(dot(x1, weights["dt"]), R_HEADS * (2 * s + y), R_HEADS)
+    dt_raw = dot(x1, weights["dt"])
     xbc = narrow(left[:, :R_CONV])
     u = narrow(jax.nn.silu(conv_sum(xbc, small["conv"])))
     kv_raw = left[:, R_CONV:]
@@ -681,7 +936,7 @@
     query = narrow(rotary(right[:, R_SSM:], 1.0))
     o, probs = attend(query, key, value)
     x = u[:, :R_SSM]
-    scan = scan_forward(x, b_rows, c_rows, dt_raw, small["heads"])
+    scan, running, dt = scan_forward(x, b_rows, c_rows, dt_raw, small["heads"])
     gated = scan * jax.nn.silu(z)
     squares = jnp.sum(gated * gated, axis=1)
     scaled = narrow(gated * small["ssm_gain"][None, :])
@@ -702,7 +957,7 @@
     kept = dict(
         resid=resid, x1=x1, xbc=xbc, u=u, b=b_rows, c=c_rows, key=key, value=value, query=query,
         probs=probs, z=z, dt_raw=dt_raw, scan=scan, spread=spread_of, mo=mo, mid=mid, x2=x2,
-        gate=gate, up=up, act=act,
+        gate=gate, up=up, act=act, running=running, dt=dt,
     )
     return leaving, kept
 
@@ -727,7 +982,7 @@
     return a, b
 
 
-def layer_backward(grad, given, kept, weights, small, queue, layer, first=()):
+def layer_backward(grad, given, kept, weights, small, queue, layer, tables, first=()):
     s, y = lax.axis_index("section"), lax.axis_index("y")
     core = lax.axis_index("core")
     length = grad.shape[0]
@@ -751,9 +1006,9 @@
 
     halves = lambda v: (v[:, :HALF], v[:, HALF:])
     g0, g1 = halves(grad)
-    down_block = product(kept["act"], (g0, g1))
+    down_block = functools.partial(product, kept["act"], (g0, g1))
     if layer == 1:
-        reduce("down1", down_block)
+        reduce("down1", down_block())
     grad_act = dot_t(g0, down[0]) + dot_t(g1, down[1])
     gate, up = kept["gate"], kept["up"]
     sig = jax.nn.sigmoid(gate)
@@ -765,6 +1020,8 @@
     d_mid, db, grad_gain1 = back_step(
         narrow(part), given, kept["mid"], small["gain1"], due("mlp") + list(first)
     )
+    if layer == 0:
+        reduce("gu0", product(kept["x2"], (d_gate, d_up), db))
     b0, b1 = halves(db)
     d_mo = dot_t(b0, out[0]) + dot_t(b1, out[1])
     mo = kept["mo"]
@@ -773,78 +1030,34 @@
     stat = jnp.broadcast_to(stat_row[None, :], (8, length))
     blocks = jnp.transpose(narrow(d_mo).reshape(length, RANKS, R_OUT // RANKS), (1, 0, 2))
     got, stats = swap(blocks, stat, due("norm"))
-    overlap = jnp.sum(stats[:, 0, :], axis=0)[:, None]
-    if layer == 0:
-        reduce("gu0", product(kept["x2"], (d_gate, d_up), got))
-    else:
-        reduce("out1", product(kept["mo"], (b0, b1), got))
-    d_norm, d_o = from_rows(got)
-    d_norm = d_norm.astype(F32)
-    spread_of = kept["spread"][:, None]
-    scan, z = kept["scan"], kept["z"]
-    sig_z = jax.nn.sigmoid(z)
-    silu_z = z * sig_z
-    gated = scan * silu_z
-    grad_ssm_gain = jnp.sum(d_norm * gated * spread_of, axis=0)
-    d_gated = spread_of * d_norm * small["ssm_gain"][None, :] - gated * (
-        spread_of * spread_of * overlap * (1.0 / D_SSM)
-    )
-    d_scan = d_gated * silu_z
-    d_z = d_gated * scan * (sig_z * (1.0 + z * (1.0 - sig_z)))
-    d_query, d_key, d_value = attend_back(
-        kept["query"], kept["key"], kept["value"], kept["probs"], d_o
-    )
-    u = kept["u"]
-    d_x, d_b, d_c, d_dt, grad_heads = scan_backward(
-        u[:, :R_SSM], kept["b"], kept["c"], kept["dt_raw"], small["heads"], d_scan
-    )
-    message = jnp.stack(
-        [
-            jnp.concatenate([d_b[:, :R_BC], d_key], axis=1),
-            jnp.concatenate([d_b[:, R_BC:], d_value], axis=1),
-            jnp.concatenate([d_c[:, :R_BC], d_key], axis=1),
-            jnp.concatenate([d_c[:, R_BC:], d_value], axis=1),
-        ]
-    )
-    back = swap(narrow(message), None, due("scan"))
-    back = back.astype(F32)
-    d_bc = back[0, :, :R_BC] + back[1, :, :R_BC] + back[2, :, :R_BC] + back[3, :, :R_BC]
-    d_kv = jnp.sum(lax.dynamic_slice_in_dim(back, 2 * s, 2, axis=0)[:, :, R_BC:], axis=0)
-    d_kv = jnp.where(y == 0, rotary(d_kv, -1.0), d_kv)
-    d_u = jnp.concatenate([d_x, d_bc], axis=1)
-    xbc = kept["xbc"]
-    table = small["conv"]
-    before = conv_sum(xbc, table)
-    sig_c = jax.nn.sigmoid(before)
-    d_before = d_u * (sig_c * (1.0 + before * (1.0 - sig_c)))
-    wide = xbc.astype(F32)
-    grad_conv = jnp.stack(
-        [jnp.sum(d_before * shifted(wide, CONV_K - 1 - tap), axis=0) for tap in range(CONV_K)]
-        + [jnp.sum(d_before, axis=0)]
-    )
-    d_xbc = 0.0
-    for tap in range(CONV_K):
-        d_xbc = d_xbc + table[tap][None, :] * shifted(d_before, tap - CONV_K + 1)
-    d_left = narrow(jnp.concatenate([d_xbc, d_kv], axis=1))
-    d_right = narrow(jnp.concatenate([d_z, rotary(d_query, -1.0)], axis=1))
-    d_dt_b = narrow(d_dt)
-    dt_own = columns(weights["dt"], R_HEADS * (2 * s + y), R_HEADS)
-    reduce(f"in{layer}", product(kept["x1"], (d_left, d_right)))
-    part = dot_t(d_left, win[0]) + dot_t(d_right, win[1]) + dot_t(d_dt_b, dt_own)
-    got_gu = None
-    if layer == 0:
-        got_gu = share(queue["gu1"], queue["gu0"], 50)
+    overlap = jnp.sum(stats[:, 0, :], axis=0)
+    message, d_right, d_x, d_raw, head_sums, lane_sums = mixer_back(
+        got, kept, small, overlap, tables
+    )
+    skip = jnp.sum(lane_sums[1].reshape(R_HEADS, SSM_HEAD), axis=1)
+    grad_heads = jnp.concatenate([head_sums[:2, :R_HEADS], skip[None]], axis=0)
+    grad_ssm_gain = lane_sums[0]
+    if layer == 1:
+        reduce("out1", product(kept["mo"], (b0, b1), message))
+    back = swap(message, None, due("scan"))
+    d_left, grad_conv = conv_back(back, d_x, kept["xbc"], small["conv"], tables)
+    grad_conv = grad_conv[: CONV_K + 1]
+    part = dot_t(d_left, win[0]) + dot_t(d_right, win[1]) + dot_t(d_raw, weights["dt"])
+    part = narrow(part)
+    reduce(f"in{layer}", product(kept["x1"], (d_left, d_right), part))
     _, entering_grad, grad_gain0 = back_step(
-        narrow(part),
+        part,
         d_mid,
         kept["resid"].astype(F32),
         small["gain0"],
-        due("in") + list(got_gu or ())[:1],
-    )
+        due("in"),
+    )
+    got_gu = None
     if layer == 0:
+        got_gu = share(queue["gu1"], queue["gu0"], 50, (entering_grad,))
         reduce("out0", product(kept["mo"], (b0, b1), got_gu[0]))
     two = lambda v: jnp.concatenate([v, flip(v, "core")], axis=0)
-    grad_dt_w = t_dot(two(jnp.pad(d_dt_b, ((0, 0), (0, 4)))), two(kept["x1"]))
+    grad_dt_w = t_dot(two(d_raw[:, :16]), two(kept["x1"]))
     smalls_grad = dict(
         heads=grad_heads, conv=grad_conv, ssm=grad_ssm_gain[None], dt=grad_dt_w,
         gains=jnp.concatenate([grad_gain0, grad_gain1], axis=0),
@@ -903,12 +1116,15 @@
         small = dict(
             gain0=gains[0],
             gain1=gains[1],
-            heads=columns(heads, R_HEADS * rank, R_HEADS),
+            heads=jnp.pad(
+                columns(heads, R_HEADS * rank, R_HEADS), ((0, 0), (0, LANES - R_HEADS))
+            ),
             conv=conv_own,
             ssm_gain=lax.dynamic_slice_in_dim(gain, R_SSM * rank, R_SSM),
             is_ssm=channel < R_SSM // nz,
         )
-        return small, part[:, starts[4] :].reshape(D, SSM_HEADS)
+        dt_w = columns(part[:, starts[4] :].reshape(D, SSM_HEADS), R_HEADS * rank, R_HEADS)
+        return small, jnp.pad(dt_w, ((0, 0), (0, LANES - R_HEADS)))
 
     def pieces(section):
         rk = 2 * section + y
@@ -1020,6 +1236,7 @@
         )
         outs.append(hidden)
         kept.append(keep)
+    tables = rotation_tables(length)
     grads = [None, None]
     smalls_grad, queue = [None, None], {}
     for layer in (1, 0):
@@ -1031,6 +1248,7 @@
             smalls[layer],
             queue,
             layer,
+            tables,
             (outs[1],) if layer == 1 else (),
         )
         grads[layer] = grad
@@ -1073,16 +1291,18 @@
     down_rows = R_FF // nz
     extra = jnp.concatenate([dt_rows, packed], axis=1)
     extra_count = extra.shape[1]
+    got_in = share(queue["in1"], queue["in0"], 50)
+    down_block = down_block(got_in[0])
     last = jnp.concatenate([down_block.reshape(nz, down_rows, HALF), narrow(extra)], axis=1)
     reduce("down0", last.reshape(-1, HALF))
     down0, extra = queue["down0"][:down_rows], queue["down0"][down_rows:]
 
     place = jnp.stack([y, core]).astype(jnp.int32)
     grad_w_gu = spread_gate_up(place, got_gu, nz)
-    got_in = share(queue["in1"], queue["in0"], 50)
     got_out = share(queue["out1"], queue["out0"], 30, (got_in[0],))
     shared = swap(extra).astype(F32)
-    got_down = share(queue["down1"], down0, 30)
+    grad_w_in, grad_w_qkv = spread_in(place, got_in)
+    got_down = share(queue["down1"], down0, 30, (grad_w_in,))
     out_rows, o_rows = R_SSM // nz, R_ATT // nz
     grad_w_out = spread_rows(place, got_out, 0, out_rows, o_rows)
     grad_w_o = spread_rows(place, got_out, out_rows, o_rows, o_rows)
@@ -1090,8 +1310,7 @@
 
     width = D // nz
     dt_all = jnp.where(s == 0, shared[:, :12, :width], shared[:, :12, width : 2 * width])
-    grad_w_in, grad_w_qkv = spread_in(place, got_in, dt_all.reshape(SSM_HEADS, width))
-    grad_w_in = grad_w_in.T
+    grad_w_in = with_dt(grad_w_in, dt_all.reshape(SSM_HEADS, width)).T
     small_sum = jnp.sum(shared[:, 16:], axis=0).reshape(-1)[:amount].reshape(2, -1)
     small_sum = jnp.where(s == 0, small_sum[0], small_sum[1])
     cuts, at = [], 0

time: 1200 us -> 1180 us (0.983)
  Pallas kernels: 551 us -> 590 us
  matrix products: 125 us -> 95.6 us
  other arithmetic: 79.5 us -> 56.3 us
  local copies, waits for them, and re-layouts: 131 us -> 109 us
    pallas_call x0 -> x5, Pallas kernels: none -> 26.6 us  [the longest x2 14.7 us: mixer_back(): pl.pallas_call(functools.partial(mixer_back_kernel, nz), grid=(1,), out_s...]
    dot_general x14 -> x0, matrix products: 24.4 us -> none  [the longest x2 7.18 us: scan_backward(): jnp.einsum('thp,shp->hts', grad_heads, x_heads, preferred_element_type=F32)]
    reduce_sum x10 -> x4, other arithmetic: 12.6 us -> 0.27 us  [the longest x2 0.23 us: layer_backward(): skip = jnp.sum(lane_sums[1].reshape(R_HEADS, SSM_HEAD), axis=1)]
    unnamed x459 -> x323, local copies, waits for them, and re-layouts: 37.5 us -> 28.7 us
    dot_general x20 -> x18, matrix products: 43.9 us -> 39 us  [dot(): return jnp.dot(left, right, preferred_element_type=F32)]
  transfers between devices with their start and end apart: 46 -> 46, of which waited for: 16 -> 13; matrix products, arithmetic and copies ran while one was open for 24% -> 19% of each run, Pallas kernels for 42% -> 47%
where the time goes in v3:
time: 1180 us; the launch traced here: 1170 us
  Pallas kernels  590 us (50%)
  waiting for transfers between devices  245 us (21%)
  local copies, waits for them, and re-layouts  109 us (9%)
  matrix products  95.6 us (8%)
  other arithmetic  56.3 us (5%)
  blocking collectives  35.1 us (3%)
  between operations  17.7 us (2%)
  starting transfers between devices  16.1 us (1%)
    pallas_call x8, Pallas kernels, rank_call(): pl.pallas_call(ignoring(kernel, len(args), len(after)), out_shape=out_sha...  225 us
    all_gather x8, waiting for transfers between devices, gather(): order.append(lax.all_gather(in_turn(piece), ('core', 'fsdp'), axis=0))  178 us
    pallas_call x4, Pallas kernels, share(): pl.pallas_call(ignoring(share_kernel, 2, len(after)), out_shape=[shape] *...  156 us
    pallas_call x9, Pallas kernels, swap(): pl.pallas_call(ignoring(functools.partial(swap_kernel, stat is not None),...  83.2 us
    pallas_call x8, Pallas kernels, outer_sum(): pl.pallas_call(ignoring(product_kernel, 4, len(tokens)), grid=(width // t...  52.3 us
    dot_general x20, matrix products, dot_t(): lax.dot_general(left, right, (((1,), (1,)), ((), ())), preferred_element_...  45 us
    ppermute x24, waiting for transfers between devices, flip(): return lax.ppermute(value, axis, [(0, 1), (1, 0)])  45 us
    dot_general x18, matrix products, dot(): return jnp.dot(left, right, preferred_element_type=F32)  39 us
  transfers between devices with their start and end apart: 46, of which 13 were waited for; matrix products, arithmetic and copies ran while one was open for 19% of the time, Pallas kernels for 47%

profile of v3, /device:TPU:0, one launch (start us, length us, event | category | flops | bytes accessed | tf_op | source)
XLA Modules:
  0.0 1165.1 jit_solution(15714241945925819497)
XLA Ops:
  20.4 35.1 %all_gather.51 = bf16[8,256,128]{2,1,0:T(8,128)(2,1)S(1)} all-gather(bf16[1,256,128]{2,1,0:T(8,128)(2,1)S(1)} %pad_bitcast_fusion), channel_id=1, replica_groups=mesh['section'=2,'y'=2,'core'=2,'fsdp'=4] {'section','fsdp'}, dimensions={0}, use_global_device_ids=true | all-gather | bytes 589824 | tf_op jit(solution)/shard_map/all_gather | solution.py:1100
  84.2 68.7 %all-gather.19.cloned.1.call-done = bf16[4096,1024]{1,0:T(8,128)(2,1)} async-done(((bf16[512,1024]{1,0:T(8,128)(2,1)}), bf16[4096,1024]{1,0:T(8,128)(2,1)}) %all-gather.19.cloned.1.call-update) | async-done | bytes 8388624 | tf_op jit(solution)/shard_map/all_gather | solution.py:1171
  156.3 35.0 %collective-permute-done.5 = bf16[768,1024]{1,0:T(8,128)(2,1)S(1)} collective-permute-done((bf16[768,1024]{1,0:T(8,128)(2,1)S(1)}, bf16[768,1024]{1,0:T(8,128)(2,1)S(1)}, u32[]{:S(2)}, u32[]{:S(2)}) %collective-permute-start.5) | collective-permute-done | bytes 1572896 | tf_op jit(solution)/shard_map/ppermute | solution.py:916
  248.2 9.8 shard_map.212
  286.1 27.3 %shard_map.215 = (f32[64,2048]{1,0:T(8,128)S(1)}, bf16[256,2048]{1,0:T(8,128)(2,1)S(1)}) custom-call(bf16[256,2048]{1,0:T(8,128)(2,1)S(1)} %pad_maximum_fusion.5.part_ref, bf16[64,2048]{1,0:T(8,128)(2,1)S(1)} %get-tuple-element.234.resid_ref, f32[1,2048]{1,0:T(1,128)S(1)} %bitcast.407), custom_call_target="tpu_custom_call" | custom-call | bytes 22950000 | tf_op jit(solution)/shard_map/pallas_call | solution.py:236
  321.5 9.8 all-gather.25.cloned.1.call-done
  335.0 28.3 %shard_map.216 = bf16[256,2048]{1,0:T(8,128)(2,1)S(1)} custom-call(bf16[256,2048]{1,0:T(8,128)(2,1)S(1)} %pad_maximum_fusion.6.part_ref, f32[64,2048]{1,0:T(8,128)S(1)} %get-tuple-element.97.resid_ref.refs_2_), custom_call_target="tpu_custom_call" | custom-call | bytes 22950000 | tf_op jit(solution)/shard_map/pallas_call | solution.py:236
  363.9 50.2 %all-gather.27.cloned.1.call-done = bf16[4096,1024]{1,0:T(8,128)(2,1)} async-done(((bf16[512,1024]{1,0:T(8,128)(2,1)}), bf16[4096,1024]{1,0:T(8,128)(2,1)}) %all-gather.27.cloned.1.call-update) | async-done | bytes 8388624 | tf_op jit(solution)/shard_map/all_gather | solution.py:1171
  463.4 27.5 %shard_map.219 = (f32[64,2048]{1,0:T(8,128)S(1)}, bf16[256,2048]{1,0:T(8,128)(2,1)}) custom-call(bf16[256,2048]{1,0:T(8,128)(2,1)S(1)} %pad_maximum_fusion.7.part_ref, bf16[64,2048]{1,0:T(8,128)(2,1)S(1)} %get-tuple-element.241.resid_ref, f32[1,2048]{1,0:T(1,128)S(1)} %bitcast.409), custom_call_target="tpu_custom_call" | custom-call | bytes 22950000 | tf_op jit(solution)/shard_map/pallas_call | solution.py:236
  513.0 30.7 %all-gather.31.cloned.1.call-done = bf16[2048,1024]{1,0:T(8,128)(2,1)} async-done(((bf16[256,1024]{1,0:T(8,128)(2,1)}), bf16[2048,1024]{1,0:T(8,128)(2,1)}) %all-gather.31.cloned.1.call-update) | async-done | bytes 4194320 | tf_op jit(solution)/shard_map/all_gather | solution.py:1171
  551.5 28.2 %shard_map.220.refs_4_ = bf16[256,2048]{1,0:T(8,128)(2,1)S(1)} custom-call(bf16[256,2048]{1,0:T(8,128)(2,1)S(1)} %pad_maximum_fusion.8.part_ref, f32[64,2048]{1,0:T(8,128)S(1)} %get-tuple-element.104.resid_ref.refs_2_), custom_call_target="tpu_custom_call" | custom-call | bytes 22950000 | tf_op jit(solution)/shard_map/pallas_call | solution.py:236
  608.3 26.5 %shard_map.221 = (f32[64,2048]{1,0:T(8,128)S(1)}, bf16[256,2048]{1,0:T(8,128)(2,1)S(1)}, f32[1,2048]{1,0:T(1,128)S(1)}) custom-call(bf16[256,2048]{1,0:T(8,128)(2,1)S(1)} %fusion.46.refs_0_, f32[64,2048]{1,0:T(8,128)S(1)} %dynamic-slice_convert_fusion.1.refs_1_, f32[64,2048]{1,0:T(8,128)S(1)} %get-tuple-element.104.resid_ref.refs_2_, ...), custom_call_target="tpu_custom_call" | custom-call | bytes 22950000 | tf_op jit(solution)/shard_map/pallas_call | solution.py:236
  645.5 10.6 shard_map.223
  718.9 29.9 %shard_map.228 = (f32[64,2048]{1,0:T(8,128)}, bf16[256,2048]{1,0:T(8,128)(2,1)S(1)}, f32[1,2048]{1,0:T(1,128)S(1)}) custom-call(bf16[256,2048]{1,0:T(8,128)(2,1)S(1)} %copy-done.4, f32[64,2048]{1,0:T(8,128)S(1)} %copy-done.26, f32[64,2048]{1,0:T(8,128)S(1)} %copy-done.20, f32[1,2048]{1,0:T(1,128)S(1)} %bitcast.412, bf16[512,1024]{1,0:T(8,128)(2,1)S(1)} %copy-done.8), custom_call_target="tpu_custom_call" | custom-call | bytes 22950000 | tf_op jit(solution)/shard_map/pallas_call | solution.py:236
  757.5 27.5 %shard_map.230 = (f32[64,2048]{1,0:T(8,128)S(1)}, bf16[256,2048]{1,0:T(8,128)(2,1)S(1)}, f32[1,2048]{1,0:T(1,128)S(1)}) custom-call(bf16[256,2048]{1,0:T(8,128)(2,1)S(1)} %fusion.49.refs_0_, f32[64,2048]{1,0:T(8,128)S(1)} %dynamic-slice_convert_fusion.refs_1_, f32[64,2048]{1,0:T(8,128)S(1)} %copy-done.13, f32[1,2048]{1,0:T(1,128)S(1)} %bitcast.408, ...), custom_call_target="tpu_custom_call" | custom-call | bytes 22950000 | tf_op jit(solution)/shard_map/pallas_call | solution.py:236
  808.6 10.5 shard_map.231
  863.5 11.0 reduce-scatter.17.cloned.1.call-done.refs_1_
  888.1 29.6 %shard_map.236 = (f32[64,2048]{1,0:T(8,128)}, bf16[256,2048]{1,0:T(8,128)(2,1)S(1)}, f32[1,2048]{1,0:T(1,128)S(1)}) custom-call(bf16[256,2048]{1,0:T(8,128)(2,1)S(1)} %copy-done.5, f32[64,2048]{1,0:T(8,128)S(1)} %copy-done.24, f32[64,2048]{1,0:T(8,128)S(1)} %copy-done.19, f32[1,2048]{1,0:T(1,128)S(1)} %bitcast.411), custom_call_target="tpu_custom_call" | custom-call | bytes 22950000 | tf_op jit(solution)/shard_map/pallas_call | solution.py:236
  918.6 50.2 %shard_map.241 = (bf16[2,512,1024]{2,1,0:T(8,128)(2,1)}, bf16[2,512,1024]{2,1,0:T(8,128)(2,1)}, bf16[2,512,1024]{2,1,0:T(8,128)(2,1)}, bf16[2,512,1024]{2,1,0:T(8,128)(2,1)}) custom-call(bf16[512,1024]{1,0:T(8,128)(2,1)} %reduce-scatter.11.cloned.1.call-done.refs_4_.refs_0_, bf16[512,1024]{1,0:T(8,128)(2,1)} %reduce-scatter.17.cloned.1.call-done.refs_1_, ...), custom_call_target="tpu_custom_call" | custom-call | bytes 42500000 | tf_op jit(solution)/shard_map/pallas_call | solution.py:398
  983.2 50.7 %shard_map.239 = (bf16[2,512,1024]{2,1,0:T(8,128)(2,1)}, bf16[2,512,1024]{2,1,0:T(8,128)(2,1)}, bf16[2,512,1024]{2,1,0:T(8,128)(2,1)}, bf16[2,512,1024]{2,1,0:T(8,128)(2,1)}) custom-call(bf16[512,1024]{1,0:T(8,128)(2,1)} %reduce-scatter.15.cloned.1.call-done.refs_1_.one_ref, bf16[512,1024]{1,0:T(8,128)(2,1)} %reduce-scatter.19.cloned.1.call-done.zero_ref), custom_call_target="tpu_custom_call" | custom-call | bytes 42500000 | tf_op jit(solution)/shard_map/pallas_call | solution.py:398
  1045.8 10.5 shard_map.249
  1056.3 10.0 shard_map.244
  1066.3 27.3 %shard_map.246 = (bf16[2,256,1024]{2,1,0:T(8,128)(2,1)}, bf16[2,256,1024]{2,1,0:T(8,128)(2,1)}, bf16[2,256,1024]{2,1,0:T(8,128)(2,1)}, bf16[2,256,1024]{2,1,0:T(8,128)(2,1)}) custom-call(bf16[256,1024]{1,0:T(8,128)(2,1)} %reduce-scatter.13.cloned.1.call-done.refs_4_.refs_0_, bf16[256,1024]{1,0:T(8,128)(2,1)} %reduce-scatter.21.cloned.1.call-done.refs_1_, ...), custom_call_target="tpu_custom_call" | custom-call | bytes 25500000 | tf_op jit(solution)/shard_map/pallas_call | solution.py:398
  1119.5 27.4 %shard_map.250 = (bf16[2,256,1024]{2,1,0:T(8,128)(2,1)}, bf16[2,256,1024]{2,1,0:T(8,128)(2,1)}, bf16[2,256,1024]{2,1,0:T(8,128)(2,1)}, bf16[2,256,1024]{2,1,0:T(8,128)(2,1)}) custom-call(bf16[256,1024]{1,0:T(8,128)(2,1)} %reduce-scatter.9.cloned.1.call-done.refs_2_.refs_0_, bf16[256,1024]{1,0:T(8,128)(2,1)} %slice.715.refs_1_, ...), custom_call_target="tpu_custom_call" | custom-call | bytes 25500000 | tf_op jit(solution)/shard_map/pallas_call | solution.py:398
  (775 shorter events, 475.2 us)
Async XLA Ops:
  7.2 62.8 %all-gather.17.cloned.1.call-start = ((), (), s32[]{:S(2)}) async-start(), calls=%async_computation.16 | async-start | bytes 4718592 | tf_op jit(solution)/shard_map/all_gather | solution.py:1171
  10.3 142.6 %all-gather.19.cloned.1.call-start = ((), (), s32[]{:S(2)}) async-start(), calls=%async_computation.17 | async-start | bytes 9437184 | tf_op jit(solution)/shard_map/all_gather | solution.py:1171
  70.0 130.7 %all-gather.21.cloned.1.call-start = ((), (), s32[]{:S(2)}) async-start(), calls=%async_computation.18 | async-start | bytes 4718592 | tf_op jit(solution)/shard_map/all_gather | solution.py:1171
  154.7 158.8 %all-gather.23.cloned.1.call-start = ((), (), s32[]{:S(2)}) async-start(), calls=%async_computation.19 | async-start | bytes 9437184 | tf_op jit(solution)/shard_map/all_gather | solution.py:1171
  200.8 130.5 %all-gather.25.cloned.1.call-start = ((), (), s32[]{:S(2)}) async-start(), calls=%async_computation.20 | async-start | bytes 4718592 | tf_op jit(solution)/shard_map/all_gather | solution.py:1171
  201.7 212.5 %all-gather.27.cloned.1.call-start = ((), (), s32[]{:S(2)}) async-start(), calls=%async_computation.21 | async-start | bytes 9437184 | tf_op jit(solution)/shard_map/all_gather | solution.py:1171
  202.3 294.1 %all-gather.29.cloned.1.call-start = ((), (), s32[]{:S(2)}) async-start(), calls=%async_computation.22 | async-start | bytes 9437184 | tf_op jit(solution)/shard_map/all_gather | solution.py:1171
  210.9 332.8 %all-gather.31.cloned.1.call-start = ((), (), s32[]{:S(2)}) async-start(), calls=%async_computation.23 | async-start | bytes 4718592 | tf_op jit(solution)/shard_map/all_gather | solution.py:1171
  237.2 268.3 %collective-permute-start.11 = (bf16[256,1024]{1,0:T(8,128)(2,1)}, bf16[256,1024]{1,0:T(8,128)(2,1)}, u32[]{:S(2)}, u32[]{:S(2)}) collective-permute-start(bf16[256,1024]{1,0:T(8,128)(2,1)} %get-tuple-element.297), channel_id=1, source_target_pairs={{0,4},{4,0},{1,5},{5,1},{2,6},{6,2},{3,7},{7,3},{8,12},{12,8},{9,1... | collective-permute-start | bytes 1572872 | tf_op jit(solution)/shard_map/ppermute | solution.py:916
  241.1 350.6 %reduce-scatter.9.cloned.1.call-start = ((), (), s32[]{:S(2)}) async-start(), calls=%async_computation.8 | async-start | bytes 2621440 | tf_op jit(solution)/shard_map/reduce_scatter | solution.py:1000
  512.9 157.2 %reduce-scatter.11.cloned.1.call-start = ((), (), s32[]{:S(2)}) async-start(), calls=%async_computation.9 | async-start | bytes 5242880 | tf_op jit(solution)/shard_map/reduce_scatter | solution.py:1000
  591.6 123.7 %reduce-scatter.13.cloned.1.call-start = ((), (), s32[]{:S(2)}) async-start(), calls=%async_computation.10 | async-start | bytes 2621440 | tf_op jit(solution)/shard_map/reduce_scatter | solution.py:1000
  670.1 126.1 %reduce-scatter.15.cloned.1.call-start = ((), (), s32[]{:S(2)}) async-start(), calls=%async_computation.11 | async-start | bytes 5242880 | tf_op jit(solution)/shard_map/reduce_scatter | solution.py:1000
  715.4 159.1 %reduce-scatter.17.cloned.1.call-start = ((), (), s32[]{:S(2)}) async-start(), calls=%async_computation.12 | async-start | bytes 5242880 | tf_op jit(solution)/shard_map/reduce_scatter | solution.py:1000
  715.5 71.3 %collective-permute-start.23 = (bf16[256,2048]{1,0:T(8,128)(2,1)}, bf16[256,2048]{1,0:T(8,128)(2,1)S(1)}, u32[]{:S(2)}, u32[]{:S(2)}) collective-permute-start(bf16[256,2048]{1,0:T(8,128)(2,1)} %copy-done.21), channel_id=1, source_target_pairs={{0,4},{4,0},{1,5},{5,1},{2,6},{6,2},{3,7},{7,3},{8,12},{12,8},{9,1... | collective-permute-start | bytes 3145736 | tf_op jit(solution)/shard_map/ppermute | solution.py:916
  796.3 177.6 %reduce-scatter.19.cloned.1.call-start = ((), (), s32[]{:S(2)}) async-start(), calls=%async_computation.13 | async-start | bytes 5242880 | tf_op jit(solution)/shard_map/reduce_scatter | solution.py:1000
  798.8 55.7 %collective-permute-start.21 = (bf16[256,2048]{1,0:T(8,128)(2,1)}, bf16[256,2048]{1,0:T(8,128)(2,1)}, u32[]{:S(2)}, u32[]{:S(2)}) collective-permute-start(bf16[256,2048]{1,0:T(8,128)(2,1)} %copy-done.34), channel_id=1, source_target_pairs={{0,4},{4,0},{1,5},{5,1},{2,6},{6,2},{3,7},{7,3},{8,12},{12,8},{9,1... | collective-permute-start | bytes 3145736 | tf_op jit(solution)/shard_map/ppermute | solution.py:916
  874.5 167.0 %reduce-scatter.21.cloned.1.call-start = ((), (), s32[]{:S(2)}) async-start(), calls=%async_computation.14 | async-start | bytes 2621440 | tf_op jit(solution)/shard_map/reduce_scatter | solution.py:1000
  874.6 159.3 %collective-permute-start.19 = (bf16[256,1024]{1,0:T(8,128)(2,1)}, bf16[256,1024]{1,0:T(8,128)(2,1)}, u32[]{:S(2)}, u32[]{:S(2)}) collective-permute-start(bf16[256,1024]{1,0:T(8,128)(2,1)} %copy-done.90), channel_id=1, source_target_pairs={{0,4},{4,0},{1,5},{5,1},{2,6},{6,2},{3,7},{7,3},{8,12},{12,8},{9,1... | collective-permute-start | bytes 1572872 | tf_op jit(solution)/shard_map/ppermute | solution.py:916
  879.8 89.0 %collective-permute-start.28 = (bf16[256,1024]{1,0:T(8,128)(2,1)}, bf16[256,1024]{1,0:T(8,128)(2,1)}, u32[]{:S(2)}, u32[]{:S(2)}) collective-permute-start(bf16[256,1024]{1,0:T(8,128)(2,1)} %get-tuple-element.236.refs_0_), channel_id=1, source_target_pairs={{0,4},{4,0},{1,5},{5,1},{2,6},{6,2},{3,7},{7,3},{8,12},{12,8},{9,1... | collective-permute-start | bytes 1572872 | tf_op jit(solution)/shard_map/ppermute | solution.py:916
  881.0 87.9 %collective-permute-start.29 = (bf16[256,1024]{1,0:T(8,128)(2,1)}, bf16[256,1024]{1,0:T(8,128)(2,1)}, u32[]{:S(2)}, u32[]{:S(2)}) collective-permute-start(bf16[256,1024]{1,0:T(8,128)(2,1)} %get-tuple-element.282), channel_id=1, source_target_pairs={{0,4},{4,0},{1,5},{5,1},{2,6},{6,2},{3,7},{7,3},{8,12},{12,8},{9,1... | collective-permute-start | bytes 1572872 | tf_op jit(solution)/shard_map/ppermute | solution.py:916
  884.1 95.1 %collective-permute-start.25 = (bf16[256,16]{1,0:T(8,128)(2,1)}, bf16[256,16]{1,0:T(8,128)(2,1)}, u32[]{:S(2)}, u32[]{:S(2)}) collective-permute-start(bf16[256,16]{1,0:T(8,128)(2,1)} %bitcast.404), channel_id=1, source_target_pairs={{0,4},{4,0},{1,5},{5,1},{2,6},{6,2},{3,7},{7,3},{8,12},{12,8},{9,1... | collective-permute-start | bytes 24584 | tf_op jit(solution)/shard_map/ppermute | solution.py:916
  973.9 133.0 %reduce-scatter.23.cloned.1.call-start = ((), (), s32[]{:S(2)}) async-start(), calls=%async_computation.15 | async-start | bytes 2949120 | tf_op jit(solution)/shard_map/reduce_scatter | solution.py:1000
  978.2 55.7 %collective-permute-start.20 = (bf16[256,1024]{1,0:T(8,128)(2,1)}, bf16[256,1024]{1,0:T(8,128)(2,1)}, u32[]{:S(2)}, u32[]{:S(2)}) collective-permute-start(bf16[256,1024]{1,0:T(8,128)(2,1)} %get-tuple-element.286), channel_id=1, source_target_pairs={{0,4},{4,0},{1,5},{5,1},{2,6},{6,2},{3,7},{7,3},{8,12},{12,8},{9,1... | collective-permute-start | bytes 1572872 | tf_op jit(solution)/shard_map/ppermute | solution.py:916
  (175 other events, 1616.0 us)
Sparse Core Ops, SparseCore 0:
  10.4 59.5 all-gather.16
  72.2 80.6 all-gather.18
  155.1 45.6 all-gather.20
  202.8 80.7 all-gather.22
  285.6 45.6 all-gather.24
  333.4 80.7 all-gather.26
  415.8 80.5 all-gather.28
  498.0 45.6 all-gather.30
  546.6 42.5 reduce-scatter.8
  592.0 76.0 reduce-scatter.10
  671.0 44.3 reduce-scatter.12
  718.2 76.0 reduce-scatter.14
  797.2 77.2 reduce-scatter.16
  877.3 77.2 reduce-scatter.18
  974.0 43.4 reduce-scatter.20
  1041.7 47.7 reduce-scatter.22

commit v4 on v3

--- a/solution.py
+++ b/solution.py
@@ -36,6 +36,7 @@
 R_FF = FF // RANKS
 R_OUT = R_SSM + R_ATT
 HALF = 1024
+PART = HALF // 2
 MESH = pl.DeviceIdType.MESH
 BF = jnp.bfloat16
 F32 = jnp.float32
@@ -203,6 +204,31 @@
     spread(me, rows, out_ref, s2, r2)
 
 
+def end_rows_kernel(part_ref, resid_ref, out_ref, slots, s1, r1, s2, r2):
+    me = rank_place()
+    greet(me)
+    total = scatter_sum(me, resid_ref.shape[0], part_ref, slots, s1, r1) + resid_ref[...]
+    out_ref[...] = total.astype(BF)
+
+
+def back_rows_kernel(
+    part_ref, given_ref, value_ref, gain_ref, out_ref, gain_grad_ref, slots, s1, r1, s2, r2
+):
+    me = rank_place()
+    greet(me)
+    grad = scatter_sum(me, given_ref.shape[0], part_ref, slots, s1, r1)
+    total, gain_grad_ref[...] = norm_back(grad, value_ref[...], gain_ref[...].astype(F32))
+    out_ref[...] = (given_ref[...] + total).astype(BF)
+
+
+def norm_back(grad, value, gain):
+    scale = lax.rsqrt(jnp.mean(value * value, axis=-1, keepdims=True) + EPSILON)
+    unit = value * scale
+    scaled = grad * gain
+    total = scale * (scaled - unit * jnp.mean(scaled * unit, axis=-1, keepdims=True))
+    return total, jnp.sum(grad * unit, axis=0, keepdims=True)
+
+
 def end_kernel(part_ref, resid_ref, out_ref, slots, s1, r1, s2, r2):
     rows = resid_ref.shape[0]
     me = rank_place()
@@ -219,14 +245,8 @@
     me = rank_place()
     greet(me)
     grad = scatter_sum(me, rows, part_ref, slots, s1, r1)
-    value = value_ref[...]
-    scale = lax.rsqrt(jnp.mean(value * value, axis=-1, keepdims=True) + EPSILON)
-    unit = value * scale
-    gain_grad_ref[...] = jnp.sum(grad * unit, axis=0, keepdims=True)
-    scaled = grad * gain_ref[...].astype(F32)
-    total = given_ref[...] + scale * (
-        scaled - unit * jnp.mean(scaled * unit, axis=-1, keepdims=True)
-    )
+    total, gain_grad_ref[...] = norm_back(grad, value_ref[...], gain_ref[...].astype(F32))
+    total = given_ref[...] + total
     wide_ref[...] = total
     out_ref[pl.ds(pl.multiple_of(me * rows, rows), rows), :] = total.astype(BF)
     spread(me, rows, out_ref, s2, r2)
@@ -264,6 +284,16 @@
 def end_step(part, resid):
     rows = resid.shape[0]
     return rank_call(end_kernel, [jax.ShapeDtypeStruct(part.shape, BF)], rows, part, resid)[0]
+
+
+def end_rows(part, resid):
+    shape = jax.ShapeDtypeStruct(resid.shape, BF)
+    return rank_call(end_rows_kernel, [shape], resid.shape[0], part, resid)[0]
+
+
+def back_rows(part, given, value, gain):
+    shapes = [jax.ShapeDtypeStruct(given.shape, BF), jax.ShapeDtypeStruct((1, D), F32)]
+    return rank_call(back_rows_kernel, shapes, given.shape[0], part, given, value, gain[None])
 
 
 def back_step(part, given, value, gain, after=()):
@@ -461,7 +491,7 @@
 
 def spread_gate_up(place, pieces, nz):
     rows = pieces[0].shape[1]
-    tile = min(rows, 64)
+    tile = min(rows, 128)
     block = pl.BlockSpec((2, tile, HALF), lambda i: (0, i, 0))
     return pl.pallas_call(
         functools.partial(gate_up_kernel, nz),
@@ -755,6 +785,63 @@
     )(place, *args)
 
 
+EXTRA = 32
+
+
+def pack_kernel(nz, *refs):
+    out_ref, conv_full, ssm_full = refs[-3:]
+    rank = rank_place()
+    out_ref[...] = jnp.zeros_like(out_ref)
+    width, conv_width, ssm_width = D // nz, CONV_W // nz, D_SSM // nz
+    heads_width, inner = SSM_HEADS // nz, nz // RANKS
+    head_of = lax.broadcasted_iota(jnp.int32, (R_SSM, LANES), 0) // SSM_HEAD
+    lane = lax.broadcasted_iota(jnp.int32, (R_SSM, LANES), 1)
+    to_heads = (head_of == lane).astype(F32)
+    for layer in range(2):
+        heads_ref, lanes_ref, conv_ref, gain0_ref, gain1_ref, dt_ref = refs[6 * layer : 6 * layer + 6]
+        conv_full[...] = jnp.zeros_like(conv_full)
+        ssm_full[...] = jnp.zeros_like(ssm_full)
+        at = lambda start, size: pl.ds(pl.multiple_of(start, LANES), size)
+        conv_full[:, at(R_SSM * rank, R_SSM)] = conv_ref[:, :R_SSM]
+        conv_full[:, at(D_SSM + R_BC * rank, R_BC)] = conv_ref[:, R_SSM:]
+        ssm_full[:, at(R_SSM * rank, R_SSM)] = lanes_ref[...]
+        skip = exact(lanes_ref[...], to_heads, ((1,), (0,)))[1:2]
+        heads = (heads_ref[0:1], heads_ref[1:2], skip)
+        row = 16 + 8 * layer
+        for z in range(nz):
+            cut = slice(width * z, width * (z + 1))
+            out_ref[z, 0:16, PART * layer : PART * layer + width] = dt_ref[:, cut]
+            out_ref[z, row : row + 1, 0:width] = gain0_ref[:, cut]
+            out_ref[z, row : row + 1, PART : PART + width] = gain1_ref[:, cut]
+            out_ref[z, row + 1 : row + 6, 0:conv_width] = conv_full[
+                0 : CONV_K + 1, conv_width * z : conv_width * (z + 1)
+            ]
+            out_ref[z, row + 6 : row + 7, 0:ssm_width] = ssm_full[
+                0:1, ssm_width * z : ssm_width * (z + 1)
+            ]
+            start = heads_width * (z % inner)
+            for k in range(3):
+                value = jnp.where(rank == z // inner, heads[k], 0.0)
+                out_ref[z, row + 7 : row + 8, LANES * k : LANES * k + heads_width] = value[
+                    :, start : start + heads_width
+                ]
+
+
+def pack(layers, nz):
+    args = [array for layer in layers for array in layer]
+    out = jax.ShapeDtypeStruct((nz, EXTRA, HALF), F32)
+    return pl.pallas_call(
+        functools.partial(pack_kernel, nz),
+        grid=(1,),
+        out_shape=out,
+        in_specs=[whole_block(arg) for arg in args],
+        out_specs=whole_block(out),
+        scratch_shapes=[pltpu.VMEM((8, CONV_W), F32), pltpu.VMEM((8, D_SSM), F32)],
+        cost_estimate=lasting(4),
+        compiler_params=pltpu.CompilerParams(vmem_limit_bytes=40 * 2**20),
+    )(*args)
+
+
 def rotation_tables(length):
     half = HEAD_DIM // 2
     frequency = ROPE_BASE ** (-jnp.arange(half, dtype=F32) / half)
@@ -916,7 +1003,7 @@
     return lax.ppermute(value, axis, [(0, 1), (1, 0)])
 
 
-def layer_forward(entering, resid, weights, small, first):
+def layer_forward(entering, resid, weights, small, then, last):
     s, y = lax.axis_index("section"), lax.axis_index("y")
     length = entering.shape[0]
     x1 = narrow(rms(entering.astype(F32), small["gain0"][None, :]))
@@ -928,6 +1015,7 @@
     kv_raw = left[:, R_CONV:]
     kv = narrow(jnp.where(y == 0, rotary(kv_raw, 1.0), kv_raw))
     shared = swap(jnp.concatenate([u[:, R_SSM:], kv], axis=1))
+    then("swap", shared)
     b_rows = jnp.concatenate([shared[0, :, :R_BC], shared[1, :, :R_BC]], axis=1)
     c_rows = jnp.concatenate([shared[2, :, :R_BC], shared[3, :, :R_BC]], axis=1)
     pair = lax.dynamic_slice_in_dim(shared, 2 * s, 2, axis=0)[:, :, R_BC:]
@@ -949,11 +1037,12 @@
     mo = narrow(jnp.where(is_ssm, wide.astype(F32) * spread_of[:, None], wide.astype(F32)))
     part = jnp.concatenate([dot(mo, weights["out"][0]), dot(mo, weights["out"][1])], axis=1)
     mid, x2 = mid_step(narrow(part), resid, small["gain1"])
+    then("mid", mid)
     gate = dot(x2, weights["gu"][0])
     up = dot(x2, weights["gu"][1])
     act = narrow(jax.nn.silu(gate) * up)
     part2 = jnp.concatenate([dot(act, weights["down"][0]), dot(act, weights["down"][1])], axis=1)
-    leaving = end_step(narrow(part2), mid)
+    leaving = (end_rows if last else end_step)(narrow(part2), mid)
     kept = dict(
         resid=resid, x1=x1, xbc=xbc, u=u, b=b_rows, c=c_rows, key=key, value=value, query=query,
         probs=probs, z=z, dt_raw=dt_raw, scan=scan, spread=spread_of, mo=mo, mid=mid, x2=x2,
@@ -1006,23 +1095,25 @@
 
     halves = lambda v: (v[:, :HALF], v[:, HALF:])
     g0, g1 = halves(grad)
-    down_block = functools.partial(product, kept["act"], (g0, g1))
+    down_block = None
     if layer == 1:
-        reduce("down1", down_block())
+        reduce("down1", product(kept["act"], (g0, g1)))
     grad_act = dot_t(g0, down[0]) + dot_t(g1, down[1])
     gate, up = kept["gate"], kept["up"]
     sig = jax.nn.sigmoid(gate)
     d_gate = narrow(grad_act * up * (sig * (1.0 + gate * (1.0 - sig))))
     d_up = narrow(grad_act * gate * sig)
+    part = dot_t(d_gate, gu[0]) + dot_t(d_up, gu[1])
     if layer == 1:
         reduce("gu1", product(kept["x2"], (d_gate, d_up), *first))
-    part = dot_t(d_gate, gu[0]) + dot_t(d_up, gu[1])
     d_mid, db, grad_gain1 = back_step(
         narrow(part), given, kept["mid"], small["gain1"], due("mlp") + list(first)
     )
     if layer == 0:
         reduce("gu0", product(kept["x2"], (d_gate, d_up), db))
     b0, b1 = halves(db)
+    if layer == 0:
+        down_block = product(kept["act"], (g0, g1), db)
     d_mo = dot_t(b0, out[0]) + dot_t(b1, out[1])
     mo = kept["mo"]
     is_ssm = small["is_ssm"][None, :]
@@ -1034,34 +1125,28 @@
     message, d_right, d_x, d_raw, head_sums, lane_sums = mixer_back(
         got, kept, small, overlap, tables
     )
-    skip = jnp.sum(lane_sums[1].reshape(R_HEADS, SSM_HEAD), axis=1)
-    grad_heads = jnp.concatenate([head_sums[:2, :R_HEADS], skip[None]], axis=0)
-    grad_ssm_gain = lane_sums[0]
     if layer == 1:
         reduce("out1", product(kept["mo"], (b0, b1), message))
     back = swap(message, None, due("scan"))
     d_left, grad_conv = conv_back(back, d_x, kept["xbc"], small["conv"], tables)
-    grad_conv = grad_conv[: CONV_K + 1]
     part = dot_t(d_left, win[0]) + dot_t(d_right, win[1]) + dot_t(d_raw, weights["dt"])
     part = narrow(part)
-    reduce(f"in{layer}", product(kept["x1"], (d_left, d_right), part))
-    _, entering_grad, grad_gain0 = back_step(
-        part,
-        d_mid,
-        kept["resid"].astype(F32),
-        small["gain0"],
-        due("in"),
-    )
+    if layer == 1:
+        reduce("in1", product(kept["x1"], (d_left, d_right), part))
+    enter = (part, d_mid, kept["resid"].astype(F32), small["gain0"])
+    if layer == 0:
+        entering_grad, grad_gain0 = back_rows(*enter)
+        reduce("in0", product(kept["x1"], (d_left, d_right), entering_grad))
+    else:
+        _, entering_grad, grad_gain0 = back_step(*enter, due("in"))
     got_gu = None
     if layer == 0:
         got_gu = share(queue["gu1"], queue["gu0"], 50, (entering_grad,))
-        reduce("out0", product(kept["mo"], (b0, b1), got_gu[0]))
-    two = lambda v: jnp.concatenate([v, flip(v, "core")], axis=0)
-    grad_dt_w = t_dot(two(d_raw[:, :16]), two(kept["x1"]))
-    smalls_grad = dict(
-        heads=grad_heads, conv=grad_conv, ssm=grad_ssm_gain[None], dt=grad_dt_w,
-        gains=jnp.concatenate([grad_gain0, grad_gain1], axis=0),
-    )
+        place = jnp.stack([y, core]).astype(jnp.int32)
+        got_gu = spread_gate_up(place, got_gu, lax.axis_size("fsdp"))
+        reduce("out0", product(kept["mo"], (b0, b1), got_gu, down_block))
+    grad_dt_w = t_dot(d_raw[:, :16], kept["x1"])
+    smalls_grad = (head_sums, lane_sums, grad_conv, grad_gain0, grad_gain1, grad_dt_w)
     return entering_grad, smalls_grad, (down_block, reduce, got_gu)
 
 
@@ -1182,26 +1267,31 @@
     mlp_arrived = flip(mlp_sent, "section")
     of_layer = lambda layer, mine, theirs: jnp.where(s == layer, mine, theirs)
     flat_rows = lambda whole: whole.reshape(2, -1, HALF)
-    in0 = gather(copy_after(of_layer(0, own["in"], in_arrived), everything))
-    out_other = gather(copy_after(out_arrived, in0))
+    in0 = gather(copy_after(of_layer(0, own["in"], in_arrived), everything, out_own))
     wide = own["gu"].shape[0]
     mlp0, mlp1 = (of_layer(layer, mlp_own, mlp_arrived) for layer in range(2))
-    gu0 = gather(mlp0[:wide])
-    down0 = gather(mlp0[wide:])
-    in1 = gather(of_layer(1, own["in"], in_arrived))
-    gu1 = gather(mlp1[:wide])
-    down1 = gather(mlp1[wide:])
+
+    def together(token, *parts):
+        whole = gather(copy_after(jnp.concatenate(parts, axis=0), token))
+        whole = whole.reshape(2, nz, -1, HALF)
+        found, at = [], 0
+        for part in parts:
+            found.append(flat_rows(whole[:, :, at : at + part.shape[0]]))
+            at += part.shape[0]
+        return found
+
+    out_other, gu0, down0 = together(in0, out_arrived, mlp0[:wide], mlp0[wide:])
     weights = [
-        dict(
-            out=flat_rows(of_layer(layer, out_own, out_other)),
-            **{"in": flat_rows((in0, in1)[layer])},
-        )
-        for layer in range(2)
+        dict(out=of_layer(layer, flat_rows(out_own), out_other)) for layer in range(2)
     ]
-    weights[0]["gu"] = flat_rows(gu0)
-    weights[0]["down"] = flat_rows(down0)
-    weights[1]["gu"] = flat_rows(gu1)
-    weights[1]["down"] = flat_rows(down1)
+    weights[0].update({"in": flat_rows(in0), "gu": gu0, "down": down0})
+
+    def then(point, token):
+        if point == "swap":
+            piece = of_layer(1, own["in"], in_arrived)
+            weights[1]["in"] = flat_rows(gather(copy_after(piece, token)))
+        elif point == "mid":
+            weights[1]["gu"], weights[1]["down"] = together(token, mlp1[:wide], mlp1[wide:])
 
     def whole_sequence(own_rows):
         place = 2 * y + core
@@ -1232,7 +1322,12 @@
     outs, kept = [], []
     for layer in range(2):
         hidden, keep = layer_forward(
-            hidden, rank_rows(hidden), weights[layer], smalls[layer], layer == 0
+            hidden,
+            rank_rows(hidden),
+            weights[layer],
+            smalls[layer],
+            then if layer == 0 else lambda *_: None,
+            layer == 1,
         )
         outs.append(hidden)
         kept.append(keep)
@@ -1253,74 +1348,65 @@
         )
         grads[layer] = grad
 
-    def block_rows(pair):
-        chosen = jnp.where(s == 0, pair[0], pair[1]).reshape(RANKS, rows, D)
-        mine = lax.dynamic_index_in_dim(chosen, 2 * y + core, 0, False)
-        sent = lax.dynamic_index_in_dim(chosen, 2 * y + (1 - core), 0, False)
+    def block_rows(whole):
+        blocks = whole.reshape(RANKS, rows, D)
+        mine = lax.dynamic_index_in_dim(blocks, 2 * y + core, 0, False)
+        sent = lax.dynamic_index_in_dim(blocks, 2 * y + (1 - core), 0, False)
         theirs = flip(sent, "core")
-        both = jnp.where(core == 0, jnp.stack([mine, theirs]), jnp.stack([theirs, mine]))
-        return both[None, :, None]
+        return jnp.where(core == 0, jnp.stack([mine, theirs]), jnp.stack([theirs, mine]))
+
+    def block_from_ranks(part, section):
+        moved = []
+        for micro in range(2):
+            pairs = [
+                (4 * a + 2 * b + micro, 4 * section + 2 * a + b)
+                for a in range(2)
+                for b in range(2)
+            ]
+            moved.append(lax.ppermute(part, ("section", "y", "core"), pairs))
+        return jnp.stack(moved)
+
+    layer_outputs = jnp.where(s == 0, block_rows(outs[0]), block_from_ranks(outs[1], 1))
+    grad_inputs = jnp.where(s == 1, block_rows(grads[1]), block_from_ranks(grads[0], 0))
 
     down_block, reduce, got_gu = blocks
-    fan = lambda array, axis: jnp.moveaxis(
-        array.reshape(array.shape[:axis] + (nz, -1) + array.shape[axis + 1 :]), axis, 0
-    )
-    dt_rows = jnp.concatenate([fan(g["dt"], 1) for g in smalls_grad], axis=2)
-    dt_rows = jnp.pad(dt_rows, ((0, 0), (0, 0), (0, HALF - dt_rows.shape[2])))
-
-    def placed(array, total, starts):
-        whole = jnp.zeros((array.shape[0], total), F32)
-        at = 0
-        for start, width in starts:
-            whole = lax.dynamic_update_slice(whole, array[:, at : at + width], (0, start))
-            at += width
-        return fan(whole, 1).reshape(nz, -1)
-
-    listed = []
-    for g in smalls_grad:
-        listed.append(fan(g["gains"], 1).reshape(nz, -1))
-        listed.append(placed(g["heads"], SSM_HEADS, [(R_HEADS * rank, R_HEADS)]))
-        listed.append(
-            placed(g["conv"], CONV_W, [(R_SSM * rank, R_SSM), (D_SSM + R_BC * rank, R_BC)])
-        )
-        listed.append(placed(g["ssm"], D_SSM, [(R_SSM * rank, R_SSM)]))
-    packed = jnp.concatenate(listed, axis=1)
-    packed = packed + flip(packed, "core")
-    amount = packed.shape[1]
-    packed = jnp.pad(packed, ((0, 0), (0, -amount % (16 * HALF)))).reshape(nz, -1, HALF)
+    extra = pack(smalls_grad, nz)
+    extra = extra + flip(extra, "core")
     down_rows = R_FF // nz
-    extra = jnp.concatenate([dt_rows, packed], axis=1)
     extra_count = extra.shape[1]
-    got_in = share(queue["in1"], queue["in0"], 50)
-    down_block = down_block(got_in[0])
-    last = jnp.concatenate([down_block.reshape(nz, down_rows, HALF), narrow(extra)], axis=1)
+    got_in = share(queue["in1"], queue["in0"], 50, (grad_inputs, layer_outputs))
+    extra = copy_after(narrow(extra).reshape(-1, HALF), got_in[0]).reshape(extra.shape)
+    last = jnp.concatenate([down_block.reshape(nz, down_rows, HALF), extra], axis=1)
     reduce("down0", last.reshape(-1, HALF))
     down0, extra = queue["down0"][:down_rows], queue["down0"][down_rows:]
 
     place = jnp.stack([y, core]).astype(jnp.int32)
-    grad_w_gu = spread_gate_up(place, got_gu, nz)
+    grad_w_gu = got_gu
     got_out = share(queue["out1"], queue["out0"], 30, (got_in[0],))
     shared = swap(extra).astype(F32)
     grad_w_in, grad_w_qkv = spread_in(place, got_in)
     got_down = share(queue["down1"], down0, 30, (grad_w_in,))
     out_rows, o_rows = R_SSM // nz, R_ATT // nz
-    grad_w_out = spread_rows(place, got_out, 0, out_rows, o_rows)
+    grad_w_out = spread_rows(place, got_out, 0, out_rows, out_rows)
     grad_w_o = spread_rows(place, got_out, out_rows, o_rows, o_rows)
-    grad_w_down = spread_rows(place, got_down, 0, down_rows, min(down_rows, 128))
-
-    width = D // nz
-    dt_all = jnp.where(s == 0, shared[:, :12, :width], shared[:, :12, width : 2 * width])
+    grad_w_down = spread_rows(place, got_down, 0, down_rows, down_rows)
+
+    width, conv_width, ssm_width = D // nz, CONV_W // nz, D_SSM // nz
+    heads_width = SSM_HEADS // nz
+    dt_all = jnp.where(s == 0, shared[:, :R_HEADS, :width], shared[:, :R_HEADS, PART : PART + width])
     grad_w_in = with_dt(grad_w_in, dt_all.reshape(SSM_HEADS, width)).T
-    small_sum = jnp.sum(shared[:, 16:], axis=0).reshape(-1)[:amount].reshape(2, -1)
-    small_sum = jnp.where(s == 0, small_sum[0], small_sum[1])
-    cuts, at = [], 0
-    for lead, total in ((2, D), (3, SSM_HEADS), (5, CONV_W), (1, D_SSM)):
-        size = lead * total // nz
-        cuts.append(small_sum[at : at + size].reshape(lead, total // nz))
-        at += size
+    small_sum = jnp.sum(shared[:, 16:], axis=0)
+    small_sum = jnp.where(s == 0, small_sum[:8], small_sum[8:])
+    head_row = small_sum[7, : 3 * LANES].reshape(3, LANES)
+    cuts = (
+        jnp.stack([small_sum[0, :width], small_sum[0, PART : PART + width]]),
+        head_row[:, :heads_width],
+        small_sum[1:6, :conv_width],
+        small_sum[6:7, :ssm_width],
+    )
     return (
-        block_rows(outs),
-        block_rows(grads),
+        layer_outputs[None, :, None],
+        grad_inputs[None, :, None],
         cuts[0][None],
         cuts[1][None],
         cuts[2][None],

time: 1180 us -> 1130 us (0.958)
  waiting for transfers between devices: 245 us -> 217 us
  matrix products: 95.6 us -> 79.8 us
    all_gather x8 -> x5, waiting for transfers between devices: 178 us -> 121 us  [gather(): order.append(lax.all_gather(in_turn(piece), ('core', 'fsdp'), axis=0))]
    pallas_call x8, Pallas kernels: 225 us -> 202 us  [rank_call(): pl.pallas_call(ignoring(kernel, len(args), len(after)), out_shape=out_sha...]
    ppermute x6, waiting for transfers between devices: 1.79 us -> 18.5 us  [whole_sequence(): here = lax.ppermute(sent, ('y', 'core'), pairs)]
    pallas_call x2 -> x5, Pallas kernels: 5.11 us -> 18.8 us  [copy_after(): pl.pallas_call(ignoring(copy_kernel, 1, len(tokens)), grid=(rows // tile,...]
    dot_general x20, matrix products: 45 us -> 32.8 us  [dot_t(): lax.dot_general(left, right, (((1,), (1,)), ((), ())), preferred_element_...]
    unnamed x323 -> x402, local copies, waits for them, and re-layouts: 28.7 us -> 39.7 us
    ppermute x24 -> x22, waiting for transfers between devices: 45 us -> 46.2 us  [flip(): return lax.ppermute(value, axis, [(0, 1), (1, 0)])]
  transfers between devices with their start and end apart: 46 -> 45, of which waited for: 13 -> 14; matrix products, arithmetic and copies ran while one was open for 19% -> 18% of each run, Pallas kernels for 47% -> 47%
where the time goes in v4:
time: 1130 us; the launch traced here: 1120 us
  Pallas kernels  583 us (52%)
  waiting for transfers between devices  217 us (19%)
  local copies, waits for them, and re-layouts  99.4 us (9%)
  matrix products  79.8 us (7%)
  other arithmetic  62.8 us (6%)
  blocking collectives  35.1 us (3%)
  starting transfers between devices  21.6 us (2%)
  between operations  17.8 us (2%)
    pallas_call x8, Pallas kernels, rank_call(): pl.pallas_call(ignoring(kernel, len(args), len(after)), out_shape=out_sha...  202 us
    pallas_call x4, Pallas kernels, share(): pl.pallas_call(ignoring(share_kernel, 2, len(after)), out_shape=[shape] *...  166 us
    all_gather x5, waiting for transfers between devices, gather(): order.append(lax.all_gather(in_turn(piece), ('core', 'fsdp'), axis=0))  121 us
    pallas_call x9, Pallas kernels, swap(): pl.pallas_call(ignoring(functools.partial(swap_kernel, stat is not None),...  80.3 us
    pallas_call x8, Pallas kernels, outer_sum(): pl.pallas_call(ignoring(product_kernel, 4, len(tokens)), grid=(width // t...  52.1 us
    ppermute x22, waiting for transfers between devices, flip(): return lax.ppermute(value, axis, [(0, 1), (1, 0)])  46.2 us
    unnamed x402, local copies, waits for them, and re-layouts  39.7 us
    dot_general x18, matrix products, dot(): return jnp.dot(left, right, preferred_element_type=F32)  36 us
  transfers between devices with their start and end apart: 45, of which 14 were waited for; matrix products, arithmetic and copies ran while one was open for 18% of the time, Pallas kernels for 47%

profile of v4, /device:TPU:0, one launch (start us, length us, event | category | flops | bytes accessed | tf_op | source)
XLA Modules:
  0.0 1116.3 jit_solution(2179522043732890788)
XLA Ops:
  20.1 35.1 %all_gather.33 = bf16[8,256,128]{2,1,0:T(8,128)(2,1)S(1)} all-gather(bf16[1,256,128]{2,1,0:T(8,128)(2,1)S(1)} %pad_bitcast_fusion), channel_id=1, replica_groups=mesh['section'=2,'y'=2,'core'=2,'fsdp'=4] {'section','fsdp'}, dimensions={0}, use_global_device_ids=true | all-gather | bytes 589824 | tf_op jit(solution)/shard_map/all_gather | solution.py:1185
  59.8 10.2 all-gather.11.cloned.1.call-done
  88.7 34.7 %collective-permute-done.5 = bf16[768,1024]{1,0:T(8,128)(2,1)S(1)} collective-permute-done((bf16[768,1024]{1,0:T(8,128)(2,1)S(1)}, bf16[768,1024]{1,0:T(8,128)(2,1)S(1)}, u32[]{:S(2)}, u32[]{:S(2)}) %collective-permute-start.5) | collective-permute-done | bytes 1572896 | tf_op jit(solution)/shard_map/ppermute | solution.py:1003
  129.0 24.9 %all-gather.13.cloned.1.call-done = bf16[4096,1024]{1,0:T(8,128)(2,1)} async-done(((bf16[512,1024]{1,0:T(8,128)(2,1)}), bf16[4096,1024]{1,0:T(8,128)(2,1)}) %all-gather.13.cloned.1.call-update) | async-done | bytes 8388624 | tf_op jit(solution)/shard_map/all_gather | solution.py:1256
  164.9 10.0 collective-permute-done.1
  237.9 71.5 %all-gather.15.cloned.1.call-done = bf16[8192,1024]{1,0:T(8,128)(2,1)} async-done(((bf16[1024,1024]{1,0:T(8,128)(2,1)}), bf16[8192,1024]{1,0:T(8,128)(2,1)}) %all-gather.15.cloned.1.call-update) | async-done | bytes 16777232 | tf_op jit(solution)/shard_map/all_gather | solution.py:1256
  317.4 29.5 %shard_map.215 = (f32[64,2048]{1,0:T(8,128)S(1)}, bf16[256,2048]{1,0:T(8,128)(2,1)}) custom-call(bf16[256,2048]{1,0:T(8,128)(2,1)S(1)} %pad_maximum_fusion.6.part_ref, bf16[64,2048]{1,0:T(8,128)(2,1)S(1)} %get-tuple-element.216.resid_ref, f32[1,2048]{1,0:T(1,128)S(1)} %bitcast.423), custom_call_target="tpu_custom_call" | custom-call | bytes 22950000 | tf_op jit(solution)/shard_map/pallas_call | solution.py:256
  386.6 27.8 %shard_map.216 = bf16[256,2048]{1,0:T(8,128)(2,1)S(1)} custom-call(bf16[256,2048]{1,0:T(8,128)(2,1)S(1)} %pad_maximum_fusion.7.part_ref, f32[64,2048]{1,0:T(8,128)S(1)} %copy-done.4), custom_call_target="tpu_custom_call" | custom-call | bytes 22950000 | tf_op jit(solution)/shard_map/pallas_call | solution.py:256
  466.9 27.3 %shard_map.220 = (f32[64,2048]{1,0:T(8,128)S(1)}, bf16[256,2048]{1,0:T(8,128)(2,1)S(1)}) custom-call(bf16[256,2048]{1,0:T(8,128)(2,1)S(1)} %pad_maximum_fusion.8.part_ref, bf16[64,2048]{1,0:T(8,128)(2,1)S(1)} %get-tuple-element.223.resid_ref, f32[1,2048]{1,0:T(1,128)S(1)} %bitcast.425), custom_call_target="tpu_custom_call" | custom-call | bytes 22950000 | tf_op jit(solution)/shard_map/pallas_call | solution.py:256
  494.2 14.8 %all-gather.19.cloned.1.call-done = bf16[6144,1024]{1,0:T(8,128)(2,1)} async-done(((bf16[768,1024]{1,0:T(8,128)(2,1)}), bf16[6144,1024]{1,0:T(8,128)(2,1)}) %all-gather.19.cloned.1.call-update) | async-done | bytes 12582928 | tf_op jit(solution)/shard_map/all_gather | solution.py:1256
  532.9 15.1 %shard_map.222.refs_4_ = bf16[64,2048]{1,0:T(8,128)(2,1)S(1)} custom-call(bf16[256,2048]{1,0:T(8,128)(2,1)S(1)} %pad_maximum_fusion.9.part_ref, f32[64,2048]{1,0:T(8,128)S(1)} %get-tuple-element.98.resid_ref.refs_2_), custom_call_target="tpu_custom_call" | custom-call | bytes 22950000 | tf_op jit(solution)/shard_map/pallas_call | solution.py:256
  574.2 27.4 %shard_map.223 = (f32[64,2048]{1,0:T(8,128)S(1)}, bf16[256,2048]{1,0:T(8,128)(2,1)S(1)}, f32[1,2048]{1,0:T(1,128)S(1)}) custom-call(bf16[256,2048]{1,0:T(8,128)(2,1)S(1)} %fusion.24.refs_0_, f32[64,2048]{1,0:T(8,128)S(1)} %dynamic-slice_convert_fusion.1.refs_1_, f32[64,2048]{1,0:T(8,128)S(1)} %get-tuple-element.98.resid_ref.refs_2_, ...), custom_call_target="tpu_custom_call" | custom-call | bytes 22950000 | tf_op jit(solution)/shard_map/pallas_call | solution.py:256
  610.6 10.0 shard_map.225
  635.2 11.2 reduce-scatter.11.cloned.1.call-done.refs_4_.refs_0_
  683.1 10.5 reduce-scatter.13.cloned.1.call-done.refs_4_.refs_0_
  697.1 29.9 %shard_map.230 = (f32[64,2048]{1,0:T(8,128)}, bf16[256,2048]{1,0:T(8,128)(2,1)S(1)}, f32[1,2048]{1,0:T(1,128)S(1)}) custom-call(bf16[256,2048]{1,0:T(8,128)(2,1)S(1)} %copy-done.2, f32[64,2048]{1,0:T(8,128)S(1)} %copy-done.24, f32[64,2048]{1,0:T(8,128)S(1)} %copy-done.19, f32[1,2048]{1,0:T(1,128)S(1)} %bitcast.428, bf16[512,1024]{1,0:T(8,128)(2,1)S(1)} %copy-done.8), custom_call_target="tpu_custom_call" | custom-call | bytes 22950000 | tf_op jit(solution)/shard_map/pallas_call | solution.py:256
  734.7 29.1 %shard_map.232 = (f32[64,2048]{1,0:T(8,128)S(1)}, bf16[256,2048]{1,0:T(8,128)(2,1)S(1)}, f32[1,2048]{1,0:T(1,128)S(1)}) custom-call(bf16[256,2048]{1,0:T(8,128)(2,1)S(1)} %fusion.25.refs_0_, f32[64,2048]{1,0:T(8,128)S(1)} %dynamic-slice_convert_fusion.refs_1_, f32[64,2048]{1,0:T(8,128)S(1)} %copy-done.5, f32[1,2048]{1,0:T(1,128)S(1)} %bitcast.424, ...), custom_call_target="tpu_custom_call" | custom-call | bytes 22950000 | tf_op jit(solution)/shard_map/pallas_call | solution.py:256
  786.7 9.9 shard_map.233
  830.7 15.7 %shard_map.238 = (bf16[64,2048]{1,0:T(8,128)(2,1)S(1)}, f32[1,2048]{1,0:T(1,128)S(1)}) custom-call(bf16[256,2048]{1,0:T(8,128)(2,1)S(1)} %fusion.27.part_ref, f32[64,2048]{1,0:T(8,128)S(1)} %copy-done.26, f32[64,2048]{1,0:T(8,128)S(1)} %copy-done.18, f32[1,2048]{1,0:T(1,128)S(1)} %bitcast.427), custom_call_target="tpu_custom_call" | custom-call | bytes 22950000 | tf_op jit(solution)/shard_map/pallas_call | solution.py:256
  865.6 50.9 %shard_map.245 = (bf16[2,512,1024]{2,1,0:T(8,128)(2,1)}, bf16[2,512,1024]{2,1,0:T(8,128)(2,1)}, bf16[2,512,1024]{2,1,0:T(8,128)(2,1)}, bf16[2,512,1024]{2,1,0:T(8,128)(2,1)}) custom-call(bf16[512,1024]{1,0:T(8,128)(2,1)} %reduce-scatter.11.cloned.1.call-done.refs_4_.refs_0_, bf16[512,1024]{1,0:T(8,128)(2,1)} %reduce-scatter.17.cloned.1.call-done.refs_1_, ...), custom_call_target="tpu_custom_call" | custom-call | bytes 42500000 | tf_op jit(solution)/shard_map/pallas_call | solution.py:428
  947.1 60.0 %shard_map.243 = (bf16[2,512,1024]{2,1,0:T(8,128)(2,1)}, bf16[2,512,1024]{2,1,0:T(8,128)(2,1)}, bf16[2,512,1024]{2,1,0:T(8,128)(2,1)}, bf16[2,512,1024]{2,1,0:T(8,128)(2,1)}) custom-call(bf16[512,1024]{1,0:T(8,128)(2,1)} %reduce-scatter.15.cloned.1.call-done.refs_1_.refs_0_, bf16[512,1024]{1,0:T(8,128)(2,1)} %reduce-scatter.19.cloned.1.call-done.refs_1_, ...), custom_call_target="tpu_custom_call" | custom-call | bytes 42500000 | tf_op jit(solution)/shard_map/pallas_call | solution.py:428
  1014.5 10.0 shard_map.249
  1024.5 27.5 %shard_map.251 = (bf16[2,256,1024]{2,1,0:T(8,128)(2,1)}, bf16[2,256,1024]{2,1,0:T(8,128)(2,1)}, bf16[2,256,1024]{2,1,0:T(8,128)(2,1)}, bf16[2,256,1024]{2,1,0:T(8,128)(2,1)}) custom-call(bf16[256,1024]{1,0:T(8,128)(2,1)} %reduce-scatter.13.cloned.1.call-done.refs_4_.refs_0_, bf16[256,1024]{1,0:T(8,128)(2,1)} %reduce-scatter.21.cloned.1.call-done.refs_1_, ...), custom_call_target="tpu_custom_call" | custom-call | bytes 25500000 | tf_op jit(solution)/shard_map/pallas_call | solution.py:428
  1072.5 27.6 %shard_map.254 = (bf16[2,256,1024]{2,1,0:T(8,128)(2,1)}, bf16[2,256,1024]{2,1,0:T(8,128)(2,1)}, bf16[2,256,1024]{2,1,0:T(8,128)(2,1)}, bf16[2,256,1024]{2,1,0:T(8,128)(2,1)}) custom-call(bf16[256,1024]{1,0:T(8,128)(2,1)} %reduce-scatter.9.cloned.1.call-done.refs_2_.refs_0_, bf16[256,1024]{1,0:T(8,128)(2,1)} %slice.664.refs_1_, ...), custom_call_target="tpu_custom_call" | custom-call | bytes 25500000 | tf_op jit(solution)/shard_map/pallas_call | solution.py:428
  (812 shorter events, 478.1 us)
Async XLA Ops:
  7.2 62.8 %all-gather.11.cloned.1.call-start = ((), (), s32[]{:S(2)}) async-start(), calls=%async_computation.16 | async-start | bytes 4718592 | tf_op jit(solution)/shard_map/all_gather | solution.py:1256
  10.3 143.7 %all-gather.13.cloned.1.call-start = ((), (), s32[]{:S(2)}) async-start(), calls=%async_computation.17 | async-start | bytes 9437184 | tf_op jit(solution)/shard_map/all_gather | solution.py:1256
  15.7 41.0 %collective-permute-start.3 = (bf16[512,1024]{1,0:T(8,128)(2,1)}, bf16[512,1024]{1,0:T(8,128)(2,1)}, u32[]{:S(2)}, u32[]{:S(2)}) collective-permute-start(bf16[512,1024]{1,0:T(8,128)(2,1)} %pad_maximum_fusion.5), channel_id=1, source_target_pairs={{0,16},{16,0},{1,17},{17,1},{2,18},{18,2},{3,19},{19,3},{4,20},{20... | collective-permute-start | bytes 3145736 | tf_op jit(solution)/shard_map/ppermute | solution.py:1003
  73.4 236.0 %all-gather.15.cloned.1.call-start = ((), (), s32[]{:S(2)}) async-start(), calls=%async_computation.18 | async-start | bytes 18874368 | tf_op jit(solution)/shard_map/all_gather | solution.py:1256
  87.6 35.8 %collective-permute-start.5 = (bf16[768,1024]{1,0:T(8,128)(2,1)S(1)}, bf16[768,1024]{1,0:T(8,128)(2,1)S(1)}, u32[]{:S(2)}, u32[]{:S(2)}) collective-permute-start(bf16[768,1024]{1,0:T(8,128)(2,1)S(1)} %pad_maximum_fusion.2), channel_id=1, source_target_pairs={{0,16},{16,0},{1,17},{17,1},{2,18},{18,2},{3,19},{19,3},{4,20},{20... | collective-permute-start | bytes 4718600 | tf_op jit(solution)/shard_map/ppermute | solution.py:1003
  159.6 255.5 %all-gather.17.cloned.1.call-start = ((), (), s32[]{:S(2)}) async-start(), calls=%async_computation.19 | async-start | bytes 9437184 | tf_op jit(solution)/shard_map/all_gather | solution.py:1256
  198.8 310.3 %all-gather.19.cloned.1.call-start = ((), (), s32[]{:S(2)}) async-start(), calls=%async_computation.20 | async-start | bytes 14155776 | tf_op jit(solution)/shard_map/all_gather | solution.py:1256
  352.4 214.9 %reduce-scatter.9.cloned.1.call-start = ((), (), s32[]{:S(2)}) async-start(), calls=%async_computation.8 | async-start | bytes 2621440 | tf_op jit(solution)/shard_map/reduce_scatter | solution.py:1089
  369.0 148.6 %collective-permute-start.13 = (bf16[256,1024]{1,0:T(8,128)(2,1)}, bf16[256,1024]{1,0:T(8,128)(2,1)}, u32[]{:S(2)}, u32[]{:S(2)}) collective-permute-start(bf16[256,1024]{1,0:T(8,128)(2,1)} %get-tuple-element.283), channel_id=1, source_target_pairs={{0,4},{4,0},{1,5},{5,1},{2,6},{6,2},{3,7},{7,3},{8,12},{12,8},{9,1... | collective-permute-start | bytes 1572872 | tf_op jit(solution)/shard_map/ppermute | solution.py:1003
  525.0 121.4 %reduce-scatter.11.cloned.1.call-start = ((), (), s32[]{:S(2)}) async-start(), calls=%async_computation.9 | async-start | bytes 5242880 | tf_op jit(solution)/shard_map/reduce_scatter | solution.py:1089
  525.0 24.5 %collective-permute-start.14 = (bf16[256,2048]{1,0:T(8,128)(2,1)S(1)}, bf16[256,2048]{1,0:T(8,128)(2,1)S(1)}, u32[]{:S(2)}, u32[]{:S(2)}) collective-permute-start(bf16[256,2048]{1,0:T(8,128)(2,1)S(1)} %get-tuple-element.96.refs_0_), channel_id=1, source_target_pairs={{0,4},{4,0},{1,5},{5,1},{2,6},{6,2},{3,7},{7,3},{8,12},{12,8},{9,1... | collective-permute-start | bytes 3145736 | tf_op jit(solution)/shard_map/ppermute | solution.py:1003
  567.2 126.3 %reduce-scatter.13.cloned.1.call-start = ((), (), s32[]{:S(2)}) async-start(), calls=%async_computation.10 | async-start | bytes 2621440 | tf_op jit(solution)/shard_map/reduce_scatter | solution.py:1089
  602.6 26.9 %collective-permute-start.18 = (bf16[256,1024]{1,0:T(8,128)(2,1)S(1)}, bf16[256,1024]{1,0:T(8,128)(2,1)S(1)}, u32[]{:S(2)}, u32[]{:S(2)}) collective-permute-start(bf16[256,1024]{1,0:T(8,128)(2,1)S(1)} %get-tuple-element.278), channel_id=1, source_target_pairs={{0,4},{4,0},{1,5},{5,1},{2,6},{6,2},{3,7},{7,3},{8,12},{12,8},{9,1... | collective-permute-start | bytes 1572872 | tf_op jit(solution)/shard_map/ppermute | solution.py:1003
  646.4 128.6 %reduce-scatter.15.cloned.1.call-start = ((), (), s32[]{:S(2)}) async-start(), calls=%async_computation.11 | async-start | bytes 5242880 | tf_op jit(solution)/shard_map/reduce_scatter | solution.py:1089
  647.8 25.9 %collective-permute-start.19 = (bf16[256,2048]{1,0:T(8,128)(2,1)S(1)}, bf16[256,2048]{1,0:T(8,128)(2,1)S(1)}, u32[]{:S(2)}, u32[]{:S(2)}) collective-permute-start(bf16[256,2048]{1,0:T(8,128)(2,1)S(1)} %copy-done.41), channel_id=1, source_target_pairs={{0,4},{4,0},{1,5},{5,1},{2,6},{6,2},{3,7},{7,3},{8,12},{12,8},{9,1... | collective-permute-start | bytes 3145736 | tf_op jit(solution)/shard_map/ppermute | solution.py:1003
  693.6 162.4 %reduce-scatter.17.cloned.1.call-start = ((), (), s32[]{:S(2)}) async-start(), calls=%async_computation.12 | async-start | bytes 5242880 | tf_op jit(solution)/shard_map/reduce_scatter | solution.py:1089
  693.7 71.9 %collective-permute-start.28 = (bf16[256,2048]{1,0:T(8,128)(2,1)}, bf16[256,2048]{1,0:T(8,128)(2,1)S(1)}, u32[]{:S(2)}, u32[]{:S(2)}) collective-permute-start(bf16[256,2048]{1,0:T(8,128)(2,1)} %get-tuple-element.91.refs_0_), channel_id=1, source_target_pairs={{0,4},{4,0},{1,5},{5,1},{2,6},{6,2},{3,7},{7,3},{8,12},{12,8},{9,1... | collective-permute-start | bytes 3145736 | tf_op jit(solution)/shard_map/ppermute | solution.py:1003
  732.4 33.2 %collective-permute-start.29 = (bf16[256,1024]{1,0:T(8,128)(2,1)S(1)}, bf16[256,1024]{1,0:T(8,128)(2,1)S(1)}, u32[]{:S(2)}, u32[]{:S(2)}) collective-permute-start(bf16[256,1024]{1,0:T(8,128)(2,1)S(1)} %get-tuple-element.212), channel_id=1, source_target_pairs={{0,4},{4,0},{1,5},{5,1},{2,6},{6,2},{3,7},{7,3},{8,12},{12,8},{9,1... | collective-permute-start | bytes 1572872 | tf_op jit(solution)/shard_map/ppermute | solution.py:1003
  775.0 158.0 %reduce-scatter.19.cloned.1.call-start = ((), (), s32[]{:S(2)}) async-start(), calls=%async_computation.13 | async-start | bytes 5242880 | tf_op jit(solution)/shard_map/reduce_scatter | solution.py:1089
  777.6 69.4 %collective-permute-start.26 = (bf16[256,2048]{1,0:T(8,128)(2,1)}, bf16[256,2048]{1,0:T(8,128)(2,1)}, u32[]{:S(2)}, u32[]{:S(2)}) collective-permute-start(bf16[256,2048]{1,0:T(8,128)(2,1)} %multiply_convert_fusion.2.refs_0_), channel_id=1, source_target_pairs={{0,4},{4,0},{1,5},{5,1},{2,6},{6,2},{3,7},{7,3},{8,12},{12,8},{9,1... | collective-permute-start | bytes 3145736 | tf_op jit(solution)/shard_map/ppermute | solution.py:1003
  856.0 155.5 %reduce-scatter.21.cloned.1.call-start = ((), (), s32[]{:S(2)}) async-start(), calls=%async_computation.14 | async-start | bytes 2621440 | tf_op jit(solution)/shard_map/reduce_scatter | solution.py:1089
  858.6 67.8 %collective-permute-start.31 = (bf16[256,1024]{1,0:T(8,128)(2,1)}, bf16[256,1024]{1,0:T(8,128)(2,1)S(1)}, u32[]{:S(2)}, u32[]{:S(2)}) collective-permute-start(bf16[256,1024]{1,0:T(8,128)(2,1)} %get-tuple-element.268), channel_id=1, source_target_pairs={{0,4},{4,0},{1,5},{5,1},{2,6},{6,2},{3,7},{7,3},{8,12},{12,8},{9,1... | collective-permute-start | bytes 1572872 | tf_op jit(solution)/shard_map/ppermute | solution.py:1003
  858.6 67.7 %collective-permute-start.30 = (bf16[256,1024]{1,0:T(8,128)(2,1)}, bf16[256,1024]{1,0:T(8,128)(2,1)S(1)}, u32[]{:S(2)}, u32[]{:S(2)}) collective-permute-start(bf16[256,1024]{1,0:T(8,128)(2,1)} %get-tuple-element.218.refs_0_), channel_id=1, source_target_pairs={{0,4},{4,0},{1,5},{5,1},{2,6},{6,2},{3,7},{7,3},{8,12},{12,8},{9,1... | collective-permute-start | bytes 1572872 | tf_op jit(solution)/shard_map/ppermute | solution.py:1003
  933.1 128.6 %reduce-scatter.23.cloned.1.call-start = ((), (), s32[]{:S(2)}) async-start(), calls=%async_computation.15 | async-start | bytes 2949120 | tf_op jit(solution)/shard_map/reduce_scatter | solution.py:1089
  (216 other events, 1240.4 us)
Sparse Core Ops, SparseCore 0:
  10.4 59.5 all-gather.10
  73.5 80.3 all-gather.12
  159.7 149.6 all-gather.14
  311.4 80.2 all-gather.16
  393.7 115.2 all-gather.18
  525.1 42.0 reduce-scatter.8
  570.2 76.1 reduce-scatter.10
  649.2 44.3 reduce-scatter.12
  696.6 76.0 reduce-scatter.14
  775.4 77.2 reduce-scatter.16
  856.2 76.7 reduce-scatter.18
  935.7 44.3 reduce-scatter.20
  1011.7 46.8 reduce-scatter.22

commit v5 on v4

--- a/solution.py
+++ b/solution.py
@@ -1071,7 +1071,7 @@
     return a, b
 
 
-def layer_backward(grad, given, kept, weights, small, queue, layer, tables, first=()):
+def layer_backward(grad, given, kept, weights, small, queue, layer, tables, first=(), earlier=None):
     s, y = lax.axis_index("section"), lax.axis_index("y")
     core = lax.axis_index("core")
     length = grad.shape[0]
@@ -1125,8 +1125,7 @@
     message, d_right, d_x, d_raw, head_sums, lane_sums = mixer_back(
         got, kept, small, overlap, tables
     )
-    if layer == 1:
-        reduce("out1", product(kept["mo"], (b0, b1), message))
+    out_block = product(kept["mo"], (b0, b1), message) if layer == 1 else None
     back = swap(message, None, due("scan"))
     d_left, grad_conv = conv_back(back, d_x, kept["xbc"], small["conv"], tables)
     part = dot_t(d_left, win[0]) + dot_t(d_right, win[1]) + dot_t(d_raw, weights["dt"])
@@ -1144,14 +1143,19 @@
         got_gu = share(queue["gu1"], queue["gu0"], 50, (entering_grad,))
         place = jnp.stack([y, core]).astype(jnp.int32)
         got_gu = spread_gate_up(place, got_gu, lax.axis_size("fsdp"))
-        reduce("out0", product(kept["mo"], (b0, b1), got_gu, down_block))
+        nz = lax.axis_size("fsdp")
+        out_block = product(kept["mo"], (b0, b1), got_gu, down_block)
+        both = [block.reshape(nz, -1, HALF) for block in (earlier, out_block)]
+        reduce("outs", jnp.concatenate(both, axis=1).reshape(-1, HALF))
     grad_dt_w = t_dot(d_raw[:, :16], kept["x1"])
     smalls_grad = (head_sums, lane_sums, grad_conv, grad_gain0, grad_gain1, grad_dt_w)
-    return entering_grad, smalls_grad, (down_block, reduce, got_gu)
+    return entering_grad, smalls_grad, (
+        out_block if layer == 1 else (down_block, reduce, got_gu)
+    )
 
 
 WAITS = (
-    {"mlp": ("out1",), "scan": ("in1",)},
+    {"scan": ("in1",)},
     {"norm": ("down1",), "in": ("gu1",)},
 )
 
@@ -1333,7 +1337,7 @@
         kept.append(keep)
     tables = rotation_tables(length)
     grads = [None, None]
-    smalls_grad, queue = [None, None], {}
+    smalls_grad, queue, blocks = [None, None], {}, None
     for layer in (1, 0):
         grad, smalls_grad[layer], blocks = layer_backward(
             grad,
@@ -1345,6 +1349,7 @@
             layer,
             tables,
             (outs[1],) if layer == 1 else (),
+            blocks,
         )
         grads[layer] = grad
 
@@ -1382,7 +1387,10 @@
 
     place = jnp.stack([y, core]).astype(jnp.int32)
     grad_w_gu = got_gu
-    got_out = share(queue["out1"], queue["out0"], 30, (got_in[0],))
+    half_rows = queue["outs"].shape[0] // 2
+    got_out = share(
+        queue["outs"][:half_rows], queue["outs"][half_rows:], 30, (got_in[0],)
+    )
     shared = swap(extra).astype(F32)
     grad_w_in, grad_w_qkv = spread_in(place, got_in)
     got_down = share(queue["down1"], down0, 30, (grad_w_in,))

time: 1130 us -> 1110 us (0.982)
  waiting for transfers between devices: 217 us -> 195 us
    reduce_scatter x8 -> x7, waiting for transfers between devices: 30.3 us -> 7.82 us  [reduce(): lax.psum_scatter(block, 'fsdp', scatter_dimension=0, tiled=True)]
    unnamed x402 -> x396, local copies, waits for them, and re-layouts: 39.7 us -> 39.8 us
  transfers between devices with their start and end apart: 45 -> 44, of which waited for: 14 -> 11; matrix products, arithmetic and copies ran while one was open for 18% -> 19% of each run, Pallas kernels for 47% -> 48%
where the time goes in v5:
time: 1110 us; the launch traced here: 1100 us
  Pallas kernels  580 us (52%)
  waiting for transfers between devices  195 us (18%)
  local copies, waits for them, and re-layouts  103 us (9%)
  matrix products  80.8 us (7%)
  other arithmetic  67.5 us (6%)
  blocking collectives  35.2 us (3%)
  starting transfers between devices  21.9 us (2%)
  between operations  18 us (2%)
    pallas_call x8, Pallas kernels, rank_call(): pl.pallas_call(ignoring(kernel, len(args), len(after)), out_shape=out_sha...  201 us
    pallas_call x4, Pallas kernels, share(): pl.pallas_call(ignoring(share_kernel, 2, len(after)), out_shape=[shape] *...  165 us
    all_gather x5, waiting for transfers between devices, gather(): order.append(lax.all_gather(in_turn(piece), ('core', 'fsdp'), axis=0))  121 us
    pallas_call x9, Pallas kernels, swap(): pl.pallas_call(ignoring(functools.partial(swap_kernel, stat is not None),...  79.3 us
    pallas_call x8, Pallas kernels, outer_sum(): pl.pallas_call(ignoring(product_kernel, 4, len(tokens)), grid=(width // t...  52.2 us
    ppermute x22, waiting for transfers between devices, flip(): return lax.ppermute(value, axis, [(0, 1), (1, 0)])  46.2 us
    unnamed x396, local copies, waits for them, and re-layouts  39.8 us
    dot_general x20, matrix products, dot_t(): lax.dot_general(left, right, (((1,), (1,)), ((), ())), preferred_element_...  35.2 us
  transfers between devices with their start and end apart: 44, of which 11 were waited for; matrix products, arithmetic and copies ran while one was open for 19% of the time, Pallas kernels for 48%

profile of v5, /device:TPU:0, one launch (start us, length us, event | category | flops | bytes accessed | tf_op | source)
XLA Modules:
  0.0 1101.6 jit_solution(6548584562642705316)
XLA Ops:
  20.1 35.2 %all_gather.33 = bf16[8,256,128]{2,1,0:T(8,128)(2,1)S(1)} all-gather(bf16[1,256,128]{2,1,0:T(8,128)(2,1)S(1)} %pad_bitcast_fusion), channel_id=1, replica_groups=mesh['section'=2,'y'=2,'core'=2,'fsdp'=4] {'section','fsdp'}, dimensions={0}, use_global_device_ids=true | all-gather | bytes 589824 | tf_op jit(solution)/shard_map/all_gather | solution.py:1189
  59.9 10.2 all-gather.11.cloned.1.call-done
  77.8 9.8 collective-permute-done.4
  88.7 34.7 %collective-permute-done.5 = bf16[768,1024]{1,0:T(8,128)(2,1)S(1)} collective-permute-done((bf16[768,1024]{1,0:T(8,128)(2,1)S(1)}, bf16[768,1024]{1,0:T(8,128)(2,1)S(1)}, u32[]{:S(2)}, u32[]{:S(2)}) %collective-permute-start.5) | collective-permute-done | bytes 1572896 | tf_op jit(solution)/shard_map/ppermute | solution.py:1003
  129.0 24.9 %all-gather.13.cloned.1.call-done = bf16[4096,1024]{1,0:T(8,128)(2,1)} async-done(((bf16[512,1024]{1,0:T(8,128)(2,1)}), bf16[4096,1024]{1,0:T(8,128)(2,1)}) %all-gather.13.cloned.1.call-update) | async-done | bytes 8388624 | tf_op jit(solution)/shard_map/all_gather | solution.py:1260
  164.9 10.0 collective-permute-done.1
  238.9 70.5 %all-gather.15.cloned.1.call-done = bf16[8192,1024]{1,0:T(8,128)(2,1)} async-done(((bf16[1024,1024]{1,0:T(8,128)(2,1)}), bf16[8192,1024]{1,0:T(8,128)(2,1)}) %all-gather.15.cloned.1.call-update) | async-done | bytes 16777232 | tf_op jit(solution)/shard_map/all_gather | solution.py:1260
  317.5 29.5 %shard_map.215 = (f32[64,2048]{1,0:T(8,128)S(1)}, bf16[256,2048]{1,0:T(8,128)(2,1)}) custom-call(bf16[256,2048]{1,0:T(8,128)(2,1)S(1)} %pad_maximum_fusion.7.part_ref, bf16[64,2048]{1,0:T(8,128)(2,1)S(1)} %get-tuple-element.214.resid_ref, f32[1,2048]{1,0:T(1,128)S(1)} %bitcast.426), custom_call_target="tpu_custom_call" | custom-call | bytes 22950000 | tf_op jit(solution)/shard_map/pallas_call | solution.py:256
  386.7 27.7 %shard_map.216 = bf16[256,2048]{1,0:T(8,128)(2,1)S(1)} custom-call(bf16[256,2048]{1,0:T(8,128)(2,1)S(1)} %pad_maximum_fusion.8.part_ref, f32[64,2048]{1,0:T(8,128)S(1)} %copy-done.4), custom_call_target="tpu_custom_call" | custom-call | bytes 22950000 | tf_op jit(solution)/shard_map/pallas_call | solution.py:256
  466.0 27.3 %shard_map.220 = (f32[64,2048]{1,0:T(8,128)S(1)}, bf16[256,2048]{1,0:T(8,128)(2,1)S(1)}) custom-call(bf16[256,2048]{1,0:T(8,128)(2,1)S(1)} %pad_maximum_fusion.9.part_ref, bf16[64,2048]{1,0:T(8,128)(2,1)S(1)} %get-tuple-element.221.resid_ref, f32[1,2048]{1,0:T(1,128)S(1)} %bitcast.428), custom_call_target="tpu_custom_call" | custom-call | bytes 22950000 | tf_op jit(solution)/shard_map/pallas_call | solution.py:256
  493.3 15.7 %all-gather.19.cloned.1.call-done = bf16[6144,1024]{1,0:T(8,128)(2,1)} async-done(((bf16[768,1024]{1,0:T(8,128)(2,1)}), bf16[6144,1024]{1,0:T(8,128)(2,1)}) %all-gather.19.cloned.1.call-update) | async-done | bytes 12582928 | tf_op jit(solution)/shard_map/all_gather | solution.py:1260
  532.9 15.1 %shard_map.222.refs_4_ = bf16[64,2048]{1,0:T(8,128)(2,1)S(1)} custom-call(bf16[256,2048]{1,0:T(8,128)(2,1)S(1)} %pad_maximum_fusion.10.part_ref, f32[64,2048]{1,0:T(8,128)S(1)} %get-tuple-element.97.resid_ref.refs_2_), custom_call_target="tpu_custom_call" | custom-call | bytes 22950000 | tf_op jit(solution)/shard_map/pallas_call | solution.py:256
  580.7 28.9 %shard_map.223 = (f32[64,2048]{1,0:T(8,128)S(1)}, bf16[256,2048]{1,0:T(8,128)(2,1)S(1)}, f32[1,2048]{1,0:T(1,128)S(1)}) custom-call(bf16[256,2048]{1,0:T(8,128)(2,1)S(1)} %fusion.24.refs_0_, f32[64,2048]{1,0:T(8,128)S(1)} %dynamic-slice_convert_fusion.1.refs_1_, f32[64,2048]{1,0:T(8,128)S(1)} %get-tuple-element.97.resid_ref.refs_2_, ...), custom_call_target="tpu_custom_call" | custom-call | bytes 22950000 | tf_op jit(solution)/shard_map/pallas_call | solution.py:256
  612.1 9.7 shard_map.225
  670.1 29.8 %shard_map.230 = (f32[64,2048]{1,0:T(8,128)}, bf16[256,2048]{1,0:T(8,128)(2,1)S(1)}, f32[1,2048]{1,0:T(1,128)S(1)}) custom-call(bf16[256,2048]{1,0:T(8,128)(2,1)S(1)} %copy-done.2, f32[64,2048]{1,0:T(8,128)S(1)} %copy-done.26, f32[64,2048]{1,0:T(8,128)S(1)} %copy-done.18, f32[1,2048]{1,0:T(1,128)S(1)} %bitcast.431, bf16[512,1024]{1,0:T(8,128)(2,1)S(1)} %copy-done.9), custom_call_target="tpu_custom_call" | custom-call | bytes 22950000 | tf_op jit(solution)/shard_map/pallas_call | solution.py:256
  707.5 27.2 %shard_map.231 = (f32[64,2048]{1,0:T(8,128)S(1)}, bf16[256,2048]{1,0:T(8,128)(2,1)S(1)}, f32[1,2048]{1,0:T(1,128)S(1)}) custom-call(bf16[256,2048]{1,0:T(8,128)(2,1)S(1)} %fusion.25.part_ref, f32[64,2048]{1,0:T(8,128)S(1)} %dynamic-slice_convert_fusion.given_ref, f32[64,2048]{1,0:T(8,128)S(1)} %copy-done.5, f32[1,2048]{1,0:T(1,128)S(1)} %bitcast.427), custom_call_target="tpu_custom_call" | custom-call | bytes 22950000 | tf_op jit(solution)/shard_map/pallas_call | solution.py:256
  759.2 9.9 shard_map.232
  803.7 15.3 %shard_map.237 = (bf16[64,2048]{1,0:T(8,128)(2,1)S(1)}, f32[1,2048]{1,0:T(1,128)S(1)}) custom-call(bf16[256,2048]{1,0:T(8,128)(2,1)S(1)} %fusion.27.part_ref, f32[64,2048]{1,0:T(8,128)S(1)} %copy-done.24, f32[64,2048]{1,0:T(8,128)S(1)} %copy-done.17, f32[1,2048]{1,0:T(1,128)S(1)} %bitcast.430), custom_call_target="tpu_custom_call" | custom-call | bytes 22950000 | tf_op jit(solution)/shard_map/pallas_call | solution.py:256
  846.5 51.1 %shard_map.245 = (bf16[2,512,1024]{2,1,0:T(8,128)(2,1)}, bf16[2,512,1024]{2,1,0:T(8,128)(2,1)}, bf16[2,512,1024]{2,1,0:T(8,128)(2,1)}, bf16[2,512,1024]{2,1,0:T(8,128)(2,1)}) custom-call(bf16[512,1024]{1,0:T(8,128)(2,1)} %reduce-scatter.10.cloned.1.call-done.refs_4_.refs_0_, bf16[512,1024]{1,0:T(8,128)(2,1)} %reduce-scatter.14.cloned.1.call-done.refs_1_, ...), custom_call_target="tpu_custom_call" | custom-call | bytes 42500000 | tf_op jit(solution)/shard_map/pallas_call | solution.py:428
  897.6 9.9 shard_map.246.refs_4_
  931.9 58.9 %shard_map.242 = (bf16[2,512,1024]{2,1,0:T(8,128)(2,1)}, bf16[2,512,1024]{2,1,0:T(8,128)(2,1)}, bf16[2,512,1024]{2,1,0:T(8,128)(2,1)}, bf16[2,512,1024]{2,1,0:T(8,128)(2,1)}) custom-call(bf16[512,1024]{1,0:T(8,128)(2,1)} %reduce-scatter.12.cloned.1.call-done.refs_1_.refs_0_, bf16[512,1024]{1,0:T(8,128)(2,1)} %reduce-scatter.16.cloned.1.call-done.refs_1_, ...), custom_call_target="tpu_custom_call" | custom-call | bytes 42500000 | tf_op jit(solution)/shard_map/pallas_call | solution.py:428
  998.1 10.1 shard_map.249
  1009.3 27.5 %shard_map.251 = (bf16[2,256,1024]{2,1,0:T(8,128)(2,1)}, bf16[2,256,1024]{2,1,0:T(8,128)(2,1)}, bf16[2,256,1024]{2,1,0:T(8,128)(2,1)}, bf16[2,256,1024]{2,1,0:T(8,128)(2,1)}) custom-call(bf16[256,1024]{1,0:T(8,128)(2,1)} %get-tuple-element.267.refs_0_, bf16[256,1024]{1,0:T(8,128)(2,1)} %get-tuple-element.266.refs_1_, ...), custom_call_target="tpu_custom_call" | custom-call | bytes 25500000 | tf_op jit(solution)/shard_map/pallas_call | solution.py:428
  1057.4 27.6 %shard_map.254 = (bf16[2,256,1024]{2,1,0:T(8,128)(2,1)}, bf16[2,256,1024]{2,1,0:T(8,128)(2,1)}, bf16[2,256,1024]{2,1,0:T(8,128)(2,1)}, bf16[2,256,1024]{2,1,0:T(8,128)(2,1)}) custom-call(bf16[256,1024]{1,0:T(8,128)(2,1)} %reduce-scatter.8.cloned.1.call-done.refs_2_.refs_0_, bf16[256,1024]{1,0:T(8,128)(2,1)} %slice.674.refs_1_, ...), custom_call_target="tpu_custom_call" | custom-call | bytes 25500000 | tf_op jit(solution)/shard_map/pallas_call | solution.py:428
  (805 shorter events, 467.1 us)
Async XLA Ops:
  7.2 62.8 %all-gather.11.cloned.1.call-start = ((), (), s32[]{:S(2)}) async-start(), calls=%async_computation.14 | async-start | bytes 4718592 | tf_op jit(solution)/shard_map/all_gather | solution.py:1260
  10.3 143.6 %all-gather.13.cloned.1.call-start = ((), (), s32[]{:S(2)}) async-start(), calls=%async_computation.15 | async-start | bytes 9437184 | tf_op jit(solution)/shard_map/all_gather | solution.py:1260
  15.7 41.0 %collective-permute-start.3 = (bf16[512,1024]{1,0:T(8,128)(2,1)}, bf16[512,1024]{1,0:T(8,128)(2,1)}, u32[]{:S(2)}, u32[]{:S(2)}) collective-permute-start(bf16[512,1024]{1,0:T(8,128)(2,1)} %pad_maximum_fusion.6), channel_id=1, source_target_pairs={{0,16},{16,0},{1,17},{17,1},{2,18},{18,2},{3,19},{19,3},{4,20},{20... | collective-permute-start | bytes 3145736 | tf_op jit(solution)/shard_map/ppermute | solution.py:1003
  73.4 236.0 %all-gather.15.cloned.1.call-start = ((), (), s32[]{:S(2)}) async-start(), calls=%async_computation.16 | async-start | bytes 18874368 | tf_op jit(solution)/shard_map/all_gather | solution.py:1260
  87.6 35.8 %collective-permute-start.5 = (bf16[768,1024]{1,0:T(8,128)(2,1)S(1)}, bf16[768,1024]{1,0:T(8,128)(2,1)S(1)}, u32[]{:S(2)}, u32[]{:S(2)}) collective-permute-start(bf16[768,1024]{1,0:T(8,128)(2,1)S(1)} %pad_maximum_fusion.3), channel_id=1, source_target_pairs={{0,16},{16,0},{1,17},{17,1},{2,18},{18,2},{3,19},{19,3},{4,20},{20... | collective-permute-start | bytes 4718600 | tf_op jit(solution)/shard_map/ppermute | solution.py:1003
  159.6 255.5 %all-gather.17.cloned.1.call-start = ((), (), s32[]{:S(2)}) async-start(), calls=%async_computation.17 | async-start | bytes 9437184 | tf_op jit(solution)/shard_map/all_gather | solution.py:1260
  198.8 310.2 %all-gather.19.cloned.1.call-start = ((), (), s32[]{:S(2)}) async-start(), calls=%async_computation.18 | async-start | bytes 14155776 | tf_op jit(solution)/shard_map/all_gather | solution.py:1260
  352.4 214.9 %reduce-scatter.8.cloned.1.call-start = ((), (), s32[]{:S(2)}) async-start(), calls=%async_computation.7 | async-start | bytes 2621440 | tf_op jit(solution)/shard_map/reduce_scatter | solution.py:1089
  369.1 148.6 %collective-permute-start.13 = (bf16[256,1024]{1,0:T(8,128)(2,1)}, bf16[256,1024]{1,0:T(8,128)(2,1)}, u32[]{:S(2)}, u32[]{:S(2)}) collective-permute-start(bf16[256,1024]{1,0:T(8,128)(2,1)} %get-tuple-element.283), channel_id=1, source_target_pairs={{0,4},{4,0},{1,5},{5,1},{2,6},{6,2},{3,7},{7,3},{8,12},{12,8},{9,1... | collective-permute-start | bytes 1572872 | tf_op jit(solution)/shard_map/ppermute | solution.py:1003
  525.0 140.6 %reduce-scatter.10.cloned.1.call-start = ((), (), s32[]{:S(2)}) async-start(), calls=%async_computation.8 | async-start | bytes 5242880 | tf_op jit(solution)/shard_map/reduce_scatter | solution.py:1089
  525.0 24.5 %collective-permute-start.14 = (bf16[256,2048]{1,0:T(8,128)(2,1)S(1)}, bf16[256,2048]{1,0:T(8,128)(2,1)S(1)}, u32[]{:S(2)}, u32[]{:S(2)}) collective-permute-start(bf16[256,2048]{1,0:T(8,128)(2,1)S(1)} %get-tuple-element.95.refs_0_), channel_id=1, source_target_pairs={{0,4},{4,0},{1,5},{5,1},{2,6},{6,2},{3,7},{7,3},{8,12},{12,8},{9,1... | collective-permute-start | bytes 3145736 | tf_op jit(solution)/shard_map/ppermute | solution.py:1003
  531.1 18.5 %collective-permute-start.15 = (bf16[256,1024]{1,0:T(8,128)(2,1)S(1)}, bf16[256,1024]{1,0:T(8,128)(2,1)S(1)}, u32[]{:S(2)}, u32[]{:S(2)}) collective-permute-start(bf16[256,1024]{1,0:T(8,128)(2,1)S(1)} %get-tuple-element.217), channel_id=1, source_target_pairs={{0,4},{4,0},{1,5},{5,1},{2,6},{6,2},{3,7},{7,3},{8,12},{12,8},{9,1... | collective-permute-start | bytes 1572872 | tf_op jit(solution)/shard_map/ppermute | solution.py:1003
  567.3 179.3 %reduce-scatter.12.cloned.1.call-start = ((), (), s32[]{:S(2)}) async-start(), calls=%async_computation.9 | async-start | bytes 5242880 | tf_op jit(solution)/shard_map/reduce_scatter | solution.py:1089
  572.2 84.4 %collective-permute-start.17 = (bf16[256,2048]{1,0:T(8,128)(2,1)}, bf16[256,2048]{1,0:T(8,128)(2,1)}, u32[]{:S(2)}, u32[]{:S(2)}) collective-permute-start(bf16[256,2048]{1,0:T(8,128)(2,1)} %copy-done.42), channel_id=1, source_target_pairs={{0,4},{4,0},{1,5},{5,1},{2,6},{6,2},{3,7},{7,3},{8,12},{12,8},{9,1... | collective-permute-start | bytes 3145736 | tf_op jit(solution)/shard_map/ppermute | solution.py:1003
  665.6 163.2 %reduce-scatter.14.cloned.1.call-start = ((), (), s32[]{:S(2)}) async-start(), calls=%async_computation.10 | async-start | bytes 5242880 | tf_op jit(solution)/shard_map/reduce_scatter | solution.py:1089
  666.2 71.0 %collective-permute-start.26 = (bf16[256,2048]{1,0:T(8,128)(2,1)}, bf16[256,2048]{1,0:T(8,128)(2,1)S(1)}, u32[]{:S(2)}, u32[]{:S(2)}) collective-permute-start(bf16[256,2048]{1,0:T(8,128)(2,1)} %get-tuple-element.90.refs_0_), channel_id=1, source_target_pairs={{0,4},{4,0},{1,5},{5,1},{2,6},{6,2},{3,7},{7,3},{8,12},{12,8},{9,1... | collective-permute-start | bytes 3145736 | tf_op jit(solution)/shard_map/ppermute | solution.py:1003
  705.2 32.1 %collective-permute-start.27 = (bf16[256,1024]{1,0:T(8,128)(2,1)S(1)}, bf16[256,1024]{1,0:T(8,128)(2,1)S(1)}, u32[]{:S(2)}, u32[]{:S(2)}) collective-permute-start(bf16[256,1024]{1,0:T(8,128)(2,1)S(1)} %get-tuple-element.210), channel_id=1, source_target_pairs={{0,4},{4,0},{1,5},{5,1},{2,6},{6,2},{3,7},{7,3},{8,12},{12,8},{9,1... | collective-permute-start | bytes 1572872 | tf_op jit(solution)/shard_map/ppermute | solution.py:1003
  746.6 170.8 %reduce-scatter.16.cloned.1.call-start = ((), (), s32[]{:S(2)}) async-start(), calls=%async_computation.11 | async-start | bytes 5242880 | tf_op jit(solution)/shard_map/reduce_scatter | solution.py:1089
  750.2 69.6 %collective-permute-start.24 = (bf16[256,2048]{1,0:T(8,128)(2,1)}, bf16[256,2048]{1,0:T(8,128)(2,1)}, u32[]{:S(2)}, u32[]{:S(2)}) collective-permute-start(bf16[256,2048]{1,0:T(8,128)(2,1)} %copy-done.40), channel_id=1, source_target_pairs={{0,4},{4,0},{1,5},{5,1},{2,6},{6,2},{3,7},{7,3},{8,12},{12,8},{9,1... | collective-permute-start | bytes 3145736 | tf_op jit(solution)/shard_map/ppermute | solution.py:1003
  799.0 20.8 %collective-permute-start.25 = (bf16[256,1024]{1,0:T(8,128)(2,1)S(1)}, bf16[256,1024]{1,0:T(8,128)(2,1)S(1)}, u32[]{:S(2)}, u32[]{:S(2)}) collective-permute-start(bf16[256,1024]{1,0:T(8,128)(2,1)S(1)} %get-tuple-element.274), channel_id=1, source_target_pairs={{0,4},{4,0},{1,5},{5,1},{2,6},{6,2},{3,7},{7,3},{8,12},{12,8},{9,1... | collective-permute-start | bytes 1572872 | tf_op jit(solution)/shard_map/ppermute | solution.py:1003
  828.8 166.4 %reduce-scatter.18.cloned.1.call-start = ((), (), s32[]{:S(2)}) async-start(), calls=%async_computation.12 | async-start | bytes 5242880 | tf_op jit(solution)/shard_map/reduce_scatter | solution.py:1089
  833.8 73.6 %collective-permute-start.31 = (bf16[256,1024]{1,0:T(8,128)(2,1)}, bf16[256,1024]{1,0:T(8,128)(2,1)S(1)}, u32[]{:S(2)}, u32[]{:S(2)}) collective-permute-start(bf16[256,1024]{1,0:T(8,128)(2,1)} %get-tuple-element.270), channel_id=1, source_target_pairs={{0,4},{4,0},{1,5},{5,1},{2,6},{6,2},{3,7},{7,3},{8,12},{12,8},{9,1... | collective-permute-start | bytes 1572872 | tf_op jit(solution)/shard_map/ppermute | solution.py:1003
  833.9 73.6 %collective-permute-start.30 = (bf16[256,1024]{1,0:T(8,128)(2,1)}, bf16[256,1024]{1,0:T(8,128)(2,1)S(1)}, u32[]{:S(2)}, u32[]{:S(2)}) collective-permute-start(bf16[256,1024]{1,0:T(8,128)(2,1)} %get-tuple-element.216.refs_0_), channel_id=1, source_target_pairs={{0,4},{4,0},{1,5},{5,1},{2,6},{6,2},{3,7},{7,3},{8,12},{12,8},{9,1... | collective-permute-start | bytes 1572872 | tf_op jit(solution)/shard_map/ppermute | solution.py:1003
  917.6 129.0 %reduce-scatter.20.cloned.1.call-start = ((), (), s32[]{:S(2)}) async-start(), calls=%async_computation.13 | async-start | bytes 2949120 | tf_op jit(solution)/shard_map/reduce_scatter | solution.py:1089
  (212 other events, 1263.9 us)
Sparse Core Ops, SparseCore 0:
  10.4 59.5 all-gather.10
  73.5 80.3 all-gather.12
  159.7 149.6 all-gather.14
  311.4 80.2 all-gather.16
  393.7 115.2 all-gather.18
  525.1 42.1 reduce-scatter.7
  570.2 76.0 reduce-scatter.9
  665.7 76.1 reduce-scatter.11
  746.7 76.4 reduce-scatter.13
  828.9 76.5 reduce-scatter.15
  917.6 75.7 reduce-scatter.17
  995.6 48.5 reduce-scatter.19

commit v6 on v5

--- a/solution.py
+++ b/solution.py
@@ -1186,10 +1186,13 @@
     )
     count = flat.shape[0]
     flat = jnp.pad(flat, (0, -count % 2048)).reshape(-1, 128)
-    everything = lax.all_gather(flat, ("section", "fsdp"), axis=0).reshape(2, nz, -1)[..., :count]
+    everything = lax.all_gather(flat, "fsdp", axis=0)
+    beyond = flip(everything, "section")
+    both = jnp.where(s == 0, jnp.stack([everything, beyond]), jnp.stack([beyond, everything]))
+    both = both.reshape(2, nz, -1)[..., :count]
 
     def unpack(layer):
-        part = everything[layer]
+        part = both[layer]
         sizes = [2 * D // nz, 3 * SSM_HEADS // nz, 5 * CONV_W // nz, D_SSM // nz]
         starts = [0]
         for size in sizes:

time: 1110 us -> 1110 us (level)
  blocking collectives: 35.2 us -> 16.9 us
  waiting for transfers between devices: 195 us -> 209 us
    all_gather x1, blocking collectives: 35.2 us -> 16.9 us  [body(): everything = lax.all_gather(flat, 'fsdp', axis=0)]
    ppermute x22 -> x23, waiting for transfers between devices: 46.2 us -> 55.6 us  [flip(): return lax.ppermute(value, axis, [(0, 1), (1, 0)])]
    unnamed x396 -> x390, local copies, waits for them, and re-layouts: 39.8 us -> 37.5 us
  transfers between devices with their start and end apart: 44 -> 45, of which waited for: 11 -> 13; matrix products, arithmetic and copies ran while one was open for 19% -> 19% of each run, Pallas kernels for 48% -> 48%
where the time goes in v6:
time: 1110 us; the launch traced here: 1100 us
  Pallas kernels  581 us (52%)
  waiting for transfers between devices  209 us (19%)
  local copies, waits for them, and re-layouts  101 us (9%)
  matrix products  81.2 us (7%)
  other arithmetic  67 us (6%)
  starting transfers between devices  23.4 us (2%)
  between operations  17.9 us (2%)
  blocking collectives  16.9 us (2%)
    pallas_call x8, Pallas kernels, rank_call(): pl.pallas_call(ignoring(kernel, len(args), len(after)), out_shape=out_sha...  201 us
    pallas_call x4, Pallas kernels, share(): pl.pallas_call(ignoring(share_kernel, 2, len(after)), out_shape=[shape] *...  165 us
    all_gather x5, waiting for transfers between devices, gather(): order.append(lax.all_gather(in_turn(piece), ('core', 'fsdp'), axis=0))  131 us
    pallas_call x9, Pallas kernels, swap(): pl.pallas_call(ignoring(functools.partial(swap_kernel, stat is not None),...  79.4 us
    ppermute x23, waiting for transfers between devices, flip(): return lax.ppermute(value, axis, [(0, 1), (1, 0)])  55.6 us
    pallas_call x8, Pallas kernels, outer_sum(): pl.pallas_call(ignoring(product_kernel, 4, len(tokens)), grid=(width // t...  52.1 us
    unnamed x390, local copies, waits for them, and re-layouts  37.5 us
    dot_general x20, matrix products, dot_t(): lax.dot_general(left, right, (((1,), (1,)), ((), ())), preferred_element_...  35.2 us
  transfers between devices with their start and end apart: 45, of which 13 were waited for; matrix products, arithmetic and copies ran while one was open for 19% of the time, Pallas kernels for 48%

profile of v6, /device:TPU:0, one launch (start us, length us, event | category | flops | bytes accessed | tf_op | source)
XLA Modules:
  0.0 1096.4 jit_solution(11453879874486025807)
XLA Ops:
  20.4 16.9 %all_gather.33.refs_1_ = bf16[4,256,128]{2,1,0:T(8,128)(2,1)} all-gather(bf16[1,256,128]{2,1,0:T(8,128)(2,1)S(1)} %pad_bitcast_fusion), channel_id=1, replica_groups=mesh['section'=2,'y'=2,'core'=2,'fsdp'=4] {'fsdp'}, dimensions={0}, use_global_device_ids=true | all-gather | bytes 327680 | tf_op jit(solution)/shard_map/all_gather | solution.py:1189
  45.2 19.3 %all-gather.11.cloned.1.call-done = bf16[2048,1024]{1,0:T(8,128)(2,1)} async-done(((bf16[256,1024]{1,0:T(8,128)(2,1)}), bf16[2048,1024]{1,0:T(8,128)(2,1)}) %all-gather.11.cloned.1.call-update) | async-done | bytes 4194320 | tf_op jit(solution)/shard_map/all_gather | solution.py:1263
  72.3 9.9 collective-permute-done.5
  83.2 34.8 %collective-permute-done.6 = bf16[768,1024]{1,0:T(8,128)(2,1)S(1)} collective-permute-done((bf16[768,1024]{1,0:T(8,128)(2,1)S(1)}, bf16[768,1024]{1,0:T(8,128)(2,1)S(1)}, u32[]{:S(2)}, u32[]{:S(2)}) %collective-permute-start.6) | collective-permute-done | bytes 1572896 | tf_op jit(solution)/shard_map/ppermute | solution.py:1003
  123.6 25.1 %all-gather.13.cloned.1.call-done = bf16[4096,1024]{1,0:T(8,128)(2,1)} async-done(((bf16[512,1024]{1,0:T(8,128)(2,1)}), bf16[4096,1024]{1,0:T(8,128)(2,1)}) %all-gather.13.cloned.1.call-update) | async-done | bytes 8388624 | tf_op jit(solution)/shard_map/all_gather | solution.py:1263
  231.4 72.7 %all-gather.15.cloned.1.call-done = bf16[8192,1024]{1,0:T(8,128)(2,1)} async-done(((bf16[1024,1024]{1,0:T(8,128)(2,1)}), bf16[8192,1024]{1,0:T(8,128)(2,1)}) %all-gather.15.cloned.1.call-update) | async-done | bytes 16777232 | tf_op jit(solution)/shard_map/all_gather | solution.py:1263
  312.2 29.5 %shard_map.215 = (f32[64,2048]{1,0:T(8,128)S(1)}, bf16[256,2048]{1,0:T(8,128)(2,1)}) custom-call(bf16[256,2048]{1,0:T(8,128)(2,1)S(1)} %pad_maximum_fusion.7.part_ref, bf16[64,2048]{1,0:T(8,128)(2,1)S(1)} %get-tuple-element.226.resid_ref, f32[1,2048]{1,0:T(1,128)S(1)} %bitcast.426), custom_call_target="tpu_custom_call" | custom-call | bytes 22950000 | tf_op jit(solution)/shard_map/pallas_call | solution.py:256
  351.5 10.2 collective-permute-done.11
  382.9 27.9 %shard_map.216 = bf16[256,2048]{1,0:T(8,128)(2,1)S(1)} custom-call(bf16[256,2048]{1,0:T(8,128)(2,1)S(1)} %pad_maximum_fusion.8.part_ref, f32[64,2048]{1,0:T(8,128)S(1)} %copy-done.4), custom_call_target="tpu_custom_call" | custom-call | bytes 22950000 | tf_op jit(solution)/shard_map/pallas_call | solution.py:256
  462.4 27.3 %shard_map.220 = (f32[64,2048]{1,0:T(8,128)S(1)}, bf16[256,2048]{1,0:T(8,128)(2,1)S(1)}) custom-call(bf16[256,2048]{1,0:T(8,128)(2,1)S(1)} %pad_maximum_fusion.9.part_ref, bf16[64,2048]{1,0:T(8,128)(2,1)S(1)} %get-tuple-element.233.resid_ref, f32[1,2048]{1,0:T(1,128)S(1)} %bitcast.428), custom_call_target="tpu_custom_call" | custom-call | bytes 22950000 | tf_op jit(solution)/shard_map/pallas_call | solution.py:256
  489.8 14.1 %all-gather.19.cloned.1.call-done = bf16[6144,1024]{1,0:T(8,128)(2,1)} async-done(((bf16[768,1024]{1,0:T(8,128)(2,1)}), bf16[6144,1024]{1,0:T(8,128)(2,1)}) %all-gather.19.cloned.1.call-update) | async-done | bytes 12582928 | tf_op jit(solution)/shard_map/all_gather | solution.py:1263
  527.6 15.1 %shard_map.222.refs_4_ = bf16[64,2048]{1,0:T(8,128)(2,1)S(1)} custom-call(bf16[256,2048]{1,0:T(8,128)(2,1)S(1)} %pad_maximum_fusion.10.part_ref, f32[64,2048]{1,0:T(8,128)S(1)} %get-tuple-element.97.resid_ref.refs_2_), custom_call_target="tpu_custom_call" | custom-call | bytes 22950000 | tf_op jit(solution)/shard_map/pallas_call | solution.py:256
  575.5 28.9 %shard_map.223 = (f32[64,2048]{1,0:T(8,128)S(1)}, bf16[256,2048]{1,0:T(8,128)(2,1)S(1)}, f32[1,2048]{1,0:T(1,128)S(1)}) custom-call(bf16[256,2048]{1,0:T(8,128)(2,1)S(1)} %fusion.24.refs_0_, f32[64,2048]{1,0:T(8,128)S(1)} %dynamic-slice_convert_fusion.1.refs_1_, f32[64,2048]{1,0:T(8,128)S(1)} %get-tuple-element.97.resid_ref.refs_2_, ...), custom_call_target="tpu_custom_call" | custom-call | bytes 22950000 | tf_op jit(solution)/shard_map/pallas_call | solution.py:256
  606.9 9.7 shard_map.225
  664.9 29.7 %shard_map.230 = (f32[64,2048]{1,0:T(8,128)}, bf16[256,2048]{1,0:T(8,128)(2,1)S(1)}, f32[1,2048]{1,0:T(1,128)S(1)}) custom-call(bf16[256,2048]{1,0:T(8,128)(2,1)S(1)} %copy-done.2, f32[64,2048]{1,0:T(8,128)S(1)} %copy-done.26, f32[64,2048]{1,0:T(8,128)S(1)} %copy-done.18, f32[1,2048]{1,0:T(1,128)S(1)} %bitcast.431, bf16[512,1024]{1,0:T(8,128)(2,1)S(1)} %copy-done.9), custom_call_target="tpu_custom_call" | custom-call | bytes 22950000 | tf_op jit(solution)/shard_map/pallas_call | solution.py:256
  702.3 27.1 %shard_map.231 = (f32[64,2048]{1,0:T(8,128)S(1)}, bf16[256,2048]{1,0:T(8,128)(2,1)S(1)}, f32[1,2048]{1,0:T(1,128)S(1)}) custom-call(bf16[256,2048]{1,0:T(8,128)(2,1)S(1)} %fusion.25.part_ref, f32[64,2048]{1,0:T(8,128)S(1)} %dynamic-slice_convert_fusion.given_ref, f32[64,2048]{1,0:T(8,128)S(1)} %copy-done.5, f32[1,2048]{1,0:T(1,128)S(1)} %bitcast.427), custom_call_target="tpu_custom_call" | custom-call | bytes 22950000 | tf_op jit(solution)/shard_map/pallas_call | solution.py:256
  753.9 9.9 shard_map.232
  798.5 15.3 %shard_map.237 = (bf16[64,2048]{1,0:T(8,128)(2,1)S(1)}, f32[1,2048]{1,0:T(1,128)S(1)}) custom-call(bf16[256,2048]{1,0:T(8,128)(2,1)S(1)} %fusion.27.part_ref, f32[64,2048]{1,0:T(8,128)S(1)} %copy-done.24, f32[64,2048]{1,0:T(8,128)S(1)} %copy-done.17, f32[1,2048]{1,0:T(1,128)S(1)} %bitcast.430), custom_call_target="tpu_custom_call" | custom-call | bytes 22950000 | tf_op jit(solution)/shard_map/pallas_call | solution.py:256
  841.2 51.1 %shard_map.245 = (bf16[2,512,1024]{2,1,0:T(8,128)(2,1)}, bf16[2,512,1024]{2,1,0:T(8,128)(2,1)}, bf16[2,512,1024]{2,1,0:T(8,128)(2,1)}, bf16[2,512,1024]{2,1,0:T(8,128)(2,1)}) custom-call(bf16[512,1024]{1,0:T(8,128)(2,1)} %reduce-scatter.10.cloned.1.call-done.refs_4_.refs_0_, bf16[512,1024]{1,0:T(8,128)(2,1)} %reduce-scatter.14.cloned.1.call-done.refs_1_, ...), custom_call_target="tpu_custom_call" | custom-call | bytes 42500000 | tf_op jit(solution)/shard_map/pallas_call | solution.py:428
  892.4 9.9 shard_map.246.refs_4_
  926.7 58.9 %shard_map.242 = (bf16[2,512,1024]{2,1,0:T(8,128)(2,1)}, bf16[2,512,1024]{2,1,0:T(8,128)(2,1)}, bf16[2,512,1024]{2,1,0:T(8,128)(2,1)}, bf16[2,512,1024]{2,1,0:T(8,128)(2,1)}) custom-call(bf16[512,1024]{1,0:T(8,128)(2,1)} %reduce-scatter.12.cloned.1.call-done.refs_1_.refs_0_, bf16[512,1024]{1,0:T(8,128)(2,1)} %reduce-scatter.16.cloned.1.call-done.refs_1_, ...), custom_call_target="tpu_custom_call" | custom-call | bytes 42500000 | tf_op jit(solution)/shard_map/pallas_call | solution.py:428
  992.9 10.1 shard_map.249
  1004.0 27.6 %shard_map.251 = (bf16[2,256,1024]{2,1,0:T(8,128)(2,1)}, bf16[2,256,1024]{2,1,0:T(8,128)(2,1)}, bf16[2,256,1024]{2,1,0:T(8,128)(2,1)}, bf16[2,256,1024]{2,1,0:T(8,128)(2,1)}) custom-call(bf16[256,1024]{1,0:T(8,128)(2,1)} %get-tuple-element.279.refs_0_, bf16[256,1024]{1,0:T(8,128)(2,1)} %get-tuple-element.278.refs_1_, ...), custom_call_target="tpu_custom_call" | custom-call | bytes 25500000 | tf_op jit(solution)/shard_map/pallas_call | solution.py:428
  1052.2 27.6 %shard_map.254 = (bf16[2,256,1024]{2,1,0:T(8,128)(2,1)}, bf16[2,256,1024]{2,1,0:T(8,128)(2,1)}, bf16[2,256,1024]{2,1,0:T(8,128)(2,1)}, bf16[2,256,1024]{2,1,0:T(8,128)(2,1)}) custom-call(bf16[256,1024]{1,0:T(8,128)(2,1)} %reduce-scatter.8.cloned.1.call-done.refs_2_.refs_0_, bf16[256,1024]{1,0:T(8,128)(2,1)} %slice.670.refs_1_, ...), custom_call_target="tpu_custom_call" | custom-call | bytes 25500000 | tf_op jit(solution)/shard_map/pallas_call | solution.py:428
  (802 shorter events, 469.9 us)
Async XLA Ops:
  7.2 57.4 %all-gather.11.cloned.1.call-start = ((), (), s32[]{:S(2)}) async-start(), calls=%async_computation.14 | async-start | bytes 4718592 | tf_op jit(solution)/shard_map/all_gather | solution.py:1263
  10.3 138.4 %all-gather.13.cloned.1.call-start = ((), (), s32[]{:S(2)}) async-start(), calls=%async_computation.15 | async-start | bytes 9437184 | tf_op jit(solution)/shard_map/all_gather | solution.py:1263
  15.7 26.4 %collective-permute-start.4 = (bf16[512,1024]{1,0:T(8,128)(2,1)}, bf16[512,1024]{1,0:T(8,128)(2,1)}, u32[]{:S(2)}, u32[]{:S(2)}) collective-permute-start(bf16[512,1024]{1,0:T(8,128)(2,1)} %pad_maximum_fusion.6), channel_id=1, source_target_pairs={{0,16},{16,0},{1,17},{17,1},{2,18},{18,2},{3,19},{19,3},{4,20},{20... | collective-permute-start | bytes 3145736 | tf_op jit(solution)/shard_map/ppermute | solution.py:1003
  68.0 236.2 %all-gather.15.cloned.1.call-start = ((), (), s32[]{:S(2)}) async-start(), calls=%async_computation.16 | async-start | bytes 18874368 | tf_op jit(solution)/shard_map/all_gather | solution.py:1263
  82.1 35.8 %collective-permute-start.6 = (bf16[768,1024]{1,0:T(8,128)(2,1)S(1)}, bf16[768,1024]{1,0:T(8,128)(2,1)S(1)}, u32[]{:S(2)}, u32[]{:S(2)}) collective-permute-start(bf16[768,1024]{1,0:T(8,128)(2,1)S(1)} %pad_maximum_fusion.3), channel_id=1, source_target_pairs={{0,16},{16,0},{1,17},{17,1},{2,18},{18,2},{3,19},{19,3},{4,20},{20... | collective-permute-start | bytes 4718600 | tf_op jit(solution)/shard_map/ppermute | solution.py:1003
  154.4 257.1 %all-gather.17.cloned.1.call-start = ((), (), s32[]{:S(2)}) async-start(), calls=%async_computation.17 | async-start | bytes 9437184 | tf_op jit(solution)/shard_map/all_gather | solution.py:1263
  193.6 310.3 %all-gather.19.cloned.1.call-start = ((), (), s32[]{:S(2)}) async-start(), calls=%async_computation.18 | async-start | bytes 14155776 | tf_op jit(solution)/shard_map/all_gather | solution.py:1263
  347.1 214.9 %reduce-scatter.8.cloned.1.call-start = ((), (), s32[]{:S(2)}) async-start(), calls=%async_computation.7 | async-start | bytes 2621440 | tf_op jit(solution)/shard_map/reduce_scatter | solution.py:1089
  363.8 148.6 %collective-permute-start.14 = (bf16[256,1024]{1,0:T(8,128)(2,1)}, bf16[256,1024]{1,0:T(8,128)(2,1)}, u32[]{:S(2)}, u32[]{:S(2)}) collective-permute-start(bf16[256,1024]{1,0:T(8,128)(2,1)} %get-tuple-element.295), channel_id=1, source_target_pairs={{0,4},{4,0},{1,5},{5,1},{2,6},{6,2},{3,7},{7,3},{8,12},{12,8},{9,1... | collective-permute-start | bytes 1572872 | tf_op jit(solution)/shard_map/ppermute | solution.py:1003
  519.7 140.6 %reduce-scatter.10.cloned.1.call-start = ((), (), s32[]{:S(2)}) async-start(), calls=%async_computation.8 | async-start | bytes 5242880 | tf_op jit(solution)/shard_map/reduce_scatter | solution.py:1089
  519.8 24.5 %collective-permute-start.15 = (bf16[256,2048]{1,0:T(8,128)(2,1)S(1)}, bf16[256,2048]{1,0:T(8,128)(2,1)S(1)}, u32[]{:S(2)}, u32[]{:S(2)}) collective-permute-start(bf16[256,2048]{1,0:T(8,128)(2,1)S(1)} %get-tuple-element.95.refs_0_), channel_id=1, source_target_pairs={{0,4},{4,0},{1,5},{5,1},{2,6},{6,2},{3,7},{7,3},{8,12},{12,8},{9,1... | collective-permute-start | bytes 3145736 | tf_op jit(solution)/shard_map/ppermute | solution.py:1003
  525.8 18.5 %collective-permute-start.16 = (bf16[256,1024]{1,0:T(8,128)(2,1)S(1)}, bf16[256,1024]{1,0:T(8,128)(2,1)S(1)}, u32[]{:S(2)}, u32[]{:S(2)}) collective-permute-start(bf16[256,1024]{1,0:T(8,128)(2,1)S(1)} %get-tuple-element.229), channel_id=1, source_target_pairs={{0,4},{4,0},{1,5},{5,1},{2,6},{6,2},{3,7},{7,3},{8,12},{12,8},{9,1... | collective-permute-start | bytes 1572872 | tf_op jit(solution)/shard_map/ppermute | solution.py:1003
  562.1 179.3 %reduce-scatter.12.cloned.1.call-start = ((), (), s32[]{:S(2)}) async-start(), calls=%async_computation.9 | async-start | bytes 5242880 | tf_op jit(solution)/shard_map/reduce_scatter | solution.py:1089
  567.0 84.4 %collective-permute-start.18 = (bf16[256,2048]{1,0:T(8,128)(2,1)}, bf16[256,2048]{1,0:T(8,128)(2,1)}, u32[]{:S(2)}, u32[]{:S(2)}) collective-permute-start(bf16[256,2048]{1,0:T(8,128)(2,1)} %copy-done.42), channel_id=1, source_target_pairs={{0,4},{4,0},{1,5},{5,1},{2,6},{6,2},{3,7},{7,3},{8,12},{12,8},{9,1... | collective-permute-start | bytes 3145736 | tf_op jit(solution)/shard_map/ppermute | solution.py:1003
  660.3 163.2 %reduce-scatter.14.cloned.1.call-start = ((), (), s32[]{:S(2)}) async-start(), calls=%async_computation.10 | async-start | bytes 5242880 | tf_op jit(solution)/shard_map/reduce_scatter | solution.py:1089
  660.4 71.6 %collective-permute-start.27 = (bf16[256,2048]{1,0:T(8,128)(2,1)}, bf16[256,2048]{1,0:T(8,128)(2,1)S(1)}, u32[]{:S(2)}, u32[]{:S(2)}) collective-permute-start(bf16[256,2048]{1,0:T(8,128)(2,1)} %get-tuple-element.90.refs_0_), channel_id=1, source_target_pairs={{0,4},{4,0},{1,5},{5,1},{2,6},{6,2},{3,7},{7,3},{8,12},{12,8},{9,1... | collective-permute-start | bytes 3145736 | tf_op jit(solution)/shard_map/ppermute | solution.py:1003
  700.0 32.0 %collective-permute-start.28 = (bf16[256,1024]{1,0:T(8,128)(2,1)S(1)}, bf16[256,1024]{1,0:T(8,128)(2,1)S(1)}, u32[]{:S(2)}, u32[]{:S(2)}) collective-permute-start(bf16[256,1024]{1,0:T(8,128)(2,1)S(1)} %get-tuple-element.222), channel_id=1, source_target_pairs={{0,4},{4,0},{1,5},{5,1},{2,6},{6,2},{3,7},{7,3},{8,12},{12,8},{9,1... | collective-permute-start | bytes 1572872 | tf_op jit(solution)/shard_map/ppermute | solution.py:1003
  741.4 170.8 %reduce-scatter.16.cloned.1.call-start = ((), (), s32[]{:S(2)}) async-start(), calls=%async_computation.11 | async-start | bytes 5242880 | tf_op jit(solution)/shard_map/reduce_scatter | solution.py:1089
  744.3 70.3 %collective-permute-start.25 = (bf16[256,2048]{1,0:T(8,128)(2,1)}, bf16[256,2048]{1,0:T(8,128)(2,1)}, u32[]{:S(2)}, u32[]{:S(2)}) collective-permute-start(bf16[256,2048]{1,0:T(8,128)(2,1)} %copy-done.40), channel_id=1, source_target_pairs={{0,4},{4,0},{1,5},{5,1},{2,6},{6,2},{3,7},{7,3},{8,12},{12,8},{9,1... | collective-permute-start | bytes 3145736 | tf_op jit(solution)/shard_map/ppermute | solution.py:1003
  793.8 20.8 %collective-permute-start.26 = (bf16[256,1024]{1,0:T(8,128)(2,1)S(1)}, bf16[256,1024]{1,0:T(8,128)(2,1)S(1)}, u32[]{:S(2)}, u32[]{:S(2)}) collective-permute-start(bf16[256,1024]{1,0:T(8,128)(2,1)S(1)} %get-tuple-element.286), channel_id=1, source_target_pairs={{0,4},{4,0},{1,5},{5,1},{2,6},{6,2},{3,7},{7,3},{8,12},{12,8},{9,1... | collective-permute-start | bytes 1572872 | tf_op jit(solution)/shard_map/ppermute | solution.py:1003
  823.6 166.3 %reduce-scatter.18.cloned.1.call-start = ((), (), s32[]{:S(2)}) async-start(), calls=%async_computation.12 | async-start | bytes 5242880 | tf_op jit(solution)/shard_map/reduce_scatter | solution.py:1089
  828.7 73.5 %collective-permute-start.32 = (bf16[256,1024]{1,0:T(8,128)(2,1)}, bf16[256,1024]{1,0:T(8,128)(2,1)S(1)}, u32[]{:S(2)}, u32[]{:S(2)}) collective-permute-start(bf16[256,1024]{1,0:T(8,128)(2,1)} %get-tuple-element.282), channel_id=1, source_target_pairs={{0,4},{4,0},{1,5},{5,1},{2,6},{6,2},{3,7},{7,3},{8,12},{12,8},{9,1... | collective-permute-start | bytes 1572872 | tf_op jit(solution)/shard_map/ppermute | solution.py:1003
  828.7 73.5 %collective-permute-start.31 = (bf16[256,1024]{1,0:T(8,128)(2,1)}, bf16[256,1024]{1,0:T(8,128)(2,1)S(1)}, u32[]{:S(2)}, u32[]{:S(2)}) collective-permute-start(bf16[256,1024]{1,0:T(8,128)(2,1)} %get-tuple-element.228.refs_0_), channel_id=1, source_target_pairs={{0,4},{4,0},{1,5},{5,1},{2,6},{6,2},{3,7},{7,3},{8,12},{12,8},{9,1... | collective-permute-start | bytes 1572872 | tf_op jit(solution)/shard_map/ppermute | solution.py:1003
  912.3 129.0 %reduce-scatter.20.cloned.1.call-start = ((), (), s32[]{:S(2)}) async-start(), calls=%async_computation.13 | async-start | bytes 2949120 | tf_op jit(solution)/shard_map/reduce_scatter | solution.py:1089
  (210 other events, 1284.5 us)
Sparse Core Ops, SparseCore 0:
  10.4 54.1 all-gather.10
  68.1 80.5 all-gather.12
  154.5 149.6 all-gather.14
  306.2 80.2 all-gather.16
  388.5 115.2 all-gather.18
  519.9 42.1 reduce-scatter.7
  565.0 76.0 reduce-scatter.9
  660.5 76.2 reduce-scatter.11
  741.5 76.4 reduce-scatter.13
  823.7 76.5 reduce-scatter.15
  912.4 75.7 reduce-scatter.17
  990.3 48.5 reduce-scatter.19
